TPU v7x, 32 devices: a whole 2x2x4 slice. The times are simulated.
32 devices in a mesh: section: 2 (over x), dp: 2 (over y), ctx: 8 (over z, core).
Axes of the slice: x: 2, y: 2, z: 4, core: 2. Of those that a mesh axis runs over, the one named last changes fastest.
Arguments:
- tokens: bfloat16 [4, 2048, 960], P('dp', 'ctx'), may hold values from -6 to 6
- cotangent: bfloat16 [4, 2048, 960], P('dp', 'ctx'), may hold values from -6 to 6
- positions: int32 [4, 2048], P('dp', 'ctx'), may hold values from 0 to 2047, as said below
- attn_gain: bfloat16 [2, 960], P('section', ('dp', 'ctx')), may hold values from 0.5 to 1.5
- w_query: bfloat16 [2, 960, 960], P('section', ('dp', 'ctx')), may hold values from -0.1875 to 0.1875
- w_key: bfloat16 [2, 960, 320], P('section', ('dp', 'ctx')), may hold values from -0.1875 to 0.1875
- w_value: bfloat16 [2, 960, 320], P('section', ('dp', 'ctx')), may hold values from -0.1875 to 0.1875
- w_out: bfloat16 [2, 960, 960], P('section', ('dp', 'ctx')), may hold values from -3.5 to 3.5
- ffn_gain: bfloat16 [2, 960], P('section', ('dp', 'ctx')), may hold values from 0.5 to 1.5
- w_gate: bfloat16 [2, 960, 2560], P('section', ('dp', 'ctx')), may hold values from -0.1875 to 0.1875
- w_up: bfloat16 [2, 960, 2560], P('section', ('dp', 'ctx')), may hold values from -0.1875 to 0.1875
- w_down: bfloat16 [2, 2560, 960], P('section', ('dp', 'ctx')), may hold values from -0.125 to 0.125
Outputs:
- section_outputs: bfloat16 [2, 4, 2048, 960], P('section', 'dp', 'ctx')
- input_grads: float32 [2, 4, 2048, 960], P('section', 'dp', 'ctx')
- grad_attn_gain: float32 [2, 960], P('section', ('dp', 'ctx'))
- grad_query: float32 [2, 960, 960], P('section', ('dp', 'ctx'))
- grad_key: float32 [2, 960, 320], P('section', ('dp', 'ctx'))
- grad_value: float32 [2, 960, 320], P('section', ('dp', 'ctx'))
- grad_out: float32 [2, 960, 960], P('section', ('dp', 'ctx'))
- grad_ffn_gain: float32 [2, 960], P('section', ('dp', 'ctx'))
- grad_gate: float32 [2, 960, 2560], P('section', ('dp', 'ctx'))
- grad_up: float32 [2, 960, 2560], P('section', ('dp', 'ctx'))
- grad_down: float32 [2, 2560, 960], P('section', ('dp', 'ctx'))
Inputs may be any that keep to these rules, and one draw needn't show every extreme that they name: `positions`: each sequence is a pack of documents: a token's position counts from its document's first token, and every sequence begins a document at its first token.
All inputs are finite; a program needn't handle non-finite values.
Results may differ from a plain program's by a relative error of at most 0.023.
Values may be sent and summed in bfloat16 or wider, within the bound.
No kernel may reach another device: no remote copies, remote signals or barrier semaphores. Data moves between devices by JAX's collectives and lax.ppermute only.
A program may use at most 192 MiB of HBM per device.

v0:
```python
import jax
import jax.numpy as jnp
from jax import lax
from jax.sharding import PartitionSpec as P

D = 960
H = 15
KV = 5
HD = 64
MB = 2


EPS = 1e-05


def shifted(block, axis, distance):
    devices = range(lax.axis_size(axis))
    route = [(i - distance, i) for i in devices if i - distance in devices]
    return lax.ppermute(block, axis, route)


def rotate_half(vector):
    half_dim = vector.shape[-1] // 2
    return jnp.concatenate([-vector[..., half_dim:], vector[..., :half_dim]], -1)


def rope_tables(seq_pos):
    half_dim = HD // 2
    inv_freq = 10000.0 ** (-(jnp.arange(half_dim, dtype=jnp.float32) * 2.0) / HD)
    angles = seq_pos.astype(jnp.float32)[..., None] * inv_freq
    angle_pair = jnp.concatenate([angles, angles], -1)[..., None, :]
    return (jnp.cos(angle_pair), jnp.sin(angle_pair))


def norm_forward(values_in, gain_vec):
    factor = lax.rsqrt(jnp.mean(values_in * values_in, -1, keepdims=True) + EPS)
    return (values_in * factor * gain_vec, factor)


def norm_backward(grad_in, values_in, factor, gain_vec):
    scaled = grad_in * gain_vec
    grad_back = factor * scaled - values_in * factor * factor * factor * jnp.mean(
        scaled * values_in, -1, keepdims=True
    )
    return (grad_back, jnp.sum(grad_in * values_in * factor, 0))


def split_groups(queries, keys, values):
    seq_count, local_len = (queries.shape[0], queries.shape[1])
    length = keys.shape[1]
    query_g = jnp.moveaxis(queries.reshape(seq_count, local_len, KV, H // KV, HD), 2, 0)
    key_g = jnp.moveaxis(keys.reshape(seq_count, length, KV, HD), 2, 0)
    value_g = jnp.moveaxis(values.reshape(seq_count, length, KV, HD), 2, 0)
    return (query_g, key_g, value_g)


def masked_scores(query_one, key_one, causal):
    scores = jnp.einsum(
        "sqgd,skd->sgqk", query_one, key_one, preferred_element_type=jnp.float32
    ) * HD ** (-0.5)
    return jnp.where(causal, scores, -1e30)


def attend_forward(queries, keys, values, causal):
    seq_count, local_len = (queries.shape[0], queries.shape[1])
    query_g, key_g, value_g = split_groups(queries, keys, values)

    def one_group(operands):
        query_one, key_one, value_one = operands
        scores = masked_scores(query_one, key_one, causal)
        row_max = jnp.max(scores, -1, keepdims=True)
        exponent = jnp.exp(scores - row_max)
        totals = jnp.sum(exponent, -1, keepdims=True)
        probs = (exponent / totals).astype(jnp.bfloat16)
        result = jnp.einsum("sgqk,skd->sqgd", probs, value_one, preferred_element_type=jnp.float32)
        return (result, (row_max + jnp.log(totals))[..., 0])

    attended, log_total = lax.map(one_group, (query_g, key_g, value_g))
    attended = jnp.moveaxis(attended, 0, 2).reshape(seq_count * local_len, H * HD)
    return (attended, log_total)


def attend_backward(queries, keys, values, d_attended, log_total, causal):
    seq_count, local_len = (queries.shape[0], queries.shape[1])
    length = keys.shape[1]
    query_g, key_g, value_g = split_groups(queries, keys, values)
    grad_g = jnp.moveaxis(d_attended.reshape(seq_count, local_len, KV, H // KV, HD), 2, 0)

    def one_group(operands):
        query_one, key_one, value_one, grad_one, total_one = operands
        scores = masked_scores(query_one, key_one, causal)
        probs = jnp.exp(scores - total_one[..., None])
        d_probs = jnp.einsum(
            "sqgd,skd->sgqk", grad_one, value_one, preferred_element_type=jnp.float32
        )
        d_value = jnp.einsum(
            "sgqk,sqgd->skd",
            probs.astype(jnp.bfloat16),
            grad_one,
            preferred_element_type=jnp.float32,
        )
        d_scores = (probs * (d_probs - jnp.sum(probs * d_probs, -1, keepdims=True))).astype(
            jnp.bfloat16
        )
        d_query = jnp.einsum(
            "sgqk,skd->sqgd", d_scores, key_one, preferred_element_type=jnp.float32
        ) * HD ** (-0.5)
        d_key = jnp.einsum(
            "sgqk,sqgd->skd", d_scores, query_one, preferred_element_type=jnp.float32
        ) * HD ** (-0.5)
        return (d_query, d_key, d_value)

    d_query, d_key, d_value = lax.map(one_group, (query_g, key_g, value_g, grad_g, log_total))
    d_query = jnp.moveaxis(d_query, 0, 2).reshape(seq_count, local_len, H, HD)
    d_key = jnp.moveaxis(d_key, 0, 2).reshape(seq_count, length, KV * HD)
    d_value = jnp.moveaxis(d_value, 0, 2).reshape(seq_count, length, KV * HD)
    return (d_query, d_key, d_value)


def layer_forward(layer_input, cosine, sine, weights, causal):
    gain_a, w_q, w_k, w_v, w_o, gain_f, w_g, w_u, w_d = weights
    seq_count, local_len = (layer_input.shape[0], layer_input.shape[1])
    row_values = layer_input.reshape(-1, D).astype(jnp.float32)
    normed_a, factor_a = norm_forward(row_values, gain_a.astype(jnp.float32))
    normed_a = normed_a.astype(jnp.bfloat16)
    queries = jnp.dot(normed_a, w_q, preferred_element_type=jnp.float32).reshape(
        seq_count, local_len, H, HD
    )
    queries = (queries * cosine + rotate_half(queries) * sine).astype(jnp.bfloat16)
    keys = jnp.dot(normed_a, w_k, preferred_element_type=jnp.float32).reshape(
        seq_count, local_len, KV, HD
    )
    keys = (
        (keys * cosine + rotate_half(keys) * sine)
        .astype(jnp.bfloat16)
        .reshape(seq_count, local_len, KV * HD)
    )
    values = (
        jnp.dot(normed_a, w_v, preferred_element_type=jnp.float32)
        .astype(jnp.bfloat16)
        .reshape(seq_count, local_len, KV * HD)
    )
    keys_all, values_all = (
        lax.all_gather(keys, "ctx", axis=1, tiled=True),
        lax.all_gather(values, "ctx", axis=1, tiled=True),
    )
    attended, log_total = attend_forward(queries, keys_all, values_all, causal)
    attended = attended.astype(jnp.bfloat16)
    mixed_res = row_values + jnp.dot(attended, w_o, preferred_element_type=jnp.float32)
    normed_f, factor_f = norm_forward(mixed_res, gain_f.astype(jnp.float32))
    normed_f = normed_f.astype(jnp.bfloat16)
    gate_act = jnp.dot(normed_f, w_g, preferred_element_type=jnp.float32)
    up_proj = jnp.dot(normed_f, w_u, preferred_element_type=jnp.float32)
    hidden = (jax.nn.silu(gate_act) * up_proj).astype(jnp.bfloat16)
    layer_out = mixed_res + jnp.dot(hidden, w_d, preferred_element_type=jnp.float32)
    saved = (
        layer_input,
        factor_a,
        normed_a,
        queries,
        keys_all,
        values_all,
        log_total,
        attended,
        mixed_res,
        factor_f,
        normed_f,
        gate_act,
        up_proj,
        hidden,
    )
    return (layer_out, saved)


def layer_backward(grad_in, saved, cosine, sine, weights, causal):
    gain_a, w_q, w_k, w_v, w_o, gain_f, w_g, w_u, w_d = weights
    (
        layer_input,
        factor_a,
        normed_a,
        queries,
        keys_all,
        values_all,
        log_total,
        attended,
        mixed_res,
        factor_f,
        normed_f,
        gate_act,
        up_proj,
        hidden,
    ) = saved
    seq_count, local_len = (layer_input.shape[0], layer_input.shape[1])
    out_low = grad_in.astype(jnp.bfloat16)
    d_hidden = jnp.einsum("td,fd->tf", out_low, w_d, preferred_element_type=jnp.float32)
    sigmoid_gate = jax.nn.sigmoid(gate_act)
    d_gate = (d_hidden * up_proj * sigmoid_gate * (1.0 + gate_act * (1.0 - sigmoid_gate))).astype(
        jnp.bfloat16
    )
    d_up = (d_hidden * gate_act * sigmoid_gate).astype(jnp.bfloat16)
    d_normed_f = jnp.einsum("tf,df->td", d_gate, w_g, preferred_element_type=jnp.float32)
    d_normed_f = d_normed_f + jnp.einsum("tf,df->td", d_up, w_u, preferred_element_type=jnp.float32)
    d_mixed_norm, d_gain_f = norm_backward(
        d_normed_f, mixed_res, factor_f, gain_f.astype(jnp.float32)
    )
    d_mixed = grad_in + d_mixed_norm
    mix_low = d_mixed.astype(jnp.bfloat16)
    d_attended = jnp.einsum("td,cd->tc", mix_low, w_o, preferred_element_type=jnp.float32).astype(
        jnp.bfloat16
    )
    d_attended = d_attended.reshape(seq_count, local_len, H, HD)
    d_query, d_keys_all, d_values_all = attend_backward(
        queries, keys_all, values_all, d_attended, log_total, causal
    )
    d_key, d_value = (
        lax.psum_scatter(
            d_keys_all.astype(jnp.bfloat16), "ctx", scatter_dimension=1, tiled=True
        ).astype(jnp.float32),
        lax.psum_scatter(
            d_values_all.astype(jnp.bfloat16), "ctx", scatter_dimension=1, tiled=True
        ).astype(jnp.float32),
    )
    d_query = (
        (d_query * cosine - rotate_half(d_query * sine)).astype(jnp.bfloat16).reshape(-1, H * HD)
    )
    d_key = d_key.reshape(seq_count, local_len, KV, HD)
    d_key = (d_key * cosine - rotate_half(d_key * sine)).astype(jnp.bfloat16).reshape(-1, KV * HD)
    d_value = d_value.astype(jnp.bfloat16).reshape(-1, KV * HD)
    d_normed_a = jnp.einsum("tc,dc->td", d_query, w_q, preferred_element_type=jnp.float32)
    d_normed_a = d_normed_a + jnp.einsum(
        "tc,dc->td", d_key, w_k, preferred_element_type=jnp.float32
    )
    d_normed_a = d_normed_a + jnp.einsum(
        "tc,dc->td", d_value, w_v, preferred_element_type=jnp.float32
    )
    row_values = layer_input.reshape(-1, D).astype(jnp.float32)
    d_rows_norm, d_gain_a = norm_backward(
        d_normed_a, row_values, factor_a, gain_a.astype(jnp.float32)
    )
    d_layer_in = d_mixed + d_rows_norm
    pieces = (out_low, d_gate, d_up, mix_low, d_query, d_key, d_value, d_gain_a, d_gain_f)
    return (d_layer_in, pieces)


def merged(array_in):
    return array_in.reshape(-1, array_in.shape[-1])


def per_device(
    tokens,
    cotangent,
    positions,
    attn_gain,
    w_query,
    w_key,
    w_value,
    w_out,
    ffn_gain,
    w_gate,
    w_up,
    w_down,
):
    section_index = lax.axis_index("section")
    group_size, local_len = (tokens.shape[0], tokens.shape[1])
    seq_count = group_size // MB
    length = local_len * lax.axis_size("ctx")
    query_ids = lax.axis_index("ctx") * local_len + jnp.arange(local_len, dtype=jnp.int32)
    causal = jnp.arange(length, dtype=jnp.int32)[None, :] <= query_ids[:, None]
    shards = (
        attn_gain[0],
        w_query[0],
        w_key[0],
        w_value[0],
        w_out[0],
        ffn_gain[0],
        w_gate[0],
        w_up[0],
        w_down[0],
    )
    weights = (
        lax.all_gather(shards[0], ("dp", "ctx"), axis=0, tiled=True),
        lax.all_gather(shards[1], ("dp", "ctx"), axis=0, tiled=True),
        lax.all_gather(shards[2], ("dp", "ctx"), axis=0, tiled=True),
        lax.all_gather(shards[3], ("dp", "ctx"), axis=0, tiled=True),
        lax.all_gather(shards[4], ("dp", "ctx"), axis=0, tiled=True),
        lax.all_gather(shards[5], ("dp", "ctx"), axis=0, tiled=True),
        lax.all_gather(shards[6], ("dp", "ctx"), axis=0, tiled=True),
        lax.all_gather(shards[7], ("dp", "ctx"), axis=0, tiled=True),
        lax.all_gather(shards[8], ("dp", "ctx"), axis=0, tiled=True),
    )

    def micro_slice(array_in, micro_index):
        return lax.dynamic_slice_in_dim(array_in, micro_index * seq_count, seq_count, 0)

    received = jnp.zeros((seq_count, local_len, D), jnp.bfloat16)
    layer_outs = []
    saved_list = []
    for step_tick in range(MB + 1):
        micro_index = jnp.clip(step_tick - section_index, 0, MB - 1)
        cosine, sine = rope_tables(micro_slice(positions, micro_index))
        layer_input = jnp.where(section_index == 0, micro_slice(tokens, micro_index), received)
        layer_out, saved = layer_forward(layer_input, cosine, sine, weights, causal)
        layer_out = layer_out.astype(jnp.bfloat16).reshape(seq_count, local_len, D)
        if step_tick < MB:
            received = shifted(layer_out, "section", 1)
        layer_outs.append(layer_out)
        saved_list.append(saved)
    section_out = lax.dynamic_slice_in_dim(jnp.stack(layer_outs), section_index, MB, 0).reshape(
        group_size, local_len, D
    )
    stacked = tuple((jnp.stack(group_items) for group_items in zip(*saved_list)))
    weights = (
        lax.all_gather(shards[0], ("dp", "ctx"), axis=0, tiled=True),
        lax.all_gather(shards[1], ("dp", "ctx"), axis=0, tiled=True),
        lax.all_gather(shards[2], ("dp", "ctx"), axis=0, tiled=True),
        lax.all_gather(shards[3], ("dp", "ctx"), axis=0, tiled=True),
        lax.all_gather(shards[4], ("dp", "ctx"), axis=0, tiled=True),
        lax.all_gather(shards[5], ("dp", "ctx"), axis=0, tiled=True),
        lax.all_gather(shards[6], ("dp", "ctx"), axis=0, tiled=True),
        lax.all_gather(shards[7], ("dp", "ctx"), axis=0, tiled=True),
        lax.all_gather(shards[8], ("dp", "ctx"), axis=0, tiled=True),
    )
    back_recv = jnp.zeros((seq_count, local_len, D), jnp.bfloat16)
    input_list = []
    piece_list = []
    for step_tick in range(MB + 1):
        micro_index = jnp.clip(step_tick - 1 + section_index, 0, MB - 1)
        saved_slot = jnp.clip(step_tick - 1 + 2 * section_index, 0, MB)
        saved = tuple(
            (
                lax.dynamic_index_in_dim(part_arr, saved_slot, 0, keepdims=False)
                for part_arr in stacked
            )
        )
        cosine, sine = rope_tables(micro_slice(positions, micro_index))
        incoming = jnp.where(section_index == 1, micro_slice(cotangent, micro_index), back_recv)
        incoming = incoming.astype(jnp.float32).reshape(-1, D)
        d_layer_in, pieces = layer_backward(incoming, saved, cosine, sine, weights, causal)
        d_send = d_layer_in.astype(jnp.bfloat16)
        if step_tick < MB:
            back_recv = shifted(d_send.reshape(seq_count, local_len, D), "section", -1)
        input_list.append(
            jnp.where(section_index == 1, d_send.astype(jnp.float32), d_layer_in).reshape(
                seq_count, local_len, D
            )
        )
        piece_list.append(pieces)
    input_grad = lax.dynamic_slice_in_dim(jnp.stack(input_list), 1 - section_index, MB, 0).reshape(
        group_size, local_len, D
    )
    normed_a = merged(lax.dynamic_slice_in_dim(stacked[2], section_index, MB, 0))
    attended = merged(lax.dynamic_slice_in_dim(stacked[7], section_index, MB, 0))
    normed_f = merged(lax.dynamic_slice_in_dim(stacked[10], section_index, MB, 0))
    hidden = merged(lax.dynamic_slice_in_dim(stacked[13], section_index, MB, 0))
    chosen = tuple(
        (
            lax.dynamic_slice_in_dim(jnp.stack(group_items), 1 - section_index, MB, 0)
            for group_items in zip(*piece_list)
        )
    )
    out_low, d_gate, d_up, mix_low, d_query, d_key, d_value = (
        merged(part_arr) for part_arr in chosen[:7]
    )
    gain_grad_a = jnp.sum(chosen[7], 0)
    gain_grad_f = jnp.sum(chosen[8], 0)
    grad_wg = jnp.einsum("td,tf->df", normed_f, d_gate, preferred_element_type=jnp.float32)
    grad_wu = jnp.einsum("td,tf->df", normed_f, d_up, preferred_element_type=jnp.float32)
    grad_wd = jnp.einsum("tf,td->fd", hidden, out_low, preferred_element_type=jnp.float32)
    ffn_sums = (
        lax.psum_scatter(gain_grad_f, ("dp", "ctx"), scatter_dimension=0, tiled=True),
        lax.psum_scatter(grad_wg, ("dp", "ctx"), scatter_dimension=0, tiled=True),
        lax.psum_scatter(grad_wu, ("dp", "ctx"), scatter_dimension=0, tiled=True),
        lax.psum_scatter(grad_wd, ("dp", "ctx"), scatter_dimension=0, tiled=True),
    )
    grad_wq = jnp.einsum("td,tc->dc", normed_a, d_query, preferred_element_type=jnp.float32)
    grad_wk = jnp.einsum("td,tc->dc", normed_a, d_key, preferred_element_type=jnp.float32)
    grad_wv = jnp.einsum("td,tc->dc", normed_a, d_value, preferred_element_type=jnp.float32)
    grad_wo = jnp.einsum("tc,td->cd", attended, mix_low, preferred_element_type=jnp.float32)
    attn_sums = (
        lax.psum_scatter(gain_grad_a, ("dp", "ctx"), scatter_dimension=0, tiled=True),
        lax.psum_scatter(grad_wq, ("dp", "ctx"), scatter_dimension=0, tiled=True),
        lax.psum_scatter(grad_wk, ("dp", "ctx"), scatter_dimension=0, tiled=True),
        lax.psum_scatter(grad_wv, ("dp", "ctx"), scatter_dimension=0, tiled=True),
        lax.psum_scatter(grad_wo, ("dp", "ctx"), scatter_dimension=0, tiled=True),
    )
    return (
        section_out[None],
        input_grad[None],
        attn_sums[0][None],
        attn_sums[1][None],
        attn_sums[2][None],
        attn_sums[3][None],
        attn_sums[4][None],
        ffn_sums[0][None],
        ffn_sums[1][None],
        ffn_sums[2][None],
        ffn_sums[3][None],
    )


def solution(mesh):
    in_specs = (
        P("dp", "ctx", None),
        P("dp", "ctx", None),
        P("dp", "ctx"),
        P("section", ("dp", "ctx")),
        P("section", ("dp", "ctx"), None),
        P("section", ("dp", "ctx"), None),
        P("section", ("dp", "ctx"), None),
        P("section", ("dp", "ctx"), None),
        P("section", ("dp", "ctx")),
        P("section", ("dp", "ctx"), None),
        P("section", ("dp", "ctx"), None),
        P("section", ("dp", "ctx"), None),
    )
    out_specs = (
        P("section", "dp", "ctx", None),
        P("section", "dp", "ctx", None),
        P("section", ("dp", "ctx")),
        P("section", ("dp", "ctx"), None),
        P("section", ("dp", "ctx"), None),
        P("section", ("dp", "ctx"), None),
        P("section", ("dp", "ctx"), None),
        P("section", ("dp", "ctx")),
        P("section", ("dp", "ctx"), None),
        P("section", ("dp", "ctx"), None),
        P("section", ("dp", "ctx"), None),
    )
    return jax.shard_map(
        per_device, mesh=mesh, in_specs=in_specs, out_specs=out_specs, check_vma=False
    )
```

profile of v0, /device:TPU:0, one launch (start us, length us, event | category | flops | bytes accessed | tf_op | source)
XLA Modules:
  0.0 1627.3 jit_solution(7250925057100944878)
XLA Ops:
  14.8 35.5 %all-reduce.17 = (bf16[960]{0:T(1024)(128)(2,1)S(1)}, bf16[960]{0:T(1024)(128)(2,1)S(1)}) all-reduce(bf16[960]{0:T(1024)(128)(2,1)S(1)} %dynamic-update-slice, bf16[960]{0:T(1024)(128)(2,1)S(1)} %dynamic-update-slice.1), channel_id=2, replica_groups=mesh['section'=2,'dp'=2,'ctx'=8] {'dp','ctx'}, use_global_device_ids=true, to_apply=%add | all-reduce | flops 1920 | bytes 7680
  51.2 30.4 %all-gather.3 = bf16[1,960,320]{2,0,1:T(2,128)(2,1)} all-gather(bf16[1,60,320]{2,0,1:T(2,128)(2,1)S(1)} %copy.176), channel_id=5, replica_groups=mesh['section'=2,'dp'=2,'ctx'=8] {'dp','ctx'}, dimensions={1}, use_global_device_ids=true | all-gather | bytes 652800 | tf_op jit(solution)/shard_map/all_gather | solution.py:283
  87.7 37.2 %all-gather.1 = bf16[1,960,320]{2,0,1:T(2,128)(2,1)} all-gather(bf16[1,60,320]{2,0,1:T(2,128)(2,1)S(1)} %copy.173), channel_id=3, replica_groups=mesh['section'=2,'dp'=2,'ctx'=8] {'dp','ctx'}, dimensions={1}, use_global_device_ids=true | all-gather | bytes 652800 | tf_op jit(solution)/shard_map/all_gather | solution.py:284
  151.5 25.9 %all-gather.27.cloned.1.call-done = bf16[2048,320]{0,1:T(8,128)(2,1)} async-done(((bf16[256,320]{0,1:T(8,128)(2,1)}), bf16[2048,320]{0,1:T(8,128)(2,1)}) %all-gather.27.cloned.1.call-update) | async-done | bytes 1310736 | tf_op jit(solution)/shard_map/all_gather | solution.py:145
  177.4 38.1 %while.84 = (s32[]{:T(128)}, bf16[5,1,256,3,64]{2,4,3,1,0:T(8,128)(2,1)}, f32[5,1,3,256]{3,2,1,0:T(4,128)S(1)}, bf16[5,1,2048,64]{2,3,1,0:T(8,128)(2,1)}, bf16[5...) while((s32[]{:T(128)}, ...), condition=%wide.region_4.5_spmd.clone, body=%wide.region_1.4_spmd.clone.sunk | while | flops 422051072 | bytes 21821528 | solution.py:78
  218.7 43.8 %all-gather.35.cloned.1.call-done = bf16[1,960,2560]{2,0,1:T(2,128)(2,1)} async-done(((bf16[1,60,2560]{2,0,1:T(2,128)(2,1)}), bf16[1,960,2560]{2,0,1:T(2,128)(2,1)}) %all-gather.35.cloned.1.call-update) | async-done | bytes 4915216 | tf_op jit(solution)/shard_map/all_gather | solution.py:287
  262.6 7.3 copy.215
  269.8 77.6 %all-gather.37.cloned.1.call-done = bf16[1,960,2560]{2,0,1:T(2,128)(2,1)} async-done(((bf16[1,60,2560]{2,0,1:T(2,128)(2,1)}), bf16[1,960,2560]{2,0,1:T(2,128)(2,1)}) %all-gather.37.cloned.1.call-update) | async-done | bytes 4915216 | tf_op jit(solution)/shard_map/all_gather | solution.py:288
  360.4 43.5 %all-gather.39.cloned.1.call-done = bf16[1,2560,960]{2,1,0:T(8,128)(2,1)} async-done(((bf16[1,160,960]{2,1,0:T(8,128)(2,1)}), bf16[1,2560,960]{2,1,0:T(8,128)(2,1)}) %all-gather.39.cloned.1.call-update) | async-done | bytes 4915216 | tf_op jit(solution)/shard_map/all_gather | solution.py:289
  412.9 10.7 collective-permute-done
  435.0 16.5 %all-gather.43.cloned.1.call-done = bf16[2048,320]{0,1:T(8,128)(2,1)} async-done(((bf16[256,320]{0,1:T(8,128)(2,1)}), bf16[2048,320]{0,1:T(8,128)(2,1)}) %all-gather.43.cloned.1.call-update) | async-done | bytes 1310736 | tf_op jit(solution)/shard_map/all_gather | solution.py:144
  451.5 26.6 %all-gather.41.cloned.1.call-done = bf16[2048,320]{0,1:T(8,128)(2,1)} async-done(((bf16[256,320]{0,1:T(8,128)(2,1)}), bf16[2048,320]{0,1:T(8,128)(2,1)}) %all-gather.41.cloned.1.call-update) | async-done | bytes 1310736 | tf_op jit(solution)/shard_map/all_gather | solution.py:145
  478.1 37.8 %while.85 = (s32[]{:T(128)}, bf16[5,1,256,3,64]{2,4,3,1,0:T(8,128)(2,1)}, f32[5,1,3,256]{3,2,1,0:T(4,128)S(1)}, bf16[5,1,2048,64]{2,3,1,0:T(8,128)(2,1)}, bf16[5...) while((s32[]{:T(128)}, ...), condition=%wide.region_10.11_spmd.clone, body=%wide.region_7.10_spmd.clone.sunk | while | flops 422051072 | bytes 21821528 | solution.py:78
  530.6 10.7 collective-permute-done.1
  553.9 16.3 %all-gather.47.cloned.1.call-done = bf16[2048,320]{0,1:T(8,128)(2,1)} async-done(((bf16[256,320]{0,1:T(8,128)(2,1)}), bf16[2048,320]{0,1:T(8,128)(2,1)}) %all-gather.47.cloned.1.call-update) | async-done | bytes 1310736 | tf_op jit(solution)/shard_map/all_gather | solution.py:144
  570.2 26.6 %all-gather.45.cloned.1.call-done = bf16[2048,320]{0,1:T(8,128)(2,1)} async-done(((bf16[256,320]{0,1:T(8,128)(2,1)}), bf16[2048,320]{0,1:T(8,128)(2,1)}) %all-gather.45.cloned.1.call-update) | async-done | bytes 1310736 | tf_op jit(solution)/shard_map/all_gather | solution.py:145
  596.8 37.6 %while.86 = (s32[]{:T(128)}, bf16[5,1,256,3,64]{2,4,3,1,0:T(8,128)(2,1)}, f32[5,1,3,256]{3,2,1,0:T(4,128)S(1)}, bf16[5,1,2048,64]{2,3,1,0:T(8,128)(2,1)}, bf16[5...) while((s32[]{:T(128)}, ...), condition=%wide.region_16.17_spmd.clone, body=%wide.region_13.16_spmd.clone.sunk | while | flops 422051072 | bytes 21821528 | solution.py:78
  658.1 9.6 fusion.269
  681.4 66.1 %while.87 = (s32[]{:T(128)}, f32[5,1,256,3,64]{2,4,3,1,0:T(8,128)}, bf16[5,1,2048,64]{2,3,1,0:T(8,128)(2,1)}, bf16[5,1,2048,64]{2,3,1,0:T(8,128)(2,1)}, bf16[5,1...) while((s32[]{:T(128)}, f32[5,1,256,3,64]{2,4,3,1,0:T(8,128)}, ...), condition=%wide.region_21.22_spmd.clone, body=%wide.region_19.21_spmd.clone.sunk | while | flops 1021492480 | bytes 50681968 | solution.py:113
  757.2 22.3 %reduce-scatter.20.cloned.1.call-done = bf16[1,256,320]{1,2,0:T(8,128)(2,1)} async-done(((bf16[1,2048,320]{1,2,0:T(8,128)(2,1)}), bf16[1,256,320]{1,2,0:T(8,128)(2,1)}) %reduce-scatter.20.cloned.1.call-update) | async-done | bytes 163856 | tf_op jit(solution)/shard_map/reduce_scatter | solution.py:216
  783.7 29.6 %reduce-scatter.22.cloned.1.call-done = bf16[1,256,320]{1,2,0:T(8,128)(2,1)} async-done(((bf16[1,2048,320]{1,2,0:T(8,128)(2,1)}), bf16[1,256,320]{1,2,0:T(8,128)(2,1)}) %reduce-scatter.22.cloned.1.call-update) | async-done | bytes 163856 | tf_op jit(solution)/shard_map/reduce_scatter | solution.py:219
  820.0 10.3 collective-permute-done.2
  850.7 66.1 %while.88 = (s32[]{:T(128)}, f32[5,1,256,3,64]{2,4,3,1,0:T(8,128)}, bf16[5,1,2048,64]{2,3,1,0:T(8,128)(2,1)}, bf16[5,1,2048,64]{2,3,1,0:T(8,128)(2,1)}, bf16[5,1...) while((s32[]{:T(128)}, f32[5,1,256,3,64]{2,4,3,1,0:T(8,128)}, ...), condition=%wide.region_28.29_spmd.clone, body=%wide.region_26.28_spmd.clone.sunk | while | flops 1021492480 | bytes 50680944 | solution.py:113
  923.2 27.9 %reduce-scatter.24.cloned.1.call-done = bf16[1,256,320]{1,2,0:T(8,128)(2,1)} async-done(((bf16[1,2048,320]{1,2,0:T(8,128)(2,1)}), bf16[1,256,320]{1,2,0:T(8,128)(2,1)}) %reduce-scatter.24.cloned.1.call-update) | async-done | bytes 163856 | tf_op jit(solution)/shard_map/reduce_scatter | solution.py:216
  955.4 29.3 %reduce-scatter.26.cloned.1.call-done = bf16[1,256,320]{1,2,0:T(8,128)(2,1)} async-done(((bf16[1,2048,320]{1,2,0:T(8,128)(2,1)}), bf16[1,256,320]{1,2,0:T(8,128)(2,1)}) %reduce-scatter.26.cloned.1.call-update) | async-done | bytes 163856 | tf_op jit(solution)/shard_map/reduce_scatter | solution.py:219
  991.3 10.1 collective-permute-done.3
  1002.7 6.7 fusion.251
  1019.9 62.6 %while.89 = (s32[]{:T(128)}, f32[5,1,256,3,64]{2,4,3,1,0:T(8,128)S(1)}, bf16[5,1,2048,64]{2,3,1,0:T(8,128)(2,1)S(1)}, bf16[5,1,2048,64]{2,3,1,0:T(8,128)(2,1)}, ...) while((s32[]{:T(128)}, ...), condition=%wide.region_35.36_spmd.clone, body=%wide.region_33.35_spmd.clone.sunk | while | flops 1021492480 | bytes 50680944 | solution.py:113
  1084.5 9.9 convolution_bitcast_fusion.3
  1136.4 14.7 reduce-scatter.30.cloned.1.call-done
  1153.9 397.2 %fusion.568 = (f32[64,960]{1,0:T(8,128)S(1)}, f32[64,320]{1,0:T(8,128)S(1)}, f32[64,320]{1,0:T(8,128)S(1)}, f32[64,960]{1,0:T(8,128)S(1)}, f32[64,2560]{1,0:T(8,128)S(1)}, /*index=5*/f32[64,2560]{1,0:T(8,128)S(1)}) fusion(f32[960,960]{1,0:T(8,128)} %convolution_bitcast_fusion.7, f32[960,320]{1,0:T(8,128)} %convolution_bitcast_fusion.9, ...), kind=kCustom, calls=%all-reduce-scatter.6 | all-reduce-scatter fusion | flops 7864321 | bytes 31457792
  1568.2 30.2 %all-reduce.16 = (f32[960]{0:T(1024)S(1)}, f32[960]{0:T(1024)S(1)}) all-reduce(f32[960]{0:T(1024)S(1)} %get-tuple-element.740, f32[960]{0:T(1024)S(1)} %get-tuple-element.741), channel_id=23, replica_groups=mesh['section'=2,'dp'=2,'ctx'=8] {'dp','ctx'}, use_global_device_ids=true, to_apply=%region_43.44.clone | all-reduce | flops 1920 | bytes 15360
  (812 shorter events, 600.5 us)
Async XLA Ops:
  7.2 129.1 %all-gather.31.cloned.1.call-start = ((), (), s32[]{:S(2)}) async-start(), calls=%async_computation.16 | async-start | bytes 4177920 | tf_op jit(solution)/shard_map/all_gather | solution.py:282
  9.1 133.4 %all-gather.33.cloned.1.call-start = ((), (), s32[]{:S(2)}) async-start(), calls=%async_computation.17 | async-start | bytes 4177920 | tf_op jit(solution)/shard_map/all_gather | solution.py:285
  11.0 140.5 %all-gather.29.cloned.1.call-start = ((), (), s32[]{:S(2)}) async-start(), calls=%async_computation.15 | async-start | bytes 1474560 | tf_op jit(solution)/shard_map/all_gather | solution.py:144
  50.3 499.6 %copy-start.113 = (f32[960]{0:T(1024)}, f32[960]{0:T(1024)S(1)}, u32[]{:S(2)}) copy-start(f32[960]{0:T(1024)S(1)} %convert_element_type.704) | copy-start | bytes 11524
  85.2 456.3 %copy-start.13 = (bf16[1,960,320]{1,2,0:T(8,128)(2,1)}, bf16[1,960,320]{1,2,0:T(8,128)(2,1)S(1)}, u32[]{:S(2)}) copy-start(bf16[1,960,320]{1,2,0:T(8,128)(2,1)S(1)} %copy.177) | copy-start | bytes 1843204
  87.6 89.8 %all-gather.27.cloned.1.call-start = ((), (), s32[]{:S(2)}) async-start(), calls=%async_computation.14 | async-start | bytes 1474560 | tf_op jit(solution)/shard_map/all_gather | solution.py:145
  128.5 415.1 %copy-start.16 = (bf16[1,960,320]{1,2,0:T(8,128)(2,1)}, bf16[1,960,320]{1,2,0:T(8,128)(2,1)S(1)}, u32[]{:S(2)}) copy-start(bf16[1,960,320]{1,2,0:T(8,128)(2,1)S(1)} %copy.174) | copy-start | bytes 1843204
  129.7 132.9 %all-gather.35.cloned.1.call-start = ((), (), s32[]{:S(2)}) async-start(), calls=%async_computation.18 | async-start | bytes 10444800 | tf_op jit(solution)/shard_map/all_gather | solution.py:287
  131.1 216.3 %all-gather.37.cloned.1.call-start = ((), (), s32[]{:S(2)}) async-start(), calls=%async_computation.19 | async-start | bytes 10444800 | tf_op jit(solution)/shard_map/all_gather | solution.py:288
  132.5 271.5 %all-gather.39.cloned.1.call-start = ((), (), s32[]{:S(2)}) async-start(), calls=%async_computation.20 | async-start | bytes 5570560 | tf_op jit(solution)/shard_map/all_gather | solution.py:289
  133.2 318.3 %all-gather.43.cloned.1.call-start = ((), (), s32[]{:S(2)}) async-start(), calls=%async_computation.22 | async-start | bytes 1474560 | tf_op jit(solution)/shard_map/all_gather | solution.py:144
  409.3 14.3 collective-permute-start
  425.9 52.2 %all-gather.41.cloned.1.call-start = ((), (), s32[]{:S(2)}) async-start(), calls=%async_computation.21 | async-start | bytes 1474560 | tf_op jit(solution)/shard_map/all_gather | solution.py:145
  428.1 142.1 %all-gather.47.cloned.1.call-start = ((), (), s32[]{:S(2)}) async-start(), calls=%async_computation.24 | async-start | bytes 1474560 | tf_op jit(solution)/shard_map/all_gather | solution.py:144
  518.2 152.5 %copy-start.128 = (f32[256]{0:T(256)}, f32[256]{0:T(256)S(1)}, u32[]{:S(2)}) copy-start(f32[256]{0:T(256)S(1)} %add_rsqrt_fusion.2) | copy-start | bytes 3076
  528.4 12.8 collective-permute-start.1
  543.1 53.6 %all-gather.45.cloned.1.call-start = ((), (), s32[]{:S(2)}) async-start(), calls=%async_computation.23 | async-start | bytes 1474560 | tf_op jit(solution)/shard_map/all_gather | solution.py:145
  545.8 233.7 %reduce-scatter.20.cloned.1.call-start = ((), (), s32[]{:S(2)}) async-start(), calls=%async_computation.7 | async-start | bytes 1474560 | tf_op jit(solution)/shard_map/reduce_scatter | solution.py:216
  747.5 65.8 %reduce-scatter.22.cloned.1.call-start = ((), (), s32[]{:S(2)}) async-start(), calls=%async_computation.8 | async-start | bytes 1474560 | tf_op jit(solution)/shard_map/reduce_scatter | solution.py:219
  748.3 202.9 %reduce-scatter.24.cloned.1.call-start = ((), (), s32[]{:S(2)}) async-start(), calls=%async_computation.9 | async-start | bytes 1474560 | tf_op jit(solution)/shard_map/reduce_scatter | solution.py:216
  818.7 11.6 collective-permute-start.2
  916.8 67.9 %reduce-scatter.26.cloned.1.call-start = ((), (), s32[]{:S(2)}) async-start(), calls=%async_computation.10 | async-start | bytes 1474560 | tf_op jit(solution)/shard_map/reduce_scatter | solution.py:219
  917.4 215.1 %reduce-scatter.28.cloned.1.call-start = ((), (), s32[]{:S(2)}) async-start(), calls=%async_computation.11 | async-start | bytes 1474560 | tf_op jit(solution)/shard_map/reduce_scatter | solution.py:216
  990.0 11.4 collective-permute-start.3
  1083.6 67.5 %reduce-scatter.30.cloned.1.call-start = ((), (), s32[]{:S(2)}) async-start(), calls=%async_computation.12 | async-start | bytes 1474560 | tf_op jit(solution)/shard_map/reduce_scatter | solution.py:219
  1084.2 536.1 %reduce-scatter.32.cloned.1.call-start = ((), (), s32[]{:S(2)}) async-start(), calls=%async_computation.13 | async-start | bytes 11141120 | tf_op jit(solution)/shard_map/reduce_scatter | solution.py:373
  1552.1 60.0 %collective-permute-start.9 = (f32[60,2560]{1,0:T(8,128)}, f32[60,2560]{1,0:T(8,128)}, u32[]{:S(2)}, u32[]{:S(2)}) collective-permute-start(f32[60,2560]{1,0:T(8,128)} %slice.125), channel_id=1, source_target_pairs={{0,1},{1,2},{2,3},{3,4},{4,5},{5,6},{6,7},{7,8},{8,9},{9,10},{10,1... | collective-permute-start | bytes 1843208
  1555.4 60.8 %collective-permute-start.8 = (f32[60,2560]{1,0:T(8,128)}, f32[60,2560]{1,0:T(8,128)}, u32[]{:S(2)}, u32[]{:S(2)}) collective-permute-start(f32[60,2560]{1,0:T(8,128)} %slice.124), channel_id=1, source_target_pairs={{0,1},{1,2},{2,3},{3,4},{4,5},{5,6},{6,7},{7,8},{8,9},{9,10},{10,1... | collective-permute-start | bytes 1843208
  1558.7 49.9 %collective-permute-start.7 = (f32[60,960]{1,0:T(8,128)}, f32[60,960]{1,0:T(8,128)}, u32[]{:S(2)}, u32[]{:S(2)}) collective-permute-start(f32[60,960]{1,0:T(8,128)} %slice.123), channel_id=1, source_target_pairs={{0,1},{1,2},{2,3},{3,4},{4,5},{5,6},{6,7},{7,8},{8,9},{9,10},{10,1... | collective-permute-start | bytes 691208
  1561.4 41.6 %collective-permute-start.6 = (f32[60,320]{1,0:T(8,128)}, f32[60,320]{1,0:T(8,128)}, u32[]{:S(2)}, u32[]{:S(2)}) collective-permute-start(f32[60,320]{1,0:T(8,128)} %slice.122), channel_id=1, source_target_pairs={{0,1},{1,2},{2,3},{3,4},{4,5},{5,6},{6,7},{7,8},{8,9},{9,10},{10,1... | collective-permute-start | bytes 230408
  1564.0 42.0 %collective-permute-start.5 = (f32[60,320]{1,0:T(8,128)}, f32[60,320]{1,0:T(8,128)}, u32[]{:S(2)}, u32[]{:S(2)}) collective-permute-start(f32[60,320]{1,0:T(8,128)} %slice.121), channel_id=1, source_target_pairs={{0,1},{1,2},{2,3},{3,4},{4,5},{5,6},{6,7},{7,8},{8,9},{9,10},{10,1... | collective-permute-start | bytes 230408
  1602.9 7.9 collective-permute-start.4
  (167 other events, 1615.2 us)
Sparse Core Ops, SparseCore 0:
  10.9 56.3 all-gather.30
  70.2 55.0 all-gather.32
  126.9 24.5 all-gather.28
  152.9 24.3 all-gather.26
  180.1 82.3 all-gather.34
  265.3 82.0 all-gather.36
  349.7 54.1 all-gather.38
  426.0 25.4 all-gather.42
  453.7 24.3 all-gather.40
  543.3 26.8 all-gather.46
  572.4 24.3 all-gather.44
  747.6 31.7 reduce-scatter.19
  781.7 31.5 reduce-scatter.21
  917.0 34.1 reduce-scatter.23
  953.3 31.3 reduce-scatter.25
  1083.7 33.9 reduce-scatter.27
  1119.8 31.2 reduce-scatter.29
  1155.6 180.5 reduce-scatter.31
where the time goes:
time: 1640 us; the launch traced here: 1630 us
  blocking collectives  530 us (32%)
  waiting for transfers between devices  451 us (28%)
  matrix products  400 us (24%)
  other arithmetic  109 us (7%)
  local copies, waits for them, and re-layouts  93.7 us (6%)
  starting transfers between devices  22.7 us (1%)
  between operations  19.2 us (1%)
    unnamed x3, blocking collectives  463 us
    all_gather x3, waiting for transfers between devices, layer_forward(): lax.all_gather(values, 'ctx', axis=1, tiled=True)  79.1 us
    dot_general x30, matrix products, masked_scores(): jnp.einsum('sqgd,skd->sgqk', query_one, key_one, preferred_element_type=j...  78.3 us
    all_gather x1, waiting for transfers between devices, per_device(): lax.all_gather(shards[7], ('dp', 'ctx'), axis=0, tiled=True)  77.6 us
    reduce_scatter x3, waiting for transfers between devices, layer_backward(): lax.psum_scatter(d_values_all.astype(jnp.bfloat16), 'ctx', scatter_dimens...  73.5 us
    unnamed x377, local copies, waits for them, and re-layouts  65.9 us
    dot_general x15, matrix products, one_group(): jnp.einsum('sgqk,skd->sqgd', probs, value_one, preferred_element_type=jnp...  52.9 us
    reduce_scatter x3, waiting for transfers between devices, layer_backward(): lax.psum_scatter(d_keys_all.astype(jnp.bfloat16), 'ctx', scatter_dimensio...  50.2 us
  transfers between devices with their start and end apart: 28, of which 18 were waited for; matrix products, arithmetic and copies ran while one was open for 37% of the time, Pallas kernels for 0%

commit v1 on v0

v1 whole, which is shorter than its diff:
```python
import functools

import jax
import jax.numpy as jnp
from jax import lax
from jax.experimental import pallas as pl
from jax.experimental.pallas import tpu as pltpu
from jax.sharding import Mesh
from jax.sharding import PartitionSpec as P

D = 960
H = 15
KV = 5
G = H // KV
HD = 64
FF = 2560
EPS = 1e-05
F32 = jnp.float32
BF = jnp.bfloat16


def dot(a,b): return jnp.dot(a,b,preferred_element_type=F32)

def fwd_kernel(rng, q_ref, kv_ref, o_ref, lse_ref, qt, vt, m_s, l_s, acc):
    T=q_ref.shape[0]; W=G*T
    qt[...]=q_ref[...].astype(F32).T.astype(BF)
    nb=kv_ref.shape[0]
    def step(b, first):
        vt[...]=kv_ref[b,:,KV*HD:].astype(F32).T.astype(BF)
        for g in range(KV):
            qg=jnp.concatenate([qt[(g*G+j)*HD:(g*G+j+1)*HD,:] for j in range(G)],1)
            s=dot(kv_ref[b,:,g*HD:(g+1)*HD],qg)
            if first:
                key=lax.broadcasted_iota(jnp.int32,(T,W),0)
                qry=lax.broadcasted_iota(jnp.int32,(T,W),1)%T
                s=jnp.where(key<=qry,s,-1e30)
                m=jnp.max(s,0,keepdims=True)
                p=jnp.exp(s-m)
                l_s[g:g+1,:]=jnp.sum(p,0,keepdims=True)
                acc[g*HD:(g+1)*HD,:]=dot(vt[g*HD:(g+1)*HD,:],p.astype(BF))
            else:
                mo=m_s[g:g+1,:]
                m=jnp.maximum(mo,jnp.max(s,0,keepdims=True))
                p=jnp.exp(s-m); al=jnp.exp(mo-m)
                l_s[g:g+1,:]=l_s[g:g+1,:]*al+jnp.sum(p,0,keepdims=True)
                acc[g*HD:(g+1)*HD,:]=acc[g*HD:(g+1)*HD,:]*al+dot(vt[g*HD:(g+1)*HD,:],p.astype(BF))
            m_s[g:g+1,:]=m
    step(0,True)
    def body(b,_):
        step(b,False); return 0
    lax.fori_loop(rng[0],rng[1],body,0)
    for g in range(KV):
        inv=1.0/l_s[g:g+1,:]
        lse_ref[g:g+1,:]=m_s[g:g+1,:]+jnp.log(l_s[g:g+1,:])
        og=acc[g*HD:(g+1)*HD,:]*inv
        for j in range(G):
            h=g*G+j
            o_ref[:,h*HD:(h+1)*HD]=og[:,j*T:(j+1)*T].T.astype(BF)

def attn_fwd(rng,q,kv):
    T=q.shape[0]; W=G*T
    return pl.pallas_call(fwd_kernel,
      out_shape=(jax.ShapeDtypeStruct((T,H*HD),BF),jax.ShapeDtypeStruct((KV,W),F32)),
      in_specs=[pl.BlockSpec(memory_space=pltpu.SMEM)]+[pl.BlockSpec(memory_space=pltpu.VMEM)]*2,
      out_specs=[pl.BlockSpec(memory_space=pltpu.VMEM)]*2,
      scratch_shapes=[pltpu.VMEM((H*HD,T),BF),pltpu.VMEM((KV*HD,T),BF),pltpu.VMEM((KV,W),F32),pltpu.VMEM((KV,W),F32),pltpu.VMEM((KV*HD,W),F32)],
      compiler_params=pltpu.CompilerParams(vmem_limit_bytes=48<<20),
    )(rng,q,kv)

def bwd_kernel(rng, q_ref, kv_ref, o_ref, do_ref, lse_ref, dq_ref, dkv_ref, qt, dot_, qn, don, kt, dl, dqa):
    T=q_ref.shape[0]; W=G*T
    nb=kv_ref.shape[0]
    qt[...]=q_ref[...].astype(F32).T.astype(BF)
    doT=do_ref[...].astype(F32).T
    dot_[...]=doT.astype(BF)
    oT=o_ref[...].astype(F32).T
    prod=doT*oT
    for h in range(H):
        g,j=divmod(h,G)
        dl[g:g+1,j*T:(j+1)*T]=jnp.sum(prod[h*HD:(h+1)*HD,:],0,keepdims=True)
        qn[g,j*T:(j+1)*T,:]=q_ref[:,h*HD:(h+1)*HD]
        don[g,j*T:(j+1)*T,:]=do_ref[:,h*HD:(h+1)*HD]
    def step(b, first):
        kt[...]=kv_ref[b,:,:KV*HD].astype(F32).T.astype(BF)
        for g in range(KV):
            qg=jnp.concatenate([qt[(g*G+j)*HD:(g*G+j+1)*HD,:] for j in range(G)],1)
            dg=jnp.concatenate([dot_[(g*G+j)*HD:(g*G+j+1)*HD,:] for j in range(G)],1)
            s=dot(kv_ref[b,:,g*HD:(g+1)*HD],qg)
            p=jnp.exp(s-lse_ref[g:g+1,:])
            if first:
                key=lax.broadcasted_iota(jnp.int32,(T,W),0)
                qry=lax.broadcasted_iota(jnp.int32,(T,W),1)%T
                p=jnp.where(key<=qry,p,0.0)
            dp=dot(kv_ref[b,:,(KV+g)*HD:(KV+g+1)*HD],dg)
            dz=(p*(dp-dl[g:g+1,:])).astype(BF)
            dkv_ref[b,:,(KV+g)*HD:(KV+g+1)*HD]=dot(p.astype(BF),don[g]).astype(BF)
            dkv_ref[b,:,g*HD:(g+1)*HD]=dot(dz,qn[g]).astype(BF)
            dq=dot(kt[g*HD:(g+1)*HD,:],dz)
            if first: dqa[g*HD:(g+1)*HD,:]=dq
            else: dqa[g*HD:(g+1)*HD,:]+=dq
    step(0,True)
    def body(b,_):
        step(b,False); return 0
    lax.fori_loop(rng[0],rng[1],body,0)
    def zero(b,_):
        dkv_ref[b]=jnp.zeros((T,2*KV*HD),BF); return 0
    lax.fori_loop(1,rng[0],zero,0)
    lax.fori_loop(rng[1],nb,zero,0)
    for g in range(KV):
        for j in range(G):
            h=g*G+j
            dq_ref[:,h*HD:(h+1)*HD]=(dqa[g*HD:(g+1)*HD,j*T:(j+1)*T]*HD**-0.5).T

def attn_bwd(rng,q,kv,o,do,lse):
    T=q.shape[0]; W=G*T
    return pl.pallas_call(bwd_kernel,
      out_shape=(jax.ShapeDtypeStruct((T,H*HD),F32),jax.ShapeDtypeStruct(kv.shape,BF)),
      in_specs=[pl.BlockSpec(memory_space=pltpu.SMEM)]+[pl.BlockSpec(memory_space=pltpu.VMEM)]*5,
      out_specs=[pl.BlockSpec(memory_space=pltpu.VMEM)]*2,
      scratch_shapes=[pltpu.VMEM((H*HD,T),BF),pltpu.VMEM((H*HD,T),BF),pltpu.VMEM((KV,W,HD),BF),pltpu.VMEM((KV,W,HD),BF),
        pltpu.VMEM((KV*HD,T),BF),pltpu.VMEM((KV,W),F32),pltpu.VMEM((KV*HD,W),F32)],
      compiler_params=pltpu.CompilerParams(vmem_limit_bytes=48<<20),
    )(rng,q,kv,o,do,lse)


def rotate_half(vector):
    half_dim = vector.shape[-1] // 2
    return jnp.concatenate([-vector[..., half_dim:], vector[..., :half_dim]], -1)


def rope_tables(seq_pos):
    half_dim = HD // 2
    inv_freq = 10000.0 ** (-(jnp.arange(half_dim, dtype=F32) * 2.0) / HD)
    angles = seq_pos.astype(F32)[..., None] * inv_freq
    angle_pair = jnp.concatenate([angles, angles], -1)[..., None, :]
    return (jnp.cos(angle_pair), jnp.sin(angle_pair))


def norm_forward(values_in, gain_vec):
    factor = lax.rsqrt(jnp.mean(values_in * values_in, -1, keepdims=True) + EPS)
    return (values_in * factor * gain_vec, factor)


def norm_backward(grad_in, values_in, factor, gain_vec):
    scaled = grad_in * gain_vec
    grad_back = factor * scaled - values_in * factor * factor * factor * jnp.mean(
        scaled * values_in, -1, keepdims=True
    )
    return (grad_back, jnp.sum(grad_in * values_in * factor, 0))


def swap(block, axis):
    return lax.ppermute(block, axis, [(0, 1), (1, 0)])


def move_z(block, distance):
    count = lax.axis_size("z")
    route = [(i, i + distance) for i in range(count) if 0 <= i + distance < count]
    return lax.ppermute(block, "z", route)


def gather_kv(block):
    count = lax.axis_size("z")
    own = [block] + [move_z(block, d) for d in range(1, count)]
    own = jnp.stack(own)
    other = swap(own, "core")
    return jnp.stack([own, other], 1).reshape((2 * count,) + block.shape)


def reduce_kv(blocks):
    count = lax.axis_size("z")
    blocks = blocks.reshape((count, 2) + blocks.shape[1:])
    mine = blocks[:, 0].astype(F32) + swap(blocks[:, 1], "core").astype(F32)
    total = mine[0]
    for d in range(1, count):
        total = total + move_z(mine[d].astype(BF), -d).astype(F32)
    return total


def project(left, right):
    return jnp.dot(left, right, preferred_element_type=F32)


def project_t(left, right):
    return lax.dot_general(left, right, (((1,), (1,)), ((), ())), preferred_element_type=F32)


def outer(left, right):
    return lax.dot_general(left, right, (((0,), (0,)), ((), ())), preferred_element_type=F32)


def rope(values, cosine, sine):
    count = values.shape[0]
    values = values.reshape(count, -1, HD)
    return (values * cosine + rotate_half(values) * sine).reshape(count, -1)


def rope_t(values, cosine, sine):
    count = values.shape[0]
    values = values.reshape(count, -1, HD)
    return (values * cosine - rotate_half(values * sine)).reshape(count, -1)


def layer_forward(rows, tables, weights, block_range):
    gain_a, w_qkv, w_o, gain_f, w_g, w_u, w_d = weights
    cosine, sine = tables
    normed_a, factor_a = norm_forward(rows, gain_a)
    normed_a = normed_a.astype(BF)
    qkv = project(normed_a, w_qkv)
    queries = (rope(qkv[:, :D], cosine, sine)).astype(BF) * BF(HD**-0.5)
    keys = rope(qkv[:, D : D + KV * HD], cosine, sine).astype(BF)
    values = qkv[:, D + KV * HD :].astype(BF)
    kv_all = gather_kv(jnp.concatenate([keys, values], -1))
    attended, log_total = attn_fwd(block_range, queries, kv_all)
    mixed = rows + project(attended, w_o)
    normed_f, factor_f = norm_forward(mixed, gain_f)
    normed_f = normed_f.astype(BF)
    gate_act = project(normed_f, w_g)
    up_proj = project(normed_f, w_u)
    hidden = (jax.nn.silu(gate_act) * up_proj).astype(BF)
    out = (mixed + project(hidden, w_d)).astype(BF)
    saved = (rows, factor_a, normed_a, queries, kv_all, log_total, attended, mixed, factor_f, normed_f, gate_act, up_proj, hidden)
    return out, saved


def layer_backward(grad_low, saved, tables, weights, block_range):
    gain_a, w_qkv, w_o, gain_f, w_g, w_u, w_d = weights
    cosine, sine = tables
    rows, factor_a, normed_a, queries, kv_all, log_total, attended, mixed, factor_f, normed_f, gate_act, up_proj, hidden = saved
    d_hidden = project_t(grad_low, w_d)
    sig = jax.nn.sigmoid(gate_act)
    d_gate = (d_hidden * up_proj * sig * (1.0 + gate_act * (1.0 - sig))).astype(BF)
    d_up = (d_hidden * gate_act * sig).astype(BF)
    d_normed_f = project_t(d_gate, w_g) + project_t(d_up, w_u)
    d_norm, d_gain_f = norm_backward(d_normed_f, mixed, factor_f, gain_f)
    d_mixed = grad_low.astype(F32) + d_norm
    mix_low = d_mixed.astype(BF)
    d_attended = project_t(mix_low, w_o).astype(BF)
    d_query, d_kv = attn_bwd(block_range, queries, kv_all, attended, d_attended, log_total)
    d_kv = reduce_kv(d_kv)
    d_query = rope_t(d_query, cosine, sine).astype(BF)
    d_key = rope_t(d_kv[:, : KV * HD], cosine, sine).astype(BF)
    d_value = d_kv[:, KV * HD :].astype(BF)
    d_qkv = jnp.concatenate([d_query, d_key, d_value], -1)
    d_normed_a = project_t(d_qkv, w_qkv)
    d_norm_a, d_gain_a = norm_backward(d_normed_a, rows, factor_a, gain_a)
    d_rows = d_mixed + d_norm_a
    grads = dict(
        gate=outer(normed_f, d_gate).astype(BF),
        up=outer(normed_f, d_up).astype(BF),
        down=outer(hidden, grad_low).astype(BF),
        out=outer(attended, mix_low).astype(BF),
        qkv=outer(normed_a, d_qkv).astype(BF),
        gains=jnp.stack([d_gain_a, d_gain_f]),
    )
    return d_rows, grads


def per_device(tokens, cotangent, positions, attn_gain, w_query, w_key, w_value, w_out, ffn_gain, w_gate, w_up, w_down):
    section = lax.axis_index("section")
    z_index, core = lax.axis_index("z"), lax.axis_index("core")
    plane = ("dp", "z", "core")
    group = tokens.shape[0]
    local = tokens.shape[1]
    block_range = jnp.stack([2 - core, 2 * z_index + 2]).astype(jnp.int32)

    def mine(array_in):
        return lax.dynamic_index_in_dim(array_in, section, 0, keepdims=False)

    rows = tokens.shape[1]
    shard_rows = w_query.shape[1]
    ff_rows = w_down.shape[1]
    half = ff_rows // 2
    qkvo = jnp.concatenate([w_query[0], w_key[0], w_value[0], w_out[0]], -1)
    down = jnp.concatenate([w_down[0, :half], jnp.zeros((half, 64), BF), w_down[0, half:], jnp.zeros((half, 576), BF)], -1)
    gains = jnp.concatenate([attn_gain, ffn_gain], -1)
    shard = jnp.concatenate([qkvo, w_gate[0], w_up[0], down], 0)
    shard = lax.dynamic_update_slice(shard, gains, (3 * shard_rows, 2048))
    other = swap(shard, "section")

    def assemble(block):
        whole = lax.all_gather(block, plane, axis=0)
        n = shard_rows

        def piece(lo, hi):
            return whole[:, lo : lo + n, :hi].reshape(-1, hi) if hi <= FF else None

        attn = whole[:, :n, :].reshape(n * whole.shape[0], FF)
        w_g = whole[:, n : 2 * n, :].reshape(-1, FF)
        w_u = whole[:, 2 * n : 3 * n, :].reshape(-1, FF)
        w_d = jnp.concatenate([whole[:, 3 * n :, :D], whole[:, 3 * n :, 1024 : 1024 + D]], 1).reshape(-1, D)
        gain_rows = whole[:, 3 * n, 2048 : 2048 + 2 * n].astype(F32)
        gain_a = gain_rows[:, :n].reshape(-1)
        gain_f = gain_rows[:, n:].reshape(-1)
        return gain_a, attn[:, : D + 2 * KV * HD], attn[:, D + 2 * KV * HD :], gain_f, w_g, w_u, w_d

    w0 = assemble(jnp.where(section == 0, shard, other))
    w1 = assemble(jnp.where(section == 1, shard, other))
    tables = rope_tables(mine(positions))
    out0, saved0 = layer_forward(mine(tokens).astype(F32), tables, w0, block_range)
    out1, saved1 = layer_forward(out0.astype(F32), tables, w1, block_range)
    d1, g1 = layer_backward(mine(cotangent), saved1, tables, w1, block_range)
    d1_low = d1.astype(BF)
    d0, g0 = layer_backward(d1_low, saved0, tables, w0, block_range)

    def pair(own, got):
        return jnp.where(section == 0, jnp.stack([own, got]), jnp.stack([got, own]))

    got = swap(jnp.where(section == 0, out1, out0), "section")
    section_out = pair(jnp.where(section == 0, out0, out1), got)
    got = swap(jnp.where(section == 0, d1_low, d0.astype(BF)), "section").astype(F32)
    input_grad = pair(jnp.where(section == 0, d0, d1_low.astype(F32)), got)

    def reduce(first, second):
        def scatter(part):
            return lax.psum_scatter(part, plane, scatter_dimension=0, tiled=True)

        s0, s1 = scatter(first), scatter(second)
        got = swap(jnp.where(section == 0, s1, s0), "section")
        return jnp.where(section == 0, s0, s1).astype(F32) + got.astype(F32)

    grads = {name: reduce(g0[name], g1[name]) for name in ("gate", "up", "down", "out", "qkv")}
    gain_grad = reduce(g0["gains"].T, g1["gains"].T)
    qkv = grads["qkv"]
    kd = KV * HD
    outs = (
        section_out,
        input_grad,
        gain_grad[:, 0],
        qkv[:, :D],
        qkv[:, D : D + kd],
        qkv[:, D + kd :],
        grads["out"],
        gain_grad[:, 1],
        grads["gate"],
        grads["up"],
        grads["down"],
    )
    return tuple(part[None] for part in outs)


LANES = 128
PADDED = 1024
CHUNK = 640
KVW = 2 * KV * HD
QKV_BLOCKS = 13
ACTS = FF + 3 * PADDED
BACK = 2 * FF + 2 * PADDED
OUT_BLOCKS = PADDED // LANES
FF_BLOCKS = FF // LANES
VMEM = pl.BlockSpec(memory_space=pltpu.VMEM)
ANY = pl.BlockSpec(memory_space=pl.ANY)
SMEM = pl.BlockSpec(memory_space=pltpu.SMEM)
BIG = pltpu.CompilerParams(vmem_limit_bytes=56 << 20)


def dot_nt(left, right):
    return lax.dot_general(left, right, (((1,), (1,)), ((), ())), preferred_element_type=F32)


def columns(ref, first, count, rows):
    parts = [
        ref[:, first + i * rows : first + (i + 1) * rows, :].reshape(-1, LANES) for i in range(count)
    ]
    return parts[0] if count == 1 else jnp.concatenate(parts, 1)


def half_of(values):
    lane = lax.broadcasted_iota(jnp.int32, values.shape, 1)
    back = pltpu.roll(values, LANES - HD // 2, 1)
    ahead = pltpu.roll(values, HD // 2, 1)
    return jnp.where(lane % HD < HD // 2, -back, ahead)


def rms(values):
    return lax.rsqrt(jnp.sum(values * values, -1, keepdims=True) / D + EPS)


def norm_back(grad, values, gain):
    factor = rms(values)
    scaled = grad * gain
    mean = jnp.sum(scaled * values, -1, keepdims=True) / D
    back = factor * scaled - values * (factor * factor * factor * mean)
    return back, jnp.sum(grad * values * factor, 0, keepdims=True)


def load_kv(blocks, other, kv_s, sems):
    copies = [pltpu.make_async_copy(block, kv_s.at[0, d], sems.at[d]) for d, block in enumerate(blocks)]
    copies.append(pltpu.make_async_copy(other, kv_s.at[1], sems.at[len(blocks)]))
    for copy in copies:
        copy.start()
    return copies


def attend_kernel(zs, rng, q_ref, *refs):
    blocks, (other, o_ref, lse_ref, kv_s, qt, vt, m_s, l_s, acc, sems) = refs[:zs], refs[zs:]
    T = q_ref.shape[0]
    W = G * T
    copies = load_kv(blocks, other, kv_s, sems)
    qt[...] = q_ref[...].astype(F32).T.astype(BF)
    for copy in copies:
        copy.wait()

    def step(b, first):
        kv = kv_s.at[lax.rem(b, 2), lax.div(b, 2)] if not first else kv_s.at[0, 0]
        vt[...] = kv[:, KV * HD :].astype(F32).T.astype(BF)
        for g in range(KV):
            at = slice(g * HD, (g + 1) * HD)
            qg = jnp.concatenate([qt[(g * G + j) * HD : (g * G + j + 1) * HD, :] for j in range(G)], 1)
            s = dot(kv[:, at], qg)
            if first:
                key = lax.broadcasted_iota(jnp.int32, (T, W), 0)
                query = lax.broadcasted_iota(jnp.int32, (T, W), 1) % T
                s = jnp.where(key <= query, s, -1e30)
                m = jnp.max(s, 0, keepdims=True)
                p = jnp.exp(s - m)
                l_s[g : g + 1, :] = jnp.sum(p, 0, keepdims=True)
                acc[at, :] = dot(vt[at, :], p.astype(BF))
            else:
                old = m_s[g : g + 1, :]
                m = jnp.maximum(old, jnp.max(s, 0, keepdims=True))
                p = jnp.exp(s - m)
                scale = jnp.exp(old - m)
                l_s[g : g + 1, :] = l_s[g : g + 1, :] * scale + jnp.sum(p, 0, keepdims=True)
                acc[at, :] = acc[at, :] * scale + dot(vt[at, :], p.astype(BF))
            m_s[g : g + 1, :] = m

    step(0, True)

    def body(b, _):
        step(b, False)
        return 0

    lax.fori_loop(rng[0], rng[1], body, 0)
    for g in range(KV):
        lse_ref[g : g + 1, :] = m_s[g : g + 1, :] + jnp.log(l_s[g : g + 1, :])
        og = acc[g * HD : (g + 1) * HD, :] / l_s[g : g + 1, :]
        for j in range(G):
            h = g * G + j
            o_ref[:, h * HD : (h + 1) * HD] = og[:, j * T : (j + 1) * T].T.astype(BF)


def attend(rng, q, kv_all):
    blocks, other = kv_all
    T, zs = q.shape[0], len(blocks)
    W = G * T
    return pl.pallas_call(
        functools.partial(attend_kernel, zs),
        out_shape=(jax.ShapeDtypeStruct((T, D), BF), jax.ShapeDtypeStruct((KV, W), F32)),
        in_specs=[SMEM, VMEM] + [ANY] * (zs + 1),
        out_specs=[VMEM] * 2,
        scratch_shapes=[
            pltpu.VMEM((2, zs, T, KVW), BF),
            pltpu.VMEM((D, T), BF),
            pltpu.VMEM((KV * HD, T), BF),
            pltpu.VMEM((KV, W), F32),
            pltpu.VMEM((KV, W), F32),
            pltpu.VMEM((KV * HD, W), F32),
            pltpu.SemaphoreType.DMA((zs + 1,)),
        ],
        compiler_params=BIG,
        name="attend",
    )(rng, q, *blocks, other)


def attend_back_kernel(zs, rng, q_ref, o_ref, do_ref, lse_ref, cos_ref, sin_ref, *refs):
    blocks, (other, dq_ref, dkv_ref, kv_s, qt, dot_, qn, don, kt, dl, dqa, sems) = refs[:zs], refs[zs:]
    T = q_ref.shape[0]
    W = G * T
    copies = load_kv(blocks, other, kv_s, sems)
    qt[...] = q_ref[...].astype(F32).T.astype(BF)
    do_t = do_ref[...].astype(F32).T
    dot_[...] = do_t.astype(BF)
    prod = do_t * o_ref[...].astype(F32).T
    for h in range(H):
        g, j = divmod(h, G)
        rows = slice(j * T, (j + 1) * T)
        dl[g : g + 1, rows] = jnp.sum(prod[h * HD : (h + 1) * HD, :], 0, keepdims=True)
        qn[g, rows, :] = q_ref[:, h * HD : (h + 1) * HD]
        don[g, rows, :] = do_ref[:, h * HD : (h + 1) * HD]
    for copy in copies:
        copy.wait()

    def step(b, first):
        side, far = (0, 0) if first else (lax.rem(b, 2), lax.div(b, 2))
        kv = kv_s.at[side, far]
        out = dkv_ref.at[side, far]
        kt[...] = kv[:, : KV * HD].astype(F32).T.astype(BF)
        for g in range(KV):
            at = slice(g * HD, (g + 1) * HD)
            vat = slice((KV + g) * HD, (KV + g + 1) * HD)
            heads = [slice((g * G + j) * HD, (g * G + j + 1) * HD) for j in range(G)]
            s = dot(kv[:, at], jnp.concatenate([qt[h, :] for h in heads], 1))
            p = jnp.exp(s - lse_ref[g : g + 1, :])
            if first:
                key = lax.broadcasted_iota(jnp.int32, (T, W), 0)
                query = lax.broadcasted_iota(jnp.int32, (T, W), 1) % T
                p = jnp.where(key <= query, p, 0.0)
            dp = dot(kv[:, vat], jnp.concatenate([dot_[h, :] for h in heads], 1))
            dz = (p * (dp - dl[g : g + 1, :])).astype(BF)
            out[:, vat] = dot(p.astype(BF), don[g]).astype(BF)
            out[:, at] = dot(dz, qn[g]).astype(BF)
            dq = dot(kt[at, :], dz)
            if first:
                dqa[at, :] = dq
            else:
                dqa[at, :] += dq

    step(0, True)

    def body(b, _):
        step(b, False)
        return 0

    def zero(b, _):
        dkv_ref[lax.rem(b, 2), lax.div(b, 2)] = jnp.zeros((T, KVW), BF)
        return 0

    lax.fori_loop(rng[0], rng[1], body, 0)
    lax.fori_loop(1, rng[0], zero, 0)
    lax.fori_loop(rng[1], 2 * zs, zero, 0)
    cos, sin = cos_ref[...], sin_ref[...]
    for pair in range(PADDED // LANES):
        parts = []
        for h in (2 * pair, 2 * pair + 1):
            g, j = divmod(h, G)
            if h < H:
                parts.append(dqa[g * HD : (g + 1) * HD, j * T : (j + 1) * T] * HD**-0.5)
            else:
                parts.append(jnp.zeros((HD, T), F32))
        grad = jnp.concatenate(parts, 0).T
        turned = grad * cos - half_of(grad * sin)
        dq_ref[:, pair * LANES : (pair + 1) * LANES] = turned.astype(BF)


def attend_back(rng, q, o, do, lse, cos, sin, kv_all):
    blocks, other = kv_all
    T, zs = q.shape[0], len(blocks)
    W = G * T
    return pl.pallas_call(
        functools.partial(attend_back_kernel, zs),
        out_shape=(jax.ShapeDtypeStruct((T, PADDED), BF), jax.ShapeDtypeStruct((2, zs, T, KVW), BF)),
        in_specs=[SMEM] + [VMEM] * 6 + [ANY] * (zs + 1),
        out_specs=[VMEM] * 2,
        scratch_shapes=[
            pltpu.VMEM((2, zs, T, KVW), BF),
            pltpu.VMEM((D, T), BF),
            pltpu.VMEM((D, T), BF),
            pltpu.VMEM((KV, W, HD), BF),
            pltpu.VMEM((KV, W, HD), BF),
            pltpu.VMEM((KV * HD, T), BF),
            pltpu.VMEM((KV, W), F32),
            pltpu.VMEM((KV * HD, W), F32),
            pltpu.SemaphoreType.DMA((zs + 1,)),
        ],
        compiler_params=BIG,
        name="attend_back",
    )(rng, q, o, do, lse, cos, sin, *blocks, other)


def spread_kv(block):
    blocks = [block] + [move_z(block, d) for d in range(1, lax.axis_size("z"))]
    return blocks, swap(jnp.stack(blocks), "core")


def collect_kv(grads):
    mine = grads[0].astype(F32) + swap(grads[1], "core").astype(F32)
    mine = mine.astype(BF)
    return [mine[0]] + [move_z(mine[d], -d) for d in range(1, lax.axis_size("z"))]


def qkv_kernel(base, x_ref, gain_ref, cos_ref, sin_ref, w_hbm, na_ref, q_ref, kv_ref, w_s, sem):
    rows = w_s.shape[1] // QKV_BLOCKS
    copy = pltpu.make_async_copy(w_hbm.at[:, pl.ds(base, w_s.shape[1]), :], w_s, sem)
    copy.start()
    x = x_ref[...].astype(F32)
    normed = (x * rms(x) * gain_ref[...]).astype(BF)
    na_ref[...] = normed
    copy.wait()
    cos, sin = cos_ref[...], sin_ref[...]
    for j in range(QKV_BLOCKS):
        out = dot(normed, columns(w_s, j * rows, 1, rows))
        if j < 5:
            turned = out * cos + half_of(out) * sin if j < 3 else out
            if j == 2:
                lane = lax.broadcasted_iota(jnp.int32, out.shape, 1)
                turned = jnp.where(lane < HD, turned, out)
            kv_ref[:, j * LANES : (j + 1) * LANES] = turned.astype(BF)
        else:
            turned = (out * cos + half_of(out) * sin).astype(BF) * BF(HD**-0.5)
            at = (j - 5) * LANES
            width = min(LANES, D - at)
            q_ref[:, at : at + width] = turned[:, :width]


def qkv_forward(x, gain, cos, sin, weights, base):
    count = x.shape[0]
    shards = weights.shape[0]
    rows = PADDED // shards
    return pl.pallas_call(
        functools.partial(qkv_kernel, base),
        out_shape=(
            jax.ShapeDtypeStruct((count, PADDED), BF),
            jax.ShapeDtypeStruct((count, D), BF),
            jax.ShapeDtypeStruct((count, KVW), BF),
        ),
        in_specs=[VMEM] * 4 + [ANY],
        out_specs=[VMEM] * 3,
        scratch_shapes=[pltpu.VMEM((shards, QKV_BLOCKS * rows, LANES), BF), pltpu.SemaphoreType.DMA],
        compiler_params=BIG,
        name="qkv_forward",
    )(x, gain, cos, sin, weights)


def weight_copies(w_hbm, w_s, sems, rows, ff_rows, first):
    steps = FF // CHUNK
    per = CHUNK // ff_rows
    blocks = CHUNK // LANES * rows
    gate = first + OUT_BLOCKS * rows
    up = gate + FF_BLOCKS * rows
    down = up + FF_BLOCKS * rows
    out = [pltpu.make_async_copy(w_hbm.at[:, pl.ds(first, OUT_BLOCKS * rows), :], w_s.at[:, pl.ds(0, OUT_BLOCKS * rows), :], sems.at[3 * steps])]
    chunks = []
    for j in range(steps):
        parts = []
        for at in (gate + j * blocks, up + j * blocks):
            parts.append((pl.ds(0, w_hbm.shape[0]), pl.ds(at, blocks), pl.ds(at - first, blocks)))
        parts.append((pl.ds(j * per, per), pl.ds(down, OUT_BLOCKS * ff_rows), pl.ds(down - first, OUT_BLOCKS * ff_rows)))
        chunks.append(
            [
                pltpu.make_async_copy(w_hbm.at[who, src, :], w_s.at[who, dst, :], sems.at[3 * j + i])
                for i, (who, src, dst) in enumerate(parts)
            ]
        )
    return out, chunks


def down_of(w_s, j, ff_rows, at):
    per = CHUNK // ff_rows
    parts = [
        w_s[j * per : (j + 1) * per, at + i * ff_rows : at + (i + 1) * ff_rows, :].reshape(CHUNK, LANES)
        for i in range(OUT_BLOCKS)
    ]
    return jnp.concatenate(parts, 1)


def ffn_kernel(first, o_ref, x_ref, na_ref, gain_ref, e_ref, w_hbm, acts_ref, m_ref, g_ref, u_ref, y_ref, w_s, acc, sems):
    step = pl.program_id(0)
    rows = PADDED // w_s.shape[0]
    ff_rows = FF // w_s.shape[0]
    out, chunks = weight_copies(w_hbm, w_s, sems, rows, ff_rows, first)
    gate = OUT_BLOCKS * rows
    up = gate + FF_BLOCKS * rows
    down = up + FF_BLOCKS * rows
    blocks = CHUNK // LANES

    @pl.when(step == 0)
    def _():
        out[0].start()
        for chunk in chunks:
            for copy in chunk:
                copy.start()
        padded = dot(o_ref[...], e_ref[...]).astype(BF)
        acts_ref[:, FF : FF + PADDED] = padded
        acts_ref[:, FF + 2 * PADDED :] = na_ref[...]
        out[0].wait()
        mixed = x_ref[...].astype(F32) + dot(padded, columns(w_s, 0, OUT_BLOCKS, rows))
        m_ref[...] = mixed
        acts_ref[:, FF + PADDED : FF + 2 * PADDED] = (mixed * rms(mixed) * gain_ref[...]).astype(BF)
        acc[...] = mixed

    for j in range(FF // CHUNK):

        @pl.when(step == j)
        def _():
            for copy in chunks[j]:
                copy.wait()
            normed = acts_ref[:, FF + PADDED : FF + 2 * PADDED]
            g = dot(normed, columns(w_s, gate + j * blocks * rows, blocks, rows))
            u = dot(normed, columns(w_s, up + j * blocks * rows, blocks, rows))
            hidden = (g * jax.nn.sigmoid(g) * u).astype(BF)
            g_ref[...] = g
            u_ref[...] = u
            acts_ref[:, j * CHUNK : (j + 1) * CHUNK] = hidden
            acc[...] += dot(hidden, down_of(w_s, j, ff_rows, down))

    @pl.when(step == FF // CHUNK - 1)
    def _():
        y_ref[...] = acc[...].astype(BF)


def ffn_forward(o, x, na, gain, e, weights, first):
    count = x.shape[0]
    shards = weights.shape[0]
    rows = PADDED // shards
    later = (OUT_BLOCKS + 2 * FF_BLOCKS) * rows + OUT_BLOCKS * (FF // shards)
    whole = lambda shape: pl.BlockSpec(shape, lambda j: (0, 0))
    chunk = pl.BlockSpec((count, CHUNK), lambda j: (0, j))
    wide = jax.ShapeDtypeStruct((count, FF), F32)
    return pl.pallas_call(
        functools.partial(ffn_kernel, first),
        grid=(FF // CHUNK,),
        out_shape=(
            jax.ShapeDtypeStruct((count, ACTS), BF),
            jax.ShapeDtypeStruct((count, PADDED), F32),
            wide,
            wide,
            jax.ShapeDtypeStruct((count, PADDED), BF),
        ),
        in_specs=[whole((count, D))] + [whole((count, PADDED))] * 2 + [whole((1, PADDED)), whole((D, PADDED)), ANY],
        out_specs=[whole((count, ACTS)), whole((count, PADDED)), chunk, chunk, whole((count, PADDED))],
        scratch_shapes=[
            pltpu.VMEM((shards, later, LANES), BF),
            pltpu.VMEM((count, PADDED), F32),
            pltpu.SemaphoreType.DMA((3 * (FF // CHUNK) + 1,)),
        ],
        compiler_params=BIG,
        name="ffn_forward",
    )(o, x, na, gain, e, weights)


def ffn_back_kernel(first, dy_ref, g_ref, u_ref, m_ref, gain_ref, e_ref, w_hbm, back_ref, dm_ref, do_ref, dgain_ref, w_s, acc, sems):
    step = pl.program_id(0)
    rows = PADDED // w_s.shape[0]
    ff_rows = FF // w_s.shape[0]
    out, chunks = weight_copies(w_hbm, w_s, sems, rows, ff_rows, first)
    gate = OUT_BLOCKS * rows
    up = gate + FF_BLOCKS * rows
    down = up + FF_BLOCKS * rows
    blocks = CHUNK // LANES

    @pl.when(step == 0)
    def _():
        for chunk in chunks:
            for copy in (chunk[2], chunk[0], chunk[1]):
                copy.start()
        out[0].start()
        acc[...] = jnp.zeros_like(acc)

    for j in range(FF // CHUNK):

        @pl.when(step == j)
        def _():
            chunks[j][2].wait()
            d_hidden = dot_nt(dy_ref[...], down_of(w_s, j, ff_rows, down))
            g = g_ref[...]
            sig = jax.nn.sigmoid(g)
            dg = (d_hidden * u_ref[...] * sig * (1.0 + g * (1.0 - sig))).astype(BF)
            du = (d_hidden * g * sig).astype(BF)
            back_ref[:, j * CHUNK : (j + 1) * CHUNK] = dg
            back_ref[:, FF + j * CHUNK : FF + (j + 1) * CHUNK] = du
            chunks[j][0].wait()
            chunks[j][1].wait()
            acc[...] += dot_nt(dg, columns(w_s, gate + j * blocks * rows, blocks, rows)) + dot_nt(
                du, columns(w_s, up + j * blocks * rows, blocks, rows)
            )

    @pl.when(step == FF // CHUNK - 1)
    def _():
        back, dgain = norm_back(acc[...], m_ref[...], gain_ref[...])
        dgain_ref[...] = dgain
        d_mixed = dy_ref[...].astype(F32) + back
        dm_ref[...] = d_mixed
        low = d_mixed.astype(BF)
        back_ref[:, 2 * FF : 2 * FF + PADDED] = low
        back_ref[:, 2 * FF + PADDED :] = dy_ref[...]
        out[0].wait()
        d_padded = dot_nt(low, columns(w_s, 0, OUT_BLOCKS, rows)).astype(BF)
        do_ref[...] = dot_nt(d_padded, e_ref[...]).astype(BF)


def ffn_backward(dy, g, u, mixed, gain, e, weights, first):
    count = dy.shape[0]
    shards = weights.shape[0]
    rows = PADDED // shards
    later = (OUT_BLOCKS + 2 * FF_BLOCKS) * rows + OUT_BLOCKS * (FF // shards)
    whole = lambda shape: pl.BlockSpec(shape, lambda j: (0, 0))
    chunk = pl.BlockSpec((count, CHUNK), lambda j: (0, j))
    full = whole((count, PADDED))
    return pl.pallas_call(
        functools.partial(ffn_back_kernel, first),
        grid=(FF // CHUNK,),
        out_shape=(
            jax.ShapeDtypeStruct((count, BACK), BF),
            jax.ShapeDtypeStruct((count, PADDED), F32),
            jax.ShapeDtypeStruct((count, D), BF),
            jax.ShapeDtypeStruct((1, PADDED), F32),
        ),
        in_specs=[full, chunk, chunk, full, whole((1, PADDED)), whole((D, PADDED)), ANY],
        out_specs=[whole((count, BACK)), full, whole((count, D)), whole((1, PADDED))],
        scratch_shapes=[
            pltpu.VMEM((shards, later, LANES), BF),
            pltpu.VMEM((count, PADDED), F32),
            pltpu.SemaphoreType.DMA((3 * (FF // CHUNK) + 1,)),
        ],
        compiler_params=BIG,
        name="ffn_backward",
    )(dy, g, u, mixed, gain, e, weights)


def qkv_back_kernel(base, zs, dq_ref, cos_ref, sin_ref, x_ref, gain_ref, dm_ref, *refs):
    shares, (w_hbm, dkv_ref, dx_ref, dgain_ref, w_s, sem) = refs[:zs], refs[zs:]
    rows = w_s.shape[1] // QKV_BLOCKS
    copy = pltpu.make_async_copy(w_hbm.at[:, pl.ds(base, w_s.shape[1]), :], w_s, sem)
    copy.start()
    cos, sin = cos_ref[...], sin_ref[...]
    for j in range(KVW // LANES):
        at = slice(j * LANES, (j + 1) * LANES)
        grad = shares[0][:, at].astype(F32)
        for share in shares[1:]:
            grad = grad + share[:, at].astype(F32)
        turned = grad * cos - half_of(grad * sin) if j < 3 else grad
        if j == 2:
            lane = lax.broadcasted_iota(jnp.int32, grad.shape, 1)
            turned = jnp.where(lane < HD, turned, grad)
        dkv_ref[:, at] = turned.astype(BF)
    copy.wait()
    kv_blocks = KVW // LANES
    d_normed = dot_nt(dkv_ref[...], columns(w_s, 0, kv_blocks, rows))
    d_normed = d_normed + dot_nt(dq_ref[...], columns(w_s, kv_blocks * rows, QKV_BLOCKS - kv_blocks, rows))
    back, dgain = norm_back(d_normed, x_ref[...].astype(F32), gain_ref[...])
    dgain_ref[...] = dgain
    dx_ref[...] = dm_ref[...] + back


def qkv_backward(dq, shares, cos, sin, x, gain, dm, weights, base):
    count = x.shape[0]
    shards = weights.shape[0]
    rows = PADDED // shards
    return pl.pallas_call(
        functools.partial(qkv_back_kernel, base, len(shares)),
        out_shape=(
            jax.ShapeDtypeStruct((count, KVW), BF),
            jax.ShapeDtypeStruct((count, PADDED), F32),
            jax.ShapeDtypeStruct((1, PADDED), F32),
        ),
        in_specs=[VMEM] * (6 + len(shares)) + [ANY],
        out_specs=[VMEM] * 3,
        scratch_shapes=[pltpu.VMEM((shards, QKV_BLOCKS * rows, LANES), BF), pltpu.SemaphoreType.DMA],
        compiler_params=BIG,
        name="qkv_backward",
    )(dq, cos, sin, x, gain, dm, *shares, weights)


def both_t(own, other, at, width):
    parts = [ref[:, at : at + width].astype(F32).T.astype(BF) for ref in (own, other)]
    return jnp.concatenate(parts, 1)


def own_rows(turned, core, rows):
    split = turned.reshape(-1, 2, rows, turned.shape[-1])
    return jnp.where(core == 0, split[:, 0], split[:, 1]).reshape(-1, turned.shape[-1])


def both(own, other, at, width):
    where = pl.ds(pl.multiple_of(at, LANES), width)
    return jnp.concatenate([own[:, where], other[:, where]], 0)


def write_split(out, keep_ref, send_ref, at, rows, half):
    for i in range(out.shape[1] // LANES):
        block = out[:, i * LANES : (i + 1) * LANES].reshape(2, -1, rows, LANES)
        place = slice(at + i * rows, at + (i + 1) * rows)
        keep_ref[:, place, :] = jnp.where(half == 0, block[0], block[1])
        send_ref[:, place, :] = jnp.where(half == 0, block[1], block[0])


def grad_ffn_kernel(place, own, other, back, back_other, keep_a, send_a, keep_u, send_u, keep_o, send_o, nft, opt, hdt):
    step = pl.program_id(0)
    core, half, section = place[0], place[1], place[2]
    chips = keep_a.shape[0]
    rows, ff_rows = PADDED // (2 * chips), FF // (2 * chips)
    steps = FF // CHUNK

    @pl.when(step == 0)
    def _():
        nft[...] = own_rows(both_t(own, other, FF + PADDED, PADDED), core, rows)

    @pl.when(step == steps)
    def _():
        hdt[...] = own_rows(both_t(own, other, 0, FF), core, ff_rows)

    @pl.when(step == 3 * steps)
    def _():
        opt[...] = own_rows(both_t(own, other, FF, PADDED), core, rows)

    def write_a(out, height, to):
        for i in range(out.shape[1] // LANES):
            to[:, i * height : (i + 1) * height, :] = out[:, i * LANES : (i + 1) * LANES].reshape(chips, height, LANES)

    @pl.when(step < steps)
    def _():
        out = dot(nft[...], both(back, back_other, step * CHUNK, CHUNK)).astype(BF)
        pl.when(section == 1)(lambda: write_a(out, rows, keep_a))
        pl.when(section == 0)(lambda: write_a(out, rows, send_a))

    @pl.when((step >= steps) & (step < 2 * steps))
    def _():
        width = PADDED // steps
        out = dot(hdt[...], both(back, back_other, 2 * FF + PADDED + (step - steps) * width, width)).astype(BF)
        pl.when(section == 0)(lambda: write_a(out, ff_rows, keep_a))
        pl.when(section == 1)(lambda: write_a(out, ff_rows, send_a))

    @pl.when((step >= 2 * steps) & (step < 3 * steps))
    def _():
        out = dot(nft[...], both(back, back_other, FF + (step - 2 * steps) * CHUNK, CHUNK)).astype(BF)
        write_split(out, keep_u, send_u, 0, rows, half)

    @pl.when(step == 3 * steps)
    def _():
        out = dot(opt[...], both(back, back_other, 2 * FF, PADDED)).astype(BF)
        write_split(out, keep_o, send_o, 0, rows, half)


def grad_ffn(place, own, other, back, back_other, shards):
    count = own.shape[0]
    chips = shards // 2
    rows, ff_rows = PADDED // shards, FF // shards
    steps = FF // CHUNK
    block = CHUNK // LANES * rows
    whole = lambda shape: pl.BlockSpec(shape, lambda j, place: (0,) * len(shape))
    early = lambda j: jnp.clip(j, 0, steps - 1)
    late = lambda j: jnp.clip(j - steps, 0, steps - 1)
    last = lambda j: jnp.clip(j - 2 * steps, 0, steps - 1)
    a_spec = lambda when: pl.BlockSpec((chips, block, LANES), lambda j, place: (0, jnp.where(place[2] == when, late(j), early(j)), 0))
    u_spec = pl.BlockSpec((chips // 2, block, LANES), lambda j, place: (0, last(j), 0))
    wide = lambda first, height: jax.ShapeDtypeStruct((first, height, LANES), BF)
    return pl.pallas_call(
        grad_ffn_kernel,
        grid_spec=pltpu.PrefetchScalarGridSpec(
            num_scalar_prefetch=1,
            grid=(3 * steps + 1,),
            in_specs=[whole((count, ACTS))] * 2 + [whole((count, BACK))] * 2,
            out_specs=[a_spec(0), a_spec(1), u_spec, u_spec] + [whole((chips // 2, OUT_BLOCKS * rows, LANES))] * 2,
            scratch_shapes=[
                pltpu.VMEM((PADDED // 2, 2 * count), BF),
                pltpu.VMEM((PADDED // 2, 2 * count), BF),
                pltpu.VMEM((FF // 2, 2 * count), BF),
            ],
        ),
        out_shape=[wide(chips, steps * block)] * 2 + [wide(chips // 2, steps * block)] * 2 + [wide(chips // 2, OUT_BLOCKS * rows)] * 2,
        compiler_params=BIG,
        name="grad_ffn",
    )(place, own, other, back, back_other)


def grad_attn_kernel(place, own, other, grad, grad_other, keep, send):
    core, half = place[0], place[1]
    blocks = grad.shape[1] // LANES
    rows = keep.shape[1] // blocks
    turned = own_rows(both_t(own, other, FF + 2 * PADDED, PADDED), core, rows)
    out = dot(turned, jnp.concatenate([grad[...], grad_other[...]], 0)).astype(BF)
    write_split(out, keep, send, 0, rows, half)


def grad_attn(place, own, other, grad, grad_other, shards):
    rows = PADDED // shards
    shape = jax.ShapeDtypeStruct((shards // 4, grad.shape[1] // LANES * rows, LANES), BF)
    return pl.pallas_call(
        grad_attn_kernel,
        out_shape=(shape, shape),
        in_specs=[SMEM] + [VMEM] * 4,
        out_specs=[VMEM] * 2,
        compiler_params=BIG,
        name="grad_attn",
    )(place, own, other, grad, grad_other)


def spread_matrix(shards):
    size, room = D // shards, PADDED // shards
    feature = lax.broadcasted_iota(jnp.int32, (D, PADDED), 0)
    place = lax.broadcasted_iota(jnp.int32, (D, PADDED), 1)
    return (feature // size * room + feature % size == place).astype(BF)


def to_blocks(matrix):
    rows, width = matrix.shape
    return matrix.reshape(rows, width // LANES, LANES).transpose(1, 0, 2).reshape(-1, LANES)


def from_blocks(blocks, rows):
    return blocks.reshape(-1, rows, LANES).transpose(1, 0, 2).reshape(rows, -1)


def plus(left, right):
    return (left.astype(F32) + right.astype(F32)).astype(BF)


def after(value, *earlier):
    return lax.optimization_barrier((value,) + earlier)[0]


def scatter_z(parts):
    return lax.psum_scatter(parts, "z", scatter_dimension=0, tiled=False)


def to_owner(part, layer):
    return lax.ppermute(part, "section", [(1 - layer, layer)])


def total_over(values):
    count = lax.axis_size("z")
    for axis in ("core", "dp"):
        values = values + swap(values, axis)
    step = 1
    while step < count:
        values = values + lax.ppermute(values, "z", [(i, i ^ step) for i in range(count)])
        step *= 2
    return values + swap(values, "section")


def per_device_blocks(tokens, cotangent, positions, attn_gain, w_query, w_key, w_value, w_out, ffn_gain, w_gate, w_up, w_down):
    section, half = lax.axis_index("section"), lax.axis_index("dp")
    z_index, core = lax.axis_index("z"), lax.axis_index("core")
    plane = ("dp", "z", "core")
    size, ff_rows = w_query.shape[1], w_down.shape[1]
    shards = D // size
    room = PADDED // shards
    chips = shards // 2
    qkv_rows = QKV_BLOCKS * room
    block_range = jnp.stack([2 - core, 2 * z_index + 2]).astype(jnp.int32)
    place = jnp.stack([core, half, section]).astype(jnp.int32)
    spread = spread_matrix(shards)

    def mine(array_in):
        return lax.dynamic_index_in_dim(array_in, section, 0, keepdims=False)

    def widen(array_in):
        return project(array_in, spread).astype(BF)

    def padded(array_in):
        return jnp.pad(array_in, ((0, room - size), (0, 0)))

    gains = jnp.concatenate([attn_gain, ffn_gain], 0).T
    qkv = jnp.concatenate([w_key[0], w_value[0], w_query[0], gains, jnp.zeros((size, HD - 2), BF)], -1)
    narrow = jnp.concatenate([qkv, widen(w_out[0]), w_gate[0], w_up[0]], -1)
    shard = jnp.concatenate([to_blocks(padded(narrow)), to_blocks(widen(w_down[0]))], 0)
    got = swap(shard, "section")
    shard0 = jnp.where(section == 0, shard, got)
    shard1 = jnp.where(section == 0, got, shard)

    early = lax.all_gather(jnp.concatenate([shard0, shard1[:qkv_rows]], 0), plane, axis=0)
    late = lax.all_gather(after(shard1[qkv_rows:], early), plane, axis=0)
    base1 = shard0.shape[0]

    def gains_at(base):
        at = base + (QKV_BLOCKS - 1) * room
        gain = early[:, at : at + room, HD : HD + 2].reshape(-1, 2).T.astype(F32)
        return gain[:1], gain[1:]

    w0 = (early, 0, early, qkv_rows) + gains_at(0)
    w1 = (early, base1, late, 0) + gains_at(base1)
    angle_cos, angle_sin = rope_tables(mine(positions))
    cos = jnp.concatenate([angle_cos[:, 0]] * 2, -1)
    sin = jnp.concatenate([angle_sin[:, 0]] * 2, -1)

    def forward(x, layer):
        w_a, at_a, w_f, at_f, gain_a, gain_f = layer
        na, q, kv = qkv_forward(x, gain_a, cos, sin, w_a, at_a)
        kv_all = spread_kv(kv)
        o, lse = attend(block_range, q, kv_all)
        acts, mixed, g, u, y = ffn_forward(o, x, na, gain_f, spread, w_f, at_f)
        return y, (x, q, kv_all, o, lse, acts, mixed, g, u)

    y0, saved0 = forward(widen(mine(tokens)), w0)
    y1, saved1 = forward(y0, w1)

    def backward_ffn(dy, layer, saved):
        w_a, at_a, w_f, at_f, gain_a, gain_f = layer
        x, q, kv_all, o, lse, acts, mixed, g, u = saved
        return ffn_backward(dy, g, u, mixed, gain_f, spread, w_f, at_f)

    def backward_attn(do, saved):
        x, q, kv_all, o, lse, acts, mixed, g, u = saved
        return attend_back(block_range, q, o, do, lse, cos, sin, kv_all)

    def backward_qkv(dq, shares, dm, layer, saved):
        w_a, at_a, w_f, at_f, gain_a, gain_f = layer
        return qkv_backward(dq, shares, cos, sin, saved[0], gain_a, dm, w_a, at_a)

    def halve(total):
        split = total.reshape((2, chips // 2) + total.shape[1:])
        return lax.dynamic_index_in_dim(split, half, 0, False), lax.dynamic_index_in_dim(split, 1 - half, 0, False)

    acts1, acts0 = saved1[5], saved0[5]
    other1, other0 = swap(acts1, "core"), swap(acts0, "core")
    back1, dm1, do1, dgf1 = backward_ffn(widen(mine(cotangent)), w1, saved1)
    back_other1 = swap(back1, "core")
    dq1, dkv1 = backward_attn(do1, saved1)
    shares1 = collect_kv(dkv1)
    dq_other1 = swap(dq1, "core")
    keep_a1, send_a1, keep_u1, send_u1, keep_o1, send_o1 = grad_ffn(place, acts1, other1, back1, back_other1, shards)
    keep_q1, send_q1 = grad_attn(place, acts1, other1, dq1, dq_other1, shards)
    got_a1, got_u1 = swap(send_a1, "section"), swap(send_u1, "dp")
    got_o1, got_q1 = swap(send_o1, "dp"), swap(send_q1, "dp")
    dkv_low1, dx1, dga1 = backward_qkv(dq1, shares1, dm1, w1, saved1)
    dkv_other1 = swap(dkv_low1, "core")
    dx1_low = dx1.astype(BF)
    back0, dm0, do0, dgf0 = backward_ffn(dx1_low, w0, saved0)
    back_other0 = swap(back0, "core")
    keep_k1, send_k1 = grad_attn(place, acts1, other1, dkv_low1, dkv_other1, shards)
    got_k1 = swap(send_k1, "dp")
    do0 = after(do0, got_a1, got_u1, got_o1, got_q1)
    keep_a1, send_a1 = halve(plus(keep_a1, got_a1))
    got_a1 = swap(send_a1, "dp")
    part_u1 = scatter_z(plus(keep_u1, got_u1))
    dq0, dkv0 = backward_attn(do0, saved0)
    shares0 = collect_kv(dkv0)
    dq_other0 = swap(dq0, "core")
    keep_a0, send_a0, keep_u0, send_u0, keep_o0, send_o0 = grad_ffn(place, acts0, other0, back0, back_other0, shards)
    keep_q0, send_q0 = grad_attn(place, acts0, other0, dq0, dq_other0, shards)
    got_a0, got_u0 = swap(send_a0, "section"), swap(send_u0, "dp")
    got_o0, got_q0 = swap(send_o0, "dp"), swap(send_q0, "dp")
    part_a1 = scatter_z(plus(keep_a1, got_a1))
    oqk = lambda keeps, gots: jnp.concatenate([plus(keep, got) for keep, got in zip(keeps, gots)], 1)
    part_s1 = scatter_z(oqk((keep_o1, keep_q1, keep_k1), (got_o1, got_q1, got_k1)))
    dkv_low0, dx0, dga0 = backward_qkv(dq0, shares0, dm0, w0, saved0)
    dkv_other0 = swap(dkv_low0, "core")
    keep_k0, send_k0 = grad_attn(place, acts0, other0, dkv_low0, dkv_other0, shards)
    got_k0 = swap(send_k0, "dp")
    keep_a0, send_a0 = halve(plus(keep_a0, got_a0))
    got_a0 = swap(send_a0, "dp")
    part_u0 = scatter_z(plus(keep_u0, got_u0))
    part_a0 = scatter_z(plus(keep_a0, got_a0))
    part_s0 = scatter_z(oqk((keep_o0, keep_q0, keep_k0), (got_o0, got_q0, got_k0)))

    def whole(part_u, part_s, part_a, layer):
        u = part_u.astype(F32) + to_owner(part_u, layer).astype(F32)
        s = part_s.astype(F32) + to_owner(part_s, layer).astype(F32)
        away = to_owner(part_a, layer)
        down, gate = (part_a, away) if layer == 0 else (away, part_a)
        return u, s, gate.astype(F32), down.astype(F32)

    sums = zip(whole(part_u0, part_s0, part_a0, 0), whole(part_u1, part_s1, part_a1, 1))
    up, small, gate, down = (jnp.where(section == 0, own0, own1) for own0, own1 in sums)

    def narrow_low(array_in):
        return project_t(array_in, spread).astype(BF)

    def narrow_wide(array_in):
        return array_in.reshape(array_in.shape[0], shards, room)[:, :, :size].reshape(array_in.shape[0], D)

    def pair(own, got):
        return jnp.where(section == 0, jnp.stack([own, got]), jnp.stack([got, own]))

    got = swap(narrow_low(jnp.where(section == 0, y1, y0)), "section")
    section_out = pair(narrow_low(jnp.where(section == 0, y0, y1)), got)
    got = swap(narrow_low(jnp.where(section == 0, dx1_low, dx0.astype(BF))), "section").astype(F32)
    input_grad = pair(narrow_wide(jnp.where(section == 0, dx0, dx1_low.astype(F32))), got)
    up = from_blocks(up, room)[:size]
    gate = from_blocks(gate, room)[:size]
    small = from_blocks(small, room)[:size]
    down = narrow_wide(from_blocks(down, ff_rows))
    kd = KV * HD
    gain_grads = total_over(jnp.concatenate([dga0, dgf0, dga1, dgf1], 0)).reshape(2, 2, PADDED)
    gain = lax.dynamic_slice_in_dim(mine(gain_grads), lax.axis_index(plane) * room, room, 1)[:, :size]
    outs = (
        section_out,
        input_grad,
        gain[0],
        small[:, PADDED : PADDED + D],
        small[:, 2 * PADDED : 2 * PADDED + kd],
        small[:, 2 * PADDED + kd :],
        narrow_wide(small[:, :PADDED]),
        gain[1],
        gate,
        up,
        down,
    )
    return tuple(part[None] for part in outs)


def solution(mesh):
    sizes = mesh.devices.shape
    grid = Mesh(mesh.devices.reshape(sizes[0], sizes[1], sizes[2] // 2, 2), ("section", "dp", "z", "core"))
    ctx = ("z", "core")
    plane = ("dp", "z", "core")
    vector = P("section", plane)
    matrix = P("section", plane, None)
    in_specs = (
        P("dp", ctx, None),
        P("dp", ctx, None),
        P("dp", ctx),
        vector,
        matrix,
        matrix,
        matrix,
        matrix,
        vector,
        matrix,
        matrix,
        matrix,
    )
    acts = P("section", "dp", ctx, None)
    out_specs = (acts, acts, vector, matrix, matrix, matrix, matrix, vector, matrix, matrix, matrix)
    shards = sizes[1] * sizes[2]
    aligned = shards == 16
    return jax.shard_map(per_device_blocks if aligned else per_device, mesh=grid, in_specs=in_specs, out_specs=out_specs, check_vma=False)
```

time: 1640 us -> 831 us (0.51)
  blocking collectives: 530 us -> 0 us
  matrix products: 400 us -> 15.3 us
  Pallas kernels: 0 us -> 173 us
  other arithmetic: 109 us -> 41.2 us
  starting transfers between devices: 22.7 us -> 82.6 us
  local copies, waits for them, and re-layouts: 93.7 us -> 35.7 us
    unnamed x3 -> x0, blocking collectives: 463 us -> none
    dot_general x154 -> x7, matrix products: 400 us -> 15.3 us  [the longest x4 8.48 us: project(): return jnp.dot(left, right, preferred_element_type=F32)]
    ppermute x4 -> x50, waiting for transfers between devices: 41.8 us -> 332 us  [the longest x12 160 us: move_z(): return lax.ppermute(block, 'z', route)]
    pallas_call x0 -> x18, Pallas kernels: none -> 173 us  [the longest x2 37.4 us: grad_ffn(): pl.pallas_call(grad_ffn_kernel, grid_spec=pltpu.PrefetchScalarGridSpec(nu...]
    all_gather x11 -> x2, waiting for transfers between devices: 283 us -> 127 us  [the longest x1 127 us: per_device_blocks(): lax.all_gather(jnp.concatenate([shard0, shard1[:qkv_rows]], 0), plane, ax...]
    reduce_scatter x7 -> x6, waiting for transfers between devices: 124 us -> 0.03 us  [scatter_z(): return lax.psum_scatter(parts, 'z', scatter_dimension=0, tiled=False)]
    ppermute x4 -> x50, starting transfers between devices: 7.9 us -> 81.9 us  [the longest x12 41.6 us: move_z(): return lax.ppermute(block, 'z', route)]
    all_gather x2 -> x0, blocking collectives: 67.6 us -> none  [the longest x1 37.2 us: per_device(): lax.all_gather(shards[3], ('dp', 'ctx'), axis=0, tiled=True)]
  transfers between devices with their start and end apart: 28 -> 58, of which waited for: 18 -> 26; matrix products, arithmetic and copies ran while one was open for 37% -> 8% of each run, Pallas kernels for 0% -> 17%
where the time goes in v1:
time: 831 us; the launch traced here: 822 us
  waiting for transfers between devices  459 us (55%)
  Pallas kernels  173 us (21%)
  starting transfers between devices  82.6 us (10%)
  other arithmetic  41.2 us (5%)
  local copies, waits for them, and re-layouts  35.7 us (4%)
  between operations  15.8 us (2%)
  matrix products  15.3 us (2%)
    ppermute x12, waiting for transfers between devices, move_z(): return lax.ppermute(block, 'z', route)  160 us
    ppermute x30, waiting for transfers between devices, swap(): return lax.ppermute(block, axis, [(0, 1), (1, 0)])  159 us
    all_gather x1, waiting for transfers between devices, per_device_blocks(): lax.all_gather(jnp.concatenate([shard0, shard1[:qkv_rows]], 0), plane, ax...  127 us
    ppermute x12, starting transfers between devices, move_z(): return lax.ppermute(block, 'z', route)  41.6 us
    pallas_call x2, Pallas kernels, grad_ffn(): pl.pallas_call(grad_ffn_kernel, grid_spec=pltpu.PrefetchScalarGridSpec(nu...  37.4 us
    pallas_call x2, Pallas kernels, ffn_backward(): pl.pallas_call(functools.partial(ffn_back_kernel, first), grid=(FF // CHU...  36.5 us
    ppermute x30, starting transfers between devices, swap(): return lax.ppermute(block, axis, [(0, 1), (1, 0)])  29 us
    pallas_call x2, Pallas kernels, ffn_forward(): pl.pallas_call(functools.partial(ffn_kernel, first), grid=(FF // CHUNK,),...  26.5 us
  transfers between devices with their start and end apart: 58, of which 26 were waited for; matrix products, arithmetic and copies ran while one was open for 8% of the time, Pallas kernels for 17%

profile of v1, /device:TPU:0, one launch (start us, length us, event | category | flops | bytes accessed | tf_op | source)
XLA Modules:
  0.0 822.3 jit_solution(17302373111973168193)
XLA Ops:
  21.1 29.2 %collective-permute-done = bf16[5184,128]{1,0:T(8,128)(2,1)} collective-permute-done((bf16[5184,128]{1,0:T(8,128)(2,1)S(1)}, bf16[5184,128]{1,0:T(8,128)(2,1)}, u32[]{:S(2)}, u32[]{:S(2)}) %collective-permute-start) | collective-permute-done | bytes 1327136 | tf_op jit(solution)/shard_map/ppermute | solution.py:153
  54.6 126.7 %all-gather.5.cloned.1.call-done = bf16[96256,128]{1,0:T(8,128)(2,1)} async-done(((bf16[6016,128]{1,0:T(8,128)(2,1)}), bf16[96256,128]{1,0:T(8,128)(2,1)}) %all-gather.5.cloned.1.call-update) | async-done | bytes 24641552 | tf_op jit(solution)/shard_map/all_gather | solution.py:1042
  187.1 6.7 qkv_forward.2
  202.7 9.5 %collective-permute-done.1.refs_1_ = bf16[256,640]{1,0:T(8,128)(2,1)S(1)} collective-permute-done((bf16[256,640]{1,0:T(8,128)(2,1)}, bf16[256,640]{1,0:T(8,128)(2,1)S(1)}, u32[]{:S(2)}, u32[]{:S(2)}) %collective-permute-start.1) | collective-permute-done | bytes 327712 | tf_op jit(solution)/shard_map/ppermute | solution.py:159
  212.2 14.0 %collective-permute-done.2.refs_2_ = bf16[256,640]{1,0:T(8,128)(2,1)S(1)} collective-permute-done((bf16[256,640]{1,0:T(8,128)(2,1)}, bf16[256,640]{1,0:T(8,128)(2,1)S(1)}, u32[]{:S(2)}, u32[]{:S(2)}) %collective-permute-start.2) | collective-permute-done | bytes 327712 | tf_op jit(solution)/shard_map/ppermute | solution.py:159
  226.3 13.8 %collective-permute-done.3.refs_3_ = bf16[256,640]{1,0:T(8,128)(2,1)S(1)} collective-permute-done((bf16[256,640]{1,0:T(8,128)(2,1)}, bf16[256,640]{1,0:T(8,128)(2,1)S(1)}, u32[]{:S(2)}, u32[]{:S(2)}) %collective-permute-start.3) | collective-permute-done | bytes 327712 | tf_op jit(solution)/shard_map/ppermute | solution.py:159
  253.9 13.4 %ffn_forward.2 = (bf16[256,5632]{1,0:T(8,128)(2,1)}, f32[256,1024]{1,0:T(8,128)}, f32[256,2560]{1,0:T(8,128)}, f32[256,2560]{1,0:T(8,128)}, bf16[256,1024]{1,0:T(8,128)(2,1)}) custom-call(bf16[256,960]{1,0:T(8,128)(2,1)} %get-tuple-element.73.o_ref, bf16[256,1024]{1,0:T(8,128)(2,1)} %convolution_convert_fusion.1.x_ref, ...), custom_call_target="tpu_custom_call" | custom-call | tf_op jit(solution)/shard_map/ffn_forward/pallas_call | solution.py:700
  273.5 8.0 collective-permute-start.5
  281.5 15.6 %collective-permute-start.6 = (bf16[256,640]{1,0:T(8,128)(2,1)}, bf16[256,640]{1,0:T(8,128)(2,1)S(1)}, u32[]{:S(2)}, u32[]{:S(2)}) collective-permute-start(bf16[256,640]{1,0:T(8,128)(2,1)} %get-tuple-element.77.refs_0_), channel_id=1, source_target_pairs={{0,4},{2,6},{1,5},{3,7},{8,12},{10,14},{9,13},{11,15},{16,20},{18,... | collective-permute-start | bytes 983048 | tf_op jit(solution)/shard_map/ppermute | solution.py:159
  298.5 9.0 %collective-permute-done.6.refs_2_ = bf16[256,640]{1,0:T(8,128)(2,1)S(1)} collective-permute-done((bf16[256,640]{1,0:T(8,128)(2,1)}, bf16[256,640]{1,0:T(8,128)(2,1)S(1)}, u32[]{:S(2)}, u32[]{:S(2)}) %collective-permute-start.6) | collective-permute-done | bytes 327712 | tf_op jit(solution)/shard_map/ppermute | solution.py:159
  307.4 7.0 collective-permute-done.7.refs_3_
  320.2 6.6 attend.3
  326.9 13.1 %ffn_forward.3 = (bf16[256,5632]{1,0:T(8,128)(2,1)}, f32[256,1024]{1,0:T(8,128)}, f32[256,2560]{1,0:T(8,128)}, f32[256,2560]{1,0:T(8,128)}, bf16[256,1024]{1,0:T(8,128)(2,1)}) custom-call(bf16[256,960]{1,0:T(8,128)(2,1)} %get-tuple-element.78.o_ref, bf16[256,1024]{1,0:T(8,128)(2,1)} %get-tuple-element.75.x_ref, bf16[256,1024]{1,0:T(8,128)(2,1)} %get-tuple-element.79.na_ref, ...), custom_call_target="tpu_custom_call" | custom-call | tf_op jit(solution)/shard_map/ffn_forward/pallas_call | solution.py:700
  340.0 18.4 %ffn_backward.2 = (bf16[256,7168]{1,0:T(8,128)(2,1)}, f32[256,1024]{1,0:T(8,128)}, bf16[256,960]{1,0:T(8,128)(2,1)}, f32[1,1024]{1,0:T(1,128)}) custom-call(bf16[256,1024]{1,0:T(8,128)(2,1)} %convolution_convert_fusion.dy_ref, f32[256,2560]{1,0:T(8,128)} %get-tuple-element.82.g_ref, f32[256,2560]{1,0:T(8,128)} %get-tuple-element.83.u_ref, ...), custom_call_target="tpu_custom_call" | custom-call | tf_op jit(solution)/shard_map/ffn_backward/pallas_call | solution.py:780
  361.4 7.8 attend_back.2
  381.4 28.4 %collective-permute-done.11.refs_1_ = bf16[256,640]{1,0:T(8,128)(2,1)S(1)} collective-permute-done((bf16[256,640]{1,0:T(8,128)(2,1)S(1)}, bf16[256,640]{1,0:T(8,128)(2,1)S(1)}, u32[]{:S(2)}, u32[]{:S(2)}) %collective-permute-start.11) | collective-permute-done | bytes 327712 | tf_op jit(solution)/shard_map/ppermute | solution.py:159
  409.8 8.2 collective-permute-done.12.refs_2_
  418.0 27.1 %collective-permute-done.13.refs_3_ = bf16[256,640]{1,0:T(8,128)(2,1)S(1)} collective-permute-done((bf16[256,640]{1,0:T(8,128)(2,1)S(1)}, bf16[256,640]{1,0:T(8,128)(2,1)S(1)}, u32[]{:S(2)}, u32[]{:S(2)}) %collective-permute-start.13) | collective-permute-done | bytes 327712 | tf_op jit(solution)/shard_map/ppermute | solution.py:159
  445.8 6.6 qkv_backward.2
  465.8 18.8 %grad_ffn.2 = (bf16[8,1280,128]{2,1,0:T(8,128)(2,1)}, bf16[8,1280,128]{2,1,0:T(8,128)(2,1)}, bf16[4,1280,128]{2,1,0:T(8,128)(2,1)}, bf16[4,1280,128]{2,1,0:T(8,1...) custom-call(s32[3]{0:T(128)} %pad_add_fusion.1.place, bf16[256,5632]{1,0:T(8,128)(2,1)} %get-tuple-element.95.own, ...), custom_call_target="tpu_custom_call" | custom-call | tf_op jit(solution)/shard_map/grad_ffn/pallas_call | solution.py:928
  486.4 18.1 %ffn_backward.3 = (bf16[256,7168]{1,0:T(8,128)(2,1)}, f32[256,1024]{1,0:T(8,128)}, bf16[256,960]{1,0:T(8,128)(2,1)}, f32[1,1024]{1,0:T(1,128)}) custom-call(bf16[256,1024]{1,0:T(8,128)(2,1)} %convert_element_type.271.dy_ref, f32[256,2560]{1,0:T(8,128)} %get-tuple-element.91.g_ref, f32[256,2560]{1,0:T(8,128)} %get-tuple-element.92.u_ref, ...), custom_call_target="tpu_custom_call" | custom-call | tf_op jit(solution)/shard_map/ffn_backward/pallas_call | solution.py:780
  510.5 28.9 %collective-permute-done.17 = bf16[4,1280,128]{2,1,0:T(8,128)(2,1)S(1)} collective-permute-done((bf16[4,1280,128]{2,1,0:T(8,128)(2,1)}, bf16[4,1280,128]{2,1,0:T(8,128)(2,1)S(1)}, u32[]{:S(2)}, u32[]{:S(2)}) %collective-permute-start.17) | collective-permute-done | bytes 1310752 | tf_op jit(solution)/shard_map/ppermute | solution.py:153
  542.1 18.6 %grad_ffn.3 = (bf16[8,1280,128]{2,1,0:T(8,128)(2,1)}, bf16[8,1280,128]{2,1,0:T(8,128)(2,1)}, bf16[4,1280,128]{2,1,0:T(8,128)(2,1)}, bf16[4,1280,128]{2,1,0:T(8,1...) custom-call(s32[3]{0:T(128)} %pad_add_fusion.1.place, bf16[256,5632]{1,0:T(8,128)(2,1)} %get-tuple-element.111.own, ...), custom_call_target="tpu_custom_call" | custom-call | tf_op jit(solution)/shard_map/grad_ffn/pallas_call | solution.py:928
  568.3 7.7 attend_back.3
  580.3 11.2 %collective-permute-done.46 = bf16[4,1280,128]{2,1,0:T(8,128)(2,1)S(1)} collective-permute-done((bf16[4,1280,128]{2,1,0:T(8,128)(2,1)}, bf16[4,1280,128]{2,1,0:T(8,128)(2,1)S(1)}, u32[]{:S(2)}, u32[]{:S(2)}) %collective-permute-start.46) | collective-permute-done | bytes 1310752 | tf_op jit(solution)/shard_map/ppermute | solution.py:153
  601.4 26.9 %collective-permute-done.22.refs_1_ = bf16[256,640]{1,0:T(8,128)(2,1)S(1)} collective-permute-done((bf16[256,640]{1,0:T(8,128)(2,1)S(1)}, bf16[256,640]{1,0:T(8,128)(2,1)S(1)}, u32[]{:S(2)}, u32[]{:S(2)}) %collective-permute-start.22) | collective-permute-done | bytes 327712 | tf_op jit(solution)/shard_map/ppermute | solution.py:159
  633.6 10.6 %collective-permute-done.24.refs_3_ = bf16[256,640]{1,0:T(8,128)(2,1)S(1)} collective-permute-done((bf16[256,640]{1,0:T(8,128)(2,1)S(1)}, bf16[256,640]{1,0:T(8,128)(2,1)S(1)}, u32[]{:S(2)}, u32[]{:S(2)}) %collective-permute-start.24) | collective-permute-done | bytes 327712 | tf_op jit(solution)/shard_map/ppermute | solution.py:159
  671.9 6.5 collective-permute-done.37
  684.5 30.4 %collective-permute-done.45 = bf16[4,1280,128]{2,1,0:T(8,128)(2,1)} collective-permute-done((bf16[4,1280,128]{2,1,0:T(8,128)(2,1)}, bf16[4,1280,128]{2,1,0:T(8,128)(2,1)}, u32[]{:S(2)}, u32[]{:S(2)}) %collective-permute-start.45) | collective-permute-done | bytes 1310752 | tf_op jit(solution)/shard_map/ppermute | solution.py:153
  729.1 23.3 %collective-permute-done.27 = f32[4,1024]{1,0:T(4,128)S(1)} collective-permute-done((f32[4,1024]{1,0:T(4,128)S(1)}, f32[4,1024]{1,0:T(4,128)S(1)}, u32[]{:S(2)}, u32[]{:S(2)}) %collective-permute-start.27) | collective-permute-done | bytes 16416 | tf_op jit(solution)/shard_map/ppermute | solution.py:153
  768.3 12.3 %collective-permute-done.30 = f32[4,1024]{1,0:T(4,128)S(1)} collective-permute-done((f32[4,1024]{1,0:T(4,128)S(1)}, f32[4,1024]{1,0:T(4,128)S(1)}, u32[]{:S(2)}, u32[]{:S(2)}) %collective-permute-start.30) | collective-permute-done | bytes 16416 | tf_op jit(solution)/shard_map/ppermute | solution.py:153
  785.7 8.4 %collective-permute-done.47 = bf16[1280,128]{1,0:T(8,128)(2,1)S(1)} collective-permute-done((bf16[1280,128]{1,0:T(8,128)(2,1)}, bf16[1280,128]{1,0:T(8,128)(2,1)S(1)}, u32[]{:S(2)}, u32[]{:S(2)}) %collective-permute-start.47) | collective-permute-done | bytes 327712 | tf_op jit(solution)/shard_map/ppermute | solution.py:998
  (332 shorter events, 215.6 us)
Async XLA Ops:
  7.2 174.1 %all-gather.5.cloned.1.call-start = ((), (), s32[]{:S(2)}) async-start(), calls=%async_computation.12 | async-start | bytes 26181632 | tf_op jit(solution)/shard_map/all_gather | solution.py:1042
  18.1 32.2 %collective-permute-start = (bf16[5184,128]{1,0:T(8,128)(2,1)S(1)}, bf16[5184,128]{1,0:T(8,128)(2,1)}, u32[]{:S(2)}, u32[]{:S(2)}) collective-permute-start(bf16[5184,128]{1,0:T(8,128)(2,1)S(1)} %pad_maximum_fusion.3), channel_id=1, source_target_pairs={{0,16},{16,0},{1,17},{17,1},{2,18},{18,2},{3,19},{19,3},{4,20},{20... | collective-permute-start | bytes 3981320 | tf_op jit(solution)/shard_map/ppermute | solution.py:153
  53.5 273.4 %all-gather.7.cloned.1.call-start = ((), (), s32[]{:S(2)}) async-start(), calls=%async_computation.13 | async-start | bytes 18939904 | tf_op jit(solution)/shard_map/all_gather | solution.py:1043
  181.3 572.3 %reduce-scatter.9.cloned.1.call-start = ((), (), s32[]{:S(2)}) async-start(), calls=%async_computation.7 | async-start | bytes 1720320 | tf_op jit(solution)/shard_map/reduce_scatter | solution.py:994
  201.2 38.9 %collective-permute-start.3 = (bf16[256,640]{1,0:T(8,128)(2,1)}, bf16[256,640]{1,0:T(8,128)(2,1)S(1)}, u32[]{:S(2)}, u32[]{:S(2)}) collective-permute-start(bf16[256,640]{1,0:T(8,128)(2,1)} %get-tuple-element.72.refs_0_), channel_id=1, source_target_pairs={{0,6},{1,7},{8,14},{9,15},{16,22},{17,23},{24,30},{25,31}} | collective-permute-start | bytes 983048 | tf_op jit(solution)/shard_map/ppermute | solution.py:159
  358.4 107.4 %collective-permute-start.15 = (bf16[256,7168]{1,0:T(8,128)(2,1)}, bf16[256,7168]{1,0:T(8,128)(2,1)}, u32[]{:S(2)}, u32[]{:S(2)}) collective-permute-start(bf16[256,7168]{1,0:T(8,128)(2,1)} %get-tuple-element.96.back), channel_id=1, source_target_pairs={{0,1},{1,0},{2,3},{3,2},{4,5},{5,4},{6,7},{7,6},{8,9},{9,8},{10,11... | collective-permute-start | bytes 11010056 | tf_op jit(solution)/shard_map/ppermute | solution.py:153
  361.3 93.2 %collective-permute-start.14 = (bf16[256,5632]{1,0:T(8,128)(2,1)S(1)}, bf16[256,5632]{1,0:T(8,128)(2,1)}, u32[]{:S(2)}, u32[]{:S(2)}) collective-permute-start(bf16[256,5632]{1,0:T(8,128)(2,1)S(1)} %copy-done.3), channel_id=1, source_target_pairs={{0,1},{1,0},{2,3},{3,2},{4,5},{5,4},{6,7},{7,6},{8,9},{9,8},{10,11... | collective-permute-start | bytes 8650760 | tf_op jit(solution)/shard_map/ppermute | solution.py:153
  377.6 32.3 %collective-permute-start.11 = (bf16[256,640]{1,0:T(8,128)(2,1)S(1)}, bf16[256,640]{1,0:T(8,128)(2,1)S(1)}, u32[]{:S(2)}, u32[]{:S(2)}) collective-permute-start(bf16[256,640]{1,0:T(8,128)(2,1)S(1)} %get-tuple-element.174), channel_id=1, source_target_pairs={{2,0},{4,2},{6,4},{3,1},{5,3},{7,5},{10,8},{12,10},{14,12},{11,9},... | collective-permute-start | bytes 983048 | tf_op jit(solution)/shard_map/ppermute | solution.py:159
  378.8 39.2 %collective-permute-start.12 = (bf16[256,640]{1,0:T(8,128)(2,1)S(1)}, bf16[256,640]{1,0:T(8,128)(2,1)S(1)}, u32[]{:S(2)}, u32[]{:S(2)}) collective-permute-start(bf16[256,640]{1,0:T(8,128)(2,1)S(1)} %get-tuple-element.173), channel_id=1, source_target_pairs={{4,0},{6,2},{5,1},{7,3},{12,8},{14,10},{13,9},{15,11},{20,16},{22,... | collective-permute-start | bytes 983048 | tf_op jit(solution)/shard_map/ppermute | solution.py:159
  380.1 65.0 %collective-permute-start.13 = (bf16[256,640]{1,0:T(8,128)(2,1)S(1)}, bf16[256,640]{1,0:T(8,128)(2,1)S(1)}, u32[]{:S(2)}, u32[]{:S(2)}) collective-permute-start(bf16[256,640]{1,0:T(8,128)(2,1)S(1)} %get-tuple-element.172), channel_id=1, source_target_pairs={{6,0},{7,1},{14,8},{15,9},{22,16},{23,17},{30,24},{31,25}} | collective-permute-start | bytes 983048 | tf_op jit(solution)/shard_map/ppermute | solution.py:159
  409.8 50.1 %collective-permute-start.19 = (bf16[256,1024]{1,0:T(8,128)(2,1)S(1)}, bf16[256,1024]{1,0:T(8,128)(2,1)}, u32[]{:S(2)}, u32[]{:S(2)}) collective-permute-start(bf16[256,1024]{1,0:T(8,128)(2,1)S(1)} %copy-done.19), channel_id=1, source_target_pairs={{0,1},{1,0},{2,3},{3,2},{4,5},{5,4},{6,7},{7,6},{8,9},{9,8},{10,11... | collective-permute-start | bytes 1572872 | tf_op jit(solution)/shard_map/ppermute | solution.py:153
  459.0 45.7 %collective-permute-start.40 = (bf16[4,320,128]{2,1,0:T(8,128)(2,1)}, bf16[4,320,128]{2,1,0:T(8,128)(2,1)S(1)}, u32[]{:S(2)}, u32[]{:S(2)}) collective-permute-start(bf16[4,320,128]{2,1,0:T(8,128)(2,1)} %get-tuple-element.124), channel_id=1, source_target_pairs={{0,8},{8,0},{1,9},{9,1},{2,10},{10,2},{3,11},{11,3},{4,12},{12,4},... | collective-permute-start | bytes 983048 | tf_op jit(solution)/shard_map/ppermute | solution.py:153
  464.7 40.1 %collective-permute-start.20 = (bf16[4,512,128]{2,1,0:T(8,128)(2,1)}, bf16[4,512,128]{2,1,0:T(8,128)(2,1)S(1)}, u32[]{:S(2)}, u32[]{:S(2)}) collective-permute-start(bf16[4,512,128]{2,1,0:T(8,128)(2,1)} %get-tuple-element.100), channel_id=1, source_target_pairs={{0,8},{8,0},{1,9},{9,1},{2,10},{10,2},{3,11},{11,3},{4,12},{12,4},... | collective-permute-start | bytes 1572872 | tf_op jit(solution)/shard_map/ppermute | solution.py:153
  504.6 37.6 %collective-permute-start.32 = (bf16[256,7168]{1,0:T(8,128)(2,1)}, bf16[256,7168]{1,0:T(8,128)(2,1)}, u32[]{:S(2)}, u32[]{:S(2)}) collective-permute-start(bf16[256,7168]{1,0:T(8,128)(2,1)} %get-tuple-element.112.back), channel_id=1, source_target_pairs={{0,1},{1,0},{2,3},{3,2},{4,5},{5,4},{6,7},{7,6},{8,9},{9,8},{10,11... | collective-permute-start | bytes 11010056 | tf_op jit(solution)/shard_map/ppermute | solution.py:153
  506.9 250.0 %reduce-scatter.17.cloned.1.call-start = ((), (), s32[]{:S(2)}) async-start(), calls=%async_computation.11 | async-start | bytes 1638400 | tf_op jit(solution)/shard_map/reduce_scatter | solution.py:994
  507.9 34.2 %collective-permute-start.31 = (bf16[256,5632]{1,0:T(8,128)(2,1)S(1)}, bf16[256,5632]{1,0:T(8,128)(2,1)}, u32[]{:S(2)}, u32[]{:S(2)}) collective-permute-start(bf16[256,5632]{1,0:T(8,128)(2,1)S(1)} %copy-done.2), channel_id=1, source_target_pairs={{0,1},{1,0},{2,3},{3,2},{4,5},{5,4},{6,7},{7,6},{8,9},{9,8},{10,11... | collective-permute-start | bytes 8650760 | tf_op jit(solution)/shard_map/ppermute | solution.py:153
  507.9 31.4 %collective-permute-start.17 = (bf16[4,1280,128]{2,1,0:T(8,128)(2,1)}, bf16[4,1280,128]{2,1,0:T(8,128)(2,1)S(1)}, u32[]{:S(2)}, u32[]{:S(2)}) collective-permute-start(bf16[4,1280,128]{2,1,0:T(8,128)(2,1)} %get-tuple-element.98), channel_id=1, source_target_pairs={{0,8},{8,0},{1,9},{9,1},{2,10},{10,2},{3,11},{11,3},{4,12},{12,4},... | collective-permute-start | bytes 3932168 | tf_op jit(solution)/shard_map/ppermute | solution.py:153
  509.0 59.3 %collective-permute-start.16 = (bf16[8,1280,128]{2,1,0:T(8,128)(2,1)}, bf16[8,1280,128]{2,1,0:T(8,128)(2,1)}, u32[]{:S(2)}, u32[]{:S(2)}) collective-permute-start(bf16[8,1280,128]{2,1,0:T(8,128)(2,1)} %get-tuple-element.97), channel_id=1, source_target_pairs={{0,16},{16,0},{1,17},{17,1},{2,18},{18,2},{3,19},{19,3},{4,20},{20... | collective-permute-start | bytes 7864328 | tf_op jit(solution)/shard_map/ppermute | solution.py:153
  542.1 239.2 %reduce-scatter.15.cloned.1.call-start = ((), (), s32[]{:S(2)}) async-start(), calls=%async_computation.10 | async-start | bytes 1638400 | tf_op jit(solution)/shard_map/reduce_scatter | solution.py:994
  560.8 30.8 %collective-permute-start.46 = (bf16[4,1280,128]{2,1,0:T(8,128)(2,1)}, bf16[4,1280,128]{2,1,0:T(8,128)(2,1)S(1)}, u32[]{:S(2)}, u32[]{:S(2)}) collective-permute-start(bf16[4,1280,128]{2,1,0:T(8,128)(2,1)} %get-tuple-element.129), channel_id=1, source_target_pairs={{0,8},{8,0},{1,9},{9,1},{2,10},{10,2},{3,11},{11,3},{4,12},{12,4},... | collective-permute-start | bytes 3932168 | tf_op jit(solution)/shard_map/ppermute | solution.py:153
  593.0 191.1 %reduce-scatter.7.cloned.1.call-start = ((), (), s32[]{:S(2)}) async-start(), calls=%async_computation.6 | async-start | bytes 1720320 | tf_op jit(solution)/shard_map/reduce_scatter | solution.py:994
  593.3 58.1 %collective-permute-start.34 = (bf16[256,1024]{1,0:T(8,128)(2,1)S(1)}, bf16[256,1024]{1,0:T(8,128)(2,1)S(1)}, u32[]{:S(2)}, u32[]{:S(2)}) collective-permute-start(bf16[256,1024]{1,0:T(8,128)(2,1)S(1)} %copy-done.18), channel_id=1, source_target_pairs={{0,1},{1,0},{2,3},{3,2},{4,5},{5,4},{6,7},{7,6},{8,9},{9,8},{10,11... | collective-permute-start | bytes 1572872 | tf_op jit(solution)/shard_map/ppermute | solution.py:153
  596.4 31.9 %collective-permute-start.22 = (bf16[256,640]{1,0:T(8,128)(2,1)S(1)}, bf16[256,640]{1,0:T(8,128)(2,1)S(1)}, u32[]{:S(2)}, u32[]{:S(2)}) collective-permute-start(bf16[256,640]{1,0:T(8,128)(2,1)S(1)} %get-tuple-element.170), channel_id=1, source_target_pairs={{2,0},{4,2},{6,4},{3,1},{5,3},{7,5},{10,8},{12,10},{14,12},{11,9},... | collective-permute-start | bytes 983048 | tf_op jit(solution)/shard_map/ppermute | solution.py:159
  597.7 35.9 %collective-permute-start.23 = (bf16[256,640]{1,0:T(8,128)(2,1)S(1)}, bf16[256,640]{1,0:T(8,128)(2,1)S(1)}, u32[]{:S(2)}, u32[]{:S(2)}) collective-permute-start(bf16[256,640]{1,0:T(8,128)(2,1)S(1)} %get-tuple-element.169), channel_id=1, source_target_pairs={{4,0},{6,2},{5,1},{7,3},{12,8},{14,10},{13,9},{15,11},{20,16},{22,... | collective-permute-start | bytes 983048 | tf_op jit(solution)/shard_map/ppermute | solution.py:159
  599.0 45.2 %collective-permute-start.24 = (bf16[256,640]{1,0:T(8,128)(2,1)S(1)}, bf16[256,640]{1,0:T(8,128)(2,1)S(1)}, u32[]{:S(2)}, u32[]{:S(2)}) collective-permute-start(bf16[256,640]{1,0:T(8,128)(2,1)S(1)} %get-tuple-element.168), channel_id=1, source_target_pairs={{6,0},{7,1},{14,8},{15,9},{22,16},{23,17},{30,24},{31,25}} | collective-permute-start | bytes 983048 | tf_op jit(solution)/shard_map/ppermute | solution.py:159
  600.3 65.2 %collective-permute-start.33 = (bf16[4,512,128]{2,1,0:T(8,128)(2,1)}, bf16[4,512,128]{2,1,0:T(8,128)(2,1)S(1)}, u32[]{:S(2)}, u32[]{:S(2)}) collective-permute-start(bf16[4,512,128]{2,1,0:T(8,128)(2,1)} %get-tuple-element.114), channel_id=1, source_target_pairs={{0,8},{8,0},{1,9},{9,1},{2,10},{10,2},{3,11},{11,3},{4,12},{12,4},... | collective-permute-start | bytes 1572872 | tf_op jit(solution)/shard_map/ppermute | solution.py:153
  657.2 60.5 %collective-permute-start.42 = (bf16[8,1280,128]{2,1,0:T(8,128)(2,1)}, bf16[8,1280,128]{2,1,0:T(8,128)(2,1)}, u32[]{:S(2)}, u32[]{:S(2)}) collective-permute-start(bf16[8,1280,128]{2,1,0:T(8,128)(2,1)} %get-tuple-element.126), channel_id=1, source_target_pairs={{0,16},{16,0},{1,17},{17,1},{2,18},{18,2},{3,19},{19,3},{4,20},{20... | collective-permute-start | bytes 7864328 | tf_op jit(solution)/shard_map/ppermute | solution.py:153
  679.7 117.4 %reduce-scatter.13.cloned.1.call-start = ((), (), s32[]{:S(2)}) async-start(), calls=%async_computation.9 | async-start | bytes 1638400 | tf_op jit(solution)/shard_map/reduce_scatter | solution.py:994
  684.1 30.8 %collective-permute-start.45 = (bf16[4,1280,128]{2,1,0:T(8,128)(2,1)}, bf16[4,1280,128]{2,1,0:T(8,128)(2,1)}, u32[]{:S(2)}, u32[]{:S(2)}) collective-permute-start(bf16[4,1280,128]{2,1,0:T(8,128)(2,1)} %dynamic-slice_bitcast_fusion), channel_id=1, source_target_pairs={{0,8},{8,0},{1,9},{9,1},{2,10},{10,2},{3,11},{11,3},{4,12},{12,4},... | collective-permute-start | bytes 3932168 | tf_op jit(solution)/shard_map/ppermute | solution.py:153
  717.7 86.2 %reduce-scatter.11.cloned.1.call-start = ((), (), s32[]{:S(2)}) async-start(), calls=%async_computation.8 | async-start | bytes 1638400 | tf_op jit(solution)/shard_map/reduce_scatter | solution.py:994
  722.2 36.9 %collective-permute-start.43 = (bf16[4,1280,128]{2,1,0:T(8,128)(2,1)}, bf16[4,1280,128]{2,1,0:T(8,128)(2,1)}, u32[]{:S(2)}, u32[]{:S(2)}) collective-permute-start(bf16[4,1280,128]{2,1,0:T(8,128)(2,1)} %dynamic-slice_bitcast_fusion.1), channel_id=1, source_target_pairs={{0,8},{8,0},{1,9},{9,1},{2,10},{10,2},{3,11},{11,3},{4,12},{12,4},... | collective-permute-start | bytes 3932168 | tf_op jit(solution)/shard_map/ppermute | solution.py:153
  753.6 45.1 %collective-permute-start.41 = (bf16[1344,128]{1,0:T(8,128)(2,1)}, bf16[1344,128]{1,0:T(8,128)(2,1)S(1)}, u32[]{:S(2)}, u32[]{:S(2)}) collective-permute-start(bf16[1344,128]{1,0:T(8,128)(2,1)} %bitcast.184), channel_id=1, source_target_pairs={{0,16},{1,17},{2,18},{3,19},{4,20},{5,21},{6,22},{7,23},{8,24},{9,... | collective-permute-start | bytes 1032200 | tf_op jit(solution)/shard_map/ppermute | solution.py:998
  (85 other events, 1643.8 us)
Sparse Core Ops, SparseCore 0:
  53.6 127.6 all-gather.4
  182.9 120.1 all-gather.6
  507.1 29.9 reduce-scatter.8
  542.2 28.9 reduce-scatter.16
  593.2 50.7 reduce-scatter.14
  679.8 29.3 reduce-scatter.6
  717.8 28.3 reduce-scatter.12
  762.0 31.5 reduce-scatter.10

commit v2 on v1

--- a/solution.py
+++ b/solution.py
@@ -342,8 +342,10 @@
 LANES = 128
 PADDED = 1024
 CHUNK = 640
+WIDE = 512
 KVW = 2 * KV * HD
 QKV_BLOCKS = 13
+EXTRA = 16
 ACTS = FF + 3 * PADDED
 BACK = 2 * FF + 2 * PADDED
 OUT_BLOCKS = PADDED // LANES
@@ -354,6 +356,10 @@
 BIG = pltpu.CompilerParams(vmem_limit_bytes=56 << 20)
 
 
+def cost(microseconds):
+    return pl.CostEstimate(flops=int(microseconds * 1.15e9), bytes_accessed=int(microseconds * 3.69e6), transcendentals=0)
+
+
 def dot_nt(left, right):
     return lax.dot_general(left, right, (((1,), (1,)), ((), ())), preferred_element_type=F32)
 
@@ -393,10 +399,12 @@
 
 
 def attend_kernel(zs, rng, q_ref, *refs):
-    blocks, (other, o_ref, lse_ref, kv_s, qt, vt, m_s, l_s, acc, sems) = refs[:zs], refs[zs:]
+    blocks, (other, e_hbm, o_ref, op_ref, lse_ref, kv_s, qt, vt, m_s, l_s, acc, e_s, sems) = refs[:zs], refs[zs:]
     T = q_ref.shape[0]
     W = G * T
     copies = load_kv(blocks, other, kv_s, sems)
+    spread = pltpu.make_async_copy(e_hbm, e_s, sems.at[zs + 1])
+    spread.start()
     qt[...] = q_ref[...].astype(F32).T.astype(BF)
     for copy in copies:
         copy.wait()
@@ -404,26 +412,31 @@
     def step(b, first):
         kv = kv_s.at[lax.rem(b, 2), lax.div(b, 2)] if not first else kv_s.at[0, 0]
         vt[...] = kv[:, KV * HD :].astype(F32).T.astype(BF)
+        ats = [slice(g * HD, (g + 1) * HD) for g in range(KV)]
+        scores = []
         for g in range(KV):
-            at = slice(g * HD, (g + 1) * HD)
             qg = jnp.concatenate([qt[(g * G + j) * HD : (g * G + j + 1) * HD, :] for j in range(G)], 1)
-            s = dot(kv[:, at], qg)
+            s = dot(kv[:, ats[g]], qg)
             if first:
                 key = lax.broadcasted_iota(jnp.int32, (T, W), 0)
                 query = lax.broadcasted_iota(jnp.int32, (T, W), 1) % T
                 s = jnp.where(key <= query, s, -1e30)
-                m = jnp.max(s, 0, keepdims=True)
-                p = jnp.exp(s - m)
-                l_s[g : g + 1, :] = jnp.sum(p, 0, keepdims=True)
-                acc[at, :] = dot(vt[at, :], p.astype(BF))
-            else:
+            scores.append(s)
+        probs, scales = [], []
+        for g in range(KV):
+            top = jnp.max(scores[g], 0, keepdims=True)
+            if not first:
                 old = m_s[g : g + 1, :]
-                m = jnp.maximum(old, jnp.max(s, 0, keepdims=True))
-                p = jnp.exp(s - m)
-                scale = jnp.exp(old - m)
-                l_s[g : g + 1, :] = l_s[g : g + 1, :] * scale + jnp.sum(p, 0, keepdims=True)
-                acc[at, :] = acc[at, :] * scale + dot(vt[at, :], p.astype(BF))
-            m_s[g : g + 1, :] = m
+                top = jnp.maximum(old, top)
+                scales.append(jnp.exp(old - top))
+            p = jnp.exp(scores[g] - top)
+            total = jnp.sum(p, 0, keepdims=True)
+            l_s[g : g + 1, :] = total if first else l_s[g : g + 1, :] * scales[g] + total
+            m_s[g : g + 1, :] = top
+            probs.append(p.astype(BF))
+        for g in range(KV):
+            out = dot(vt[ats[g], :], probs[g])
+            acc[ats[g], :] = out if first else acc[ats[g], :] * scales[g] + out
 
     step(0, True)
 
@@ -438,17 +451,23 @@
         for j in range(G):
             h = g * G + j
             o_ref[:, h * HD : (h + 1) * HD] = og[:, j * T : (j + 1) * T].T.astype(BF)
-
-
-def attend(rng, q, kv_all):
+    spread.wait()
+    op_ref[...] = dot(o_ref[...], e_s[...]).astype(BF)
+
+
+def attend(rng, q, kv_all, e):
     blocks, other = kv_all
     T, zs = q.shape[0], len(blocks)
     W = G * T
     return pl.pallas_call(
         functools.partial(attend_kernel, zs),
-        out_shape=(jax.ShapeDtypeStruct((T, D), BF), jax.ShapeDtypeStruct((KV, W), F32)),
-        in_specs=[SMEM, VMEM] + [ANY] * (zs + 1),
-        out_specs=[VMEM] * 2,
+        out_shape=(
+            jax.ShapeDtypeStruct((T, D), BF),
+            jax.ShapeDtypeStruct((T, PADDED), BF),
+            jax.ShapeDtypeStruct((KV, W), F32),
+        ),
+        in_specs=[SMEM, VMEM] + [ANY] * (zs + 2),
+        out_specs=[VMEM] * 3,
         scratch_shapes=[
             pltpu.VMEM((2, zs, T, KVW), BF),
             pltpu.VMEM((D, T), BF),
@@ -456,15 +475,20 @@
             pltpu.VMEM((KV, W), F32),
             pltpu.VMEM((KV, W), F32),
             pltpu.VMEM((KV * HD, W), F32),
-            pltpu.SemaphoreType.DMA((zs + 1,)),
+            pltpu.VMEM((D, PADDED), BF),
+            pltpu.SemaphoreType.DMA((zs + 2,)),
         ],
         compiler_params=BIG,
+        cost_estimate=cost(24),
         name="attend",
-    )(rng, q, *blocks, other)
+    )(rng, q, *blocks, other, e)
 
 
 def attend_back_kernel(zs, rng, q_ref, o_ref, do_ref, lse_ref, cos_ref, sin_ref, *refs):
-    blocks, (other, dq_ref, dkv_ref, kv_s, qt, dot_, qn, don, kt, dl, dqa, sems) = refs[:zs], refs[zs:]
+    blocks, (other, dq_ref, own_ref, send_ref, kv_s, qt, dot_, qn, don, kt, dl, dqa, sems, dkv_ref, out_sems) = (
+        refs[:zs],
+        refs[zs:],
+    )
     T = q_ref.shape[0]
     W = G * T
     copies = load_kv(blocks, other, kv_s, sems)
@@ -531,6 +555,17 @@
         grad = jnp.concatenate(parts, 0).T
         turned = grad * cos - half_of(grad * sin)
         dq_ref[:, pair * LANES : (pair + 1) * LANES] = turned.astype(BF)
+    kv_s[0, 0] = dq_ref[:, :KVW]
+    kv_s[0, 1, :, : PADDED - KVW] = dq_ref[:, KVW:]
+    copies = [
+        pltpu.make_async_copy(dkv_ref.at[0], own_ref, out_sems.at[0]),
+        pltpu.make_async_copy(dkv_ref.at[1], send_ref.at[pl.ds(0, zs)], out_sems.at[1]),
+        pltpu.make_async_copy(kv_s.at[0, pl.ds(0, 2)], send_ref.at[pl.ds(zs, 2)], out_sems.at[2]),
+    ]
+    for copy in copies:
+        copy.start()
+    for copy in copies:
+        copy.wait()
 
 
 def attend_back(rng, q, o, do, lse, cos, sin, kv_all):
@@ -539,9 +574,13 @@
     W = G * T
     return pl.pallas_call(
         functools.partial(attend_back_kernel, zs),
-        out_shape=(jax.ShapeDtypeStruct((T, PADDED), BF), jax.ShapeDtypeStruct((2, zs, T, KVW), BF)),
+        out_shape=(
+            jax.ShapeDtypeStruct((T, PADDED), BF),
+            jax.ShapeDtypeStruct((zs, T, KVW), BF),
+            jax.ShapeDtypeStruct((zs + 2, T, KVW), BF),
+        ),
         in_specs=[SMEM] + [VMEM] * 6 + [ANY] * (zs + 1),
-        out_specs=[VMEM] * 2,
+        out_specs=[VMEM, ANY, ANY],
         scratch_shapes=[
             pltpu.VMEM((2, zs, T, KVW), BF),
             pltpu.VMEM((D, T), BF),
@@ -552,8 +591,11 @@
             pltpu.VMEM((KV, W), F32),
             pltpu.VMEM((KV * HD, W), F32),
             pltpu.SemaphoreType.DMA((zs + 1,)),
+            pltpu.VMEM((2, zs, T, KVW), BF),
+            pltpu.SemaphoreType.DMA((3,)),
         ],
         compiler_params=BIG,
+        cost_estimate=cost(24),
         name="attend_back",
     )(rng, q, o, do, lse, cos, sin, *blocks, other)
 
@@ -563,10 +605,15 @@
     return blocks, swap(jnp.stack(blocks), "core")
 
 
-def collect_kv(grads):
-    mine = grads[0].astype(F32) + swap(grads[1], "core").astype(F32)
-    mine = mine.astype(BF)
-    return [mine[0]] + [move_z(mine[d], -d) for d in range(1, lax.axis_size("z"))]
+def collect_kv(grads, got, before=()):
+    count = lax.axis_size("z")
+    moving = plus(grads[count - 1], got[count - 1])
+    for d in range(count - 2, -1, -1):
+        moved = move_z(after(moving, *before[d]) if d < len(before) else moving, -1)
+        own = plus(grads[d], got[d])
+        if d == 0:
+            return [own, moved]
+        moving = plus(own, moved)
 
 
 def qkv_kernel(base, x_ref, gain_ref, cos_ref, sin_ref, w_hbm, na_ref, q_ref, kv_ref, w_s, sem):
@@ -608,202 +655,276 @@
         out_specs=[VMEM] * 3,
         scratch_shapes=[pltpu.VMEM((shards, QKV_BLOCKS * rows, LANES), BF), pltpu.SemaphoreType.DMA],
         compiler_params=BIG,
+        cost_estimate=cost(6),
         name="qkv_forward",
     )(x, gain, cos, sin, weights)
 
 
-def weight_copies(w_hbm, w_s, sems, rows, ff_rows, first):
-    steps = FF // CHUNK
-    per = CHUNK // ff_rows
-    blocks = CHUNK // LANES * rows
-    gate = first + OUT_BLOCKS * rows
-    up = gate + FF_BLOCKS * rows
-    down = up + FF_BLOCKS * rows
-    out = [pltpu.make_async_copy(w_hbm.at[:, pl.ds(first, OUT_BLOCKS * rows), :], w_s.at[:, pl.ds(0, OUT_BLOCKS * rows), :], sems.at[3 * steps])]
-    chunks = []
-    for j in range(steps):
-        parts = []
-        for at in (gate + j * blocks, up + j * blocks):
-            parts.append((pl.ds(0, w_hbm.shape[0]), pl.ds(at, blocks), pl.ds(at - first, blocks)))
-        parts.append((pl.ds(j * per, per), pl.ds(down, OUT_BLOCKS * ff_rows), pl.ds(down - first, OUT_BLOCKS * ff_rows)))
-        chunks.append(
-            [
-                pltpu.make_async_copy(w_hbm.at[who, src, :], w_s.at[who, dst, :], sems.at[3 * j + i])
-                for i, (who, src, dst) in enumerate(parts)
-            ]
-        )
-    return out, chunks
-
-
-def down_of(w_s, j, ff_rows, at):
-    per = CHUNK // ff_rows
-    parts = [
-        w_s[j * per : (j + 1) * per, at + i * ff_rows : at + (i + 1) * ff_rows, :].reshape(CHUNK, LANES)
-        for i in range(OUT_BLOCKS)
-    ]
-    return jnp.concatenate(parts, 1)
-
-
-def ffn_kernel(first, o_ref, x_ref, na_ref, gain_ref, e_ref, w_hbm, acts_ref, m_ref, g_ref, u_ref, y_ref, w_s, acc, sems):
-    step = pl.program_id(0)
-    rows = PADDED // w_s.shape[0]
-    ff_rows = FF // w_s.shape[0]
-    out, chunks = weight_copies(w_hbm, w_s, sems, rows, ff_rows, first)
+def weight_copies(w_hbm, w_s, sems, first):
+    shards = w_hbm.shape[0]
+    rows, ff_rows = PADDED // shards, FF // shards
     gate = OUT_BLOCKS * rows
     up = gate + FF_BLOCKS * rows
     down = up + FF_BLOCKS * rows
-    blocks = CHUNK // LANES
-
-    @pl.when(step == 0)
-    def _():
-        out[0].start()
-        for chunk in chunks:
-            for copy in chunk:
-                copy.start()
-        padded = dot(o_ref[...], e_ref[...]).astype(BF)
-        acts_ref[:, FF : FF + PADDED] = padded
-        acts_ref[:, FF + 2 * PADDED :] = na_ref[...]
-        out[0].wait()
-        mixed = x_ref[...].astype(F32) + dot(padded, columns(w_s, 0, OUT_BLOCKS, rows))
-        m_ref[...] = mixed
-        acts_ref[:, FF + PADDED : FF + 2 * PADDED] = (mixed * rms(mixed) * gain_ref[...]).astype(BF)
-        acc[...] = mixed
-
-    for j in range(FF // CHUNK):
-
-        @pl.when(step == j)
-        def _():
-            for copy in chunks[j]:
-                copy.wait()
-            normed = acts_ref[:, FF + PADDED : FF + 2 * PADDED]
-            g = dot(normed, columns(w_s, gate + j * blocks * rows, blocks, rows))
-            u = dot(normed, columns(w_s, up + j * blocks * rows, blocks, rows))
-            hidden = (g * jax.nn.sigmoid(g) * u).astype(BF)
-            g_ref[...] = g
-            u_ref[...] = u
-            acts_ref[:, j * CHUNK : (j + 1) * CHUNK] = hidden
-            acc[...] += dot(hidden, down_of(w_s, j, ff_rows, down))
-
-    @pl.when(step == FF // CHUNK - 1)
-    def _():
-        y_ref[...] = acc[...].astype(BF)
-
-
-def ffn_forward(o, x, na, gain, e, weights, first):
+    step = WIDE // LANES * rows
+    everyone = pl.ds(0, shards)
+    places = [(everyone, 0, gate)]
+    places += [(everyone, at + i * step, step) for i in range(FF // WIDE) for at in (gate, up)]
+    places += [(pl.ds(h * shards // 2, shards // 2), down, OUT_BLOCKS * ff_rows) for h in range(2)]
+    copies = []
+    for i, (who, at, height) in enumerate(places):
+        source, target = w_hbm.at[who, pl.ds(first + at, height), :], w_s.at[who, pl.ds(at, height), :]
+        copies.append(pltpu.make_async_copy(source, target, sems.at[i]))
+    pairs = [copies[1 + 2 * i : 3 + 2 * i] for i in range(FF // WIDE)]
+    return copies[0], pairs, copies[-2:]
+
+
+def gate_up(w_s, i):
+    rows = PADDED // w_s.shape[0]
+    at = OUT_BLOCKS * rows + i * (WIDE // LANES) * rows
+    return [columns(w_s, at + j * FF_BLOCKS * rows, WIDE // LANES, rows) for j in range(2)]
+
+
+def down_half(w_s, h):
+    shards = w_s.shape[0]
+    rows, ff_rows = PADDED // shards, FF // shards
+    at = (OUT_BLOCKS + 2 * FF_BLOCKS) * rows
+    who = slice(h * shards // 2, (h + 1) * shards // 2)
+    parts = [w_s[who, at + i * ff_rows : at + (i + 1) * ff_rows, :].reshape(-1, LANES) for i in range(OUT_BLOCKS)]
+    return jnp.concatenate(parts, 1)
+
+
+def ffn_up(x, op, na, gain, w_s, acts, loads):
+    out, pairs, downs = loads
+    rows = PADDED // w_s.shape[0]
+    acts[:, FF : FF + PADDED] = op
+    acts[:, FF + 2 * PADDED :] = na
+    out.wait()
+    mixed = x.astype(F32) + dot(op, columns(w_s, 0, OUT_BLOCKS, rows))
+    normed = (mixed * rms(mixed) * gain).astype(BF)
+    acts[:, FF + PADDED : FF + 2 * PADDED] = normed
+    gates = []
+    for i in range(FF // WIDE):
+        for copy in pairs[i]:
+            copy.wait()
+        gate, up = gate_up(w_s, i)
+        g, u = dot(normed, gate), dot(normed, up)
+        acts[:, i * WIDE : (i + 1) * WIDE] = (g * jax.nn.sigmoid(g) * u).astype(BF)
+        gates.append((g.astype(BF), u.astype(BF)))
+    return mixed, gates
+
+
+def ffn_down(mixed, w_s, acts, downs):
+    total = mixed
+    for h in range(2):
+        downs[h].wait()
+        total = total + dot(acts[:, h * FF // 2 : (h + 1) * FF // 2], down_half(w_s, h))
+    return total.astype(BF)
+
+
+def ffn_kernel(first, op_ref, x_ref, na_ref, gain_ref, w_hbm, acts_hbm, m_ref, gu_hbm, y_ref, w_s, acts, gu, sems, outs):
+    loads = weight_copies(w_hbm, w_s, sems, first)
+    for copy in [loads[0]] + sum(loads[1], []) + loads[2]:
+        copy.start()
+    mixed, gates = ffn_up(x_ref[...], op_ref[...], na_ref[...], gain_ref[...], w_s, acts, loads)
+    m_ref[...] = mixed
+    for i, pair in enumerate(gates):
+        for j in range(2):
+            gu[j, :, i * WIDE : (i + 1) * WIDE] = pair[j]
+    sends = [pltpu.make_async_copy(acts, acts_hbm, outs.at[0]), pltpu.make_async_copy(gu, gu_hbm, outs.at[1])]
+    for copy in sends:
+        copy.start()
+    y_ref[...] = ffn_down(mixed, w_s, acts, loads[2])
+    for copy in sends:
+        copy.wait()
+
+
+def ffn_forward(op, x, na, gain, weights, first):
     count = x.shape[0]
     shards = weights.shape[0]
-    rows = PADDED // shards
-    later = (OUT_BLOCKS + 2 * FF_BLOCKS) * rows + OUT_BLOCKS * (FF // shards)
-    whole = lambda shape: pl.BlockSpec(shape, lambda j: (0, 0))
-    chunk = pl.BlockSpec((count, CHUNK), lambda j: (0, j))
-    wide = jax.ShapeDtypeStruct((count, FF), F32)
+    later = (OUT_BLOCKS + 2 * FF_BLOCKS) * (PADDED // shards) + OUT_BLOCKS * (FF // shards)
     return pl.pallas_call(
         functools.partial(ffn_kernel, first),
-        grid=(FF // CHUNK,),
         out_shape=(
             jax.ShapeDtypeStruct((count, ACTS), BF),
             jax.ShapeDtypeStruct((count, PADDED), F32),
-            wide,
-            wide,
+            jax.ShapeDtypeStruct((2, count, FF), BF),
             jax.ShapeDtypeStruct((count, PADDED), BF),
         ),
-        in_specs=[whole((count, D))] + [whole((count, PADDED))] * 2 + [whole((1, PADDED)), whole((D, PADDED)), ANY],
-        out_specs=[whole((count, ACTS)), whole((count, PADDED)), chunk, chunk, whole((count, PADDED))],
+        in_specs=[VMEM] * 4 + [ANY],
+        out_specs=[ANY, VMEM, ANY, VMEM],
         scratch_shapes=[
             pltpu.VMEM((shards, later, LANES), BF),
-            pltpu.VMEM((count, PADDED), F32),
-            pltpu.SemaphoreType.DMA((3 * (FF // CHUNK) + 1,)),
+            pltpu.VMEM((count, ACTS), BF),
+            pltpu.VMEM((2, count, FF), BF),
+            pltpu.SemaphoreType.DMA((3 + 2 * (FF // WIDE),)),
+            pltpu.SemaphoreType.DMA((2,)),
         ],
         compiler_params=BIG,
+        cost_estimate=cost(9),
         name="ffn_forward",
-    )(o, x, na, gain, e, weights)
-
-
-def ffn_back_kernel(first, dy_ref, g_ref, u_ref, m_ref, gain_ref, e_ref, w_hbm, back_ref, dm_ref, do_ref, dgain_ref, w_s, acc, sems):
-    step = pl.program_id(0)
+    )(op, x, na, gain, weights)
+
+
+def ffn_back_body(dy, mixed, gain, gates, e_s, w_s, back, loads, spread):
+    out, pairs, downs = loads
     rows = PADDED // w_s.shape[0]
-    ff_rows = FF // w_s.shape[0]
-    out, chunks = weight_copies(w_hbm, w_s, sems, rows, ff_rows, first)
-    gate = OUT_BLOCKS * rows
-    up = gate + FF_BLOCKS * rows
-    down = up + FF_BLOCKS * rows
-    blocks = CHUNK // LANES
-
-    @pl.when(step == 0)
-    def _():
-        for chunk in chunks:
-            for copy in (chunk[2], chunk[0], chunk[1]):
-                copy.start()
-        out[0].start()
-        acc[...] = jnp.zeros_like(acc)
-
-    for j in range(FF // CHUNK):
-
-        @pl.when(step == j)
-        def _():
-            chunks[j][2].wait()
-            d_hidden = dot_nt(dy_ref[...], down_of(w_s, j, ff_rows, down))
-            g = g_ref[...]
-            sig = jax.nn.sigmoid(g)
-            dg = (d_hidden * u_ref[...] * sig * (1.0 + g * (1.0 - sig))).astype(BF)
-            du = (d_hidden * g * sig).astype(BF)
-            back_ref[:, j * CHUNK : (j + 1) * CHUNK] = dg
-            back_ref[:, FF + j * CHUNK : FF + (j + 1) * CHUNK] = du
-            chunks[j][0].wait()
-            chunks[j][1].wait()
-            acc[...] += dot_nt(dg, columns(w_s, gate + j * blocks * rows, blocks, rows)) + dot_nt(
-                du, columns(w_s, up + j * blocks * rows, blocks, rows)
-            )
-
-    @pl.when(step == FF // CHUNK - 1)
-    def _():
-        back, dgain = norm_back(acc[...], m_ref[...], gain_ref[...])
-        dgain_ref[...] = dgain
-        d_mixed = dy_ref[...].astype(F32) + back
-        dm_ref[...] = d_mixed
-        low = d_mixed.astype(BF)
-        back_ref[:, 2 * FF : 2 * FF + PADDED] = low
-        back_ref[:, 2 * FF + PADDED :] = dy_ref[...]
-        out[0].wait()
-        d_padded = dot_nt(low, columns(w_s, 0, OUT_BLOCKS, rows)).astype(BF)
-        do_ref[...] = dot_nt(d_padded, e_ref[...]).astype(BF)
-
-
-def ffn_backward(dy, g, u, mixed, gain, e, weights, first):
-    count = dy.shape[0]
+    back[:, 2 * FF + PADDED :] = dy
+    for h in range(2):
+        downs[h].wait()
+        at = h * FF // 2
+        d_hidden = dot_nt(dy, down_half(w_s, h))
+        g, u = (part.astype(F32) for part in gates(h))
+        sig = jax.nn.sigmoid(g)
+        back[:, at : at + FF // 2] = (d_hidden * u * sig * (1.0 + g * (1.0 - sig))).astype(BF)
+        back[:, FF + at : FF + at + FF // 2] = (d_hidden * g * sig).astype(BF)
+    grad = None
+    for i in range(FF // WIDE):
+        for copy in pairs[i]:
+            copy.wait()
+        gate, up = gate_up(w_s, i)
+        part = dot_nt(back[:, i * WIDE : (i + 1) * WIDE], gate) + dot_nt(back[:, FF + i * WIDE : FF + (i + 1) * WIDE], up)
+        grad = part if grad is None else grad + part
+    norm, dgain = norm_back(grad, mixed, gain)
+    d_mixed = dy.astype(F32) + norm
+    low = d_mixed.astype(BF)
+    back[:, 2 * FF : 2 * FF + PADDED] = low
+    out.wait()
+    d_padded = dot_nt(low, columns(w_s, 0, OUT_BLOCKS, rows)).astype(BF)
+    spread.wait()
+    return d_mixed, dgain, dot_nt(d_padded, e_s[...]).astype(BF)
+
+
+class Loaded:
+    def wait(self):
+        pass
+
+
+def turn_acts(core, acts, own_ref, send_ref):
+    at, to = 0, 0
+    for width in (FF, PADDED, PADDED, PADDED):
+        turned = acts[:, at : at + width].astype(F32).T.astype(BF)
+        own, send = own_rows(turned, core, width // 16)
+        own_ref[to : to + width // 2, :] = own
+        send_ref[to : to + width // 2, :] = send
+        at, to = at + width, to + width // 2
+
+
+def ffn_both_kernel(first, place, op_ref, x_ref, na_ref, gain_ref, dy_ref, e_hbm, w_hbm, *refs):
+    y_ref, own_ref, send_ref, back_hbm, dm_ref, do_ref, dgain_ref, w_s, acts, gu, back, e_s, sems, others = refs
+    loads = weight_copies(w_hbm, w_s, sems, first)
+    spread = pltpu.make_async_copy(e_hbm, e_s, others.at[0])
+    for copy in [loads[0]] + sum(loads[1], []) + loads[2] + [spread]:
+        copy.start()
+    mixed, gates = ffn_up(x_ref[...], op_ref[...], na_ref[...], gain_ref[...], w_s, acts, loads)
+    for i, pair in enumerate(gates):
+        for j in range(2):
+            gu[j, :, i * WIDE : (i + 1) * WIDE] = pair[j]
+    y_ref[...] = ffn_down(mixed, w_s, acts, loads[2])
+    done = Loaded()
+    loads = (done, [[done, done]] * (FF // WIDE), [done, done])
+    halves = lambda h: [gu[j, :, h * FF // 2 : (h + 1) * FF // 2] for j in range(2)]
+    dm_ref[...], dgain_ref[...], do_ref[...] = ffn_back_body(
+        dy_ref[...], mixed, gain_ref[...], halves, e_s, w_s, back, loads, spread
+    )
+    send = pltpu.make_async_copy(back, back_hbm, others.at[1])
+    send.start()
+    turn_acts(place[0], acts, own_ref, send_ref)
+    send.wait()
+
+
+def ffn_both(place, op, x, na, gain, dy, e, weights, first):
+    count = x.shape[0]
     shards = weights.shape[0]
-    rows = PADDED // shards
-    later = (OUT_BLOCKS + 2 * FF_BLOCKS) * rows + OUT_BLOCKS * (FF // shards)
-    whole = lambda shape: pl.BlockSpec(shape, lambda j: (0, 0))
-    chunk = pl.BlockSpec((count, CHUNK), lambda j: (0, j))
-    full = whole((count, PADDED))
+    later = (OUT_BLOCKS + 2 * FF_BLOCKS) * (PADDED // shards) + OUT_BLOCKS * (FF // shards)
+    turned = jax.ShapeDtypeStruct((ACTS // 2, count), BF)
     return pl.pallas_call(
-        functools.partial(ffn_back_kernel, first),
-        grid=(FF // CHUNK,),
+        functools.partial(ffn_both_kernel, first),
         out_shape=(
+            jax.ShapeDtypeStruct((count, PADDED), BF),
+            turned,
+            turned,
             jax.ShapeDtypeStruct((count, BACK), BF),
             jax.ShapeDtypeStruct((count, PADDED), F32),
             jax.ShapeDtypeStruct((count, D), BF),
             jax.ShapeDtypeStruct((1, PADDED), F32),
         ),
-        in_specs=[full, chunk, chunk, full, whole((1, PADDED)), whole((D, PADDED)), ANY],
-        out_specs=[whole((count, BACK)), full, whole((count, D)), whole((1, PADDED))],
+        in_specs=[SMEM] + [VMEM] * 5 + [ANY] * 2,
+        out_specs=[VMEM] * 3 + [ANY] + [VMEM] * 3,
         scratch_shapes=[
             pltpu.VMEM((shards, later, LANES), BF),
-            pltpu.VMEM((count, PADDED), F32),
-            pltpu.SemaphoreType.DMA((3 * (FF // CHUNK) + 1,)),
+            pltpu.VMEM((count, ACTS), BF),
+            pltpu.VMEM((2, count, FF), BF),
+            pltpu.VMEM((count, BACK), BF),
+            pltpu.VMEM((D, PADDED), BF),
+            pltpu.SemaphoreType.DMA((3 + 2 * (FF // WIDE),)),
+            pltpu.SemaphoreType.DMA((2,)),
         ],
         compiler_params=BIG,
-        name="ffn_backward",
-    )(dy, g, u, mixed, gain, e, weights)
-
-
-def qkv_back_kernel(base, zs, dq_ref, cos_ref, sin_ref, x_ref, gain_ref, dm_ref, *refs):
-    shares, (w_hbm, dkv_ref, dx_ref, dgain_ref, w_s, sem) = refs[:zs], refs[zs:]
+        cost_estimate=cost(20),
+        name="ffn_both",
+    )(place, op, x, na, gain, dy, e, weights)
+
+
+def both_back_kernel(base, first, zs, dq_ref, cos_ref, sin_ref, x_ref, gain_ref, dm_ref, *refs):
+    shares, refs = refs[:zs], refs[zs:]
+    dgf_ref, m_ref, gain_f_ref, gu_hbm, e_hbm, wa_hbm, wf_hbm = refs[:7]
+    dkv_ref, low_ref, back_hbm, dm_out, do_ref, dgain_ref, wa_s, wf_s, back, gu, e_s, sem, sems, others = refs[7:]
+    copy = pltpu.make_async_copy(wa_hbm.at[:, pl.ds(base, wa_s.shape[1]), :], wa_s, sem)
+    loads = weight_copies(wf_hbm, wf_s, sems, first)
+    load = pltpu.make_async_copy(gu_hbm, gu, others.at[0])
+    spread = pltpu.make_async_copy(e_hbm, e_s, others.at[1])
+    for each in [copy] + loads[2] + [load] + sum(loads[1], []) + [loads[0], spread]:
+        each.start()
+    dx = qkv_back_body(dq_ref, shares, cos_ref[...], sin_ref[...], x_ref, gain_ref, dm_ref, dgf_ref, copy, wa_s, dkv_ref)
+    low = dx.astype(BF)
+    low_ref[...] = low
+    load.wait()
+    halves = lambda h: [gu[j, :, h * FF // 2 : (h + 1) * FF // 2] for j in range(2)]
+    dm_out[...], dgain_ref[...], do_ref[...] = ffn_back_body(
+        low, m_ref[...], gain_f_ref[...], halves, e_s, wf_s, back, loads, spread
+    )
+    send = pltpu.make_async_copy(back, back_hbm, others.at[2])
+    send.start()
+    send.wait()
+
+
+def both_back(dq, shares, cos, sin, x, gain, dm, dgf, w_a, base, mixed, gain_f, gu, e, w_f, first):
+    count = x.shape[0]
+    shards = w_a.shape[0]
+    rows = PADDED // shards
+    later = (OUT_BLOCKS + 2 * FF_BLOCKS) * rows + OUT_BLOCKS * (FF // shards)
+    return pl.pallas_call(
+        functools.partial(both_back_kernel, base, first, len(shares)),
+        out_shape=(
+            jax.ShapeDtypeStruct((count + EXTRA, KVW), BF),
+            jax.ShapeDtypeStruct((count, PADDED), BF),
+            jax.ShapeDtypeStruct((count, BACK), BF),
+            jax.ShapeDtypeStruct((count, PADDED), F32),
+            jax.ShapeDtypeStruct((count, D), BF),
+            jax.ShapeDtypeStruct((1, PADDED), F32),
+        ),
+        in_specs=[VMEM] * (9 + len(shares)) + [ANY] * 4,
+        out_specs=[VMEM, VMEM, ANY] + [VMEM] * 3,
+        scratch_shapes=[
+            pltpu.VMEM((shards, QKV_BLOCKS * rows, LANES), BF),
+            pltpu.VMEM((shards, later, LANES), BF),
+            pltpu.VMEM((count, BACK), BF),
+            pltpu.VMEM((2, count, FF), BF),
+            pltpu.VMEM((D, PADDED), BF),
+            pltpu.SemaphoreType.DMA,
+            pltpu.SemaphoreType.DMA((3 + 2 * (FF // WIDE),)),
+            pltpu.SemaphoreType.DMA((3,)),
+        ],
+        compiler_params=BIG,
+        cost_estimate=cost(18),
+        name="both_back",
+    )(dq, cos, sin, x, gain, dm, *shares, dgf, mixed, gain_f, gu, e, w_a, w_f)
+
+
+def qkv_back_body(dq_ref, shares, cos, sin, x_ref, gain_ref, dm_ref, dgf_ref, copy, w_s, dkv_ref):
+    count = x_ref.shape[0]
     rows = w_s.shape[1] // QKV_BLOCKS
-    copy = pltpu.make_async_copy(w_hbm.at[:, pl.ds(base, w_s.shape[1]), :], w_s, sem)
-    copy.start()
-    cos, sin = cos_ref[...], sin_ref[...]
     for j in range(KVW // LANES):
         at = slice(j * LANES, (j + 1) * LANES)
         grad = shares[0][:, at].astype(F32)
@@ -813,48 +934,80 @@
         if j == 2:
             lane = lax.broadcasted_iota(jnp.int32, grad.shape, 1)
             turned = jnp.where(lane < HD, turned, grad)
-        dkv_ref[:, at] = turned.astype(BF)
+        dkv_ref[:count, at] = turned.astype(BF)
     copy.wait()
     kv_blocks = KVW // LANES
-    d_normed = dot_nt(dkv_ref[...], columns(w_s, 0, kv_blocks, rows))
+    d_normed = dot_nt(dkv_ref[:count, :], columns(w_s, 0, kv_blocks, rows))
     d_normed = d_normed + dot_nt(dq_ref[...], columns(w_s, kv_blocks * rows, QKV_BLOCKS - kv_blocks, rows))
     back, dgain = norm_back(d_normed, x_ref[...].astype(F32), gain_ref[...])
-    dgain_ref[...] = dgain
-    dx_ref[...] = dm_ref[...] + back
-
-
-def qkv_backward(dq, shares, cos, sin, x, gain, dm, weights, base):
+    dkv_ref[count:, :] = gain_rows(dgain, dgf_ref[...])
+    return dm_ref[...] + back
+
+
+def qkv_back_kernel(base, zs, dq_ref, cos_ref, sin_ref, x_ref, gain_ref, dm_ref, *refs):
+    shares, (dgf_ref, w_hbm, dkv_ref, dx_ref, low_ref, w_s, sem) = refs[:zs], refs[zs:]
+    copy = pltpu.make_async_copy(w_hbm.at[:, pl.ds(base, w_s.shape[1]), :], w_s, sem)
+    copy.start()
+    dx = qkv_back_body(dq_ref, shares, cos_ref[...], sin_ref[...], x_ref, gain_ref, dm_ref, dgf_ref, copy, w_s, dkv_ref)
+    dx_ref[...] = dx
+    low_ref[...] = dx.astype(BF)
+
+
+def gain_rows(first, second):
+    half = PADDED // 2
+    rows = [first[:, :half], first[:, half:], second[:, :half], second[:, half:]]
+    rows = jnp.concatenate(rows + [jnp.zeros((EXTRA - 4, half), F32)], 0)
+    return jnp.concatenate([rows, jnp.zeros((EXTRA, KVW - half), F32)], 1).astype(BF)
+
+
+def gain_columns(own, other):
+    total = own.astype(F32) + other.astype(F32)
+    half = PADDED // 2
+    rows = [jnp.concatenate([total[2 * i : 2 * i + 1, :half], total[2 * i + 1 : 2 * i + 2, :half]], 1) for i in range(2)]
+    return jnp.concatenate(rows + [jnp.zeros((LANES - 2, PADDED), F32)], 0).T.astype(BF)
+
+
+def qkv_backward(dq, shares, cos, sin, x, gain, dm, dgf, weights, base):
     count = x.shape[0]
     shards = weights.shape[0]
     rows = PADDED // shards
     return pl.pallas_call(
         functools.partial(qkv_back_kernel, base, len(shares)),
         out_shape=(
-            jax.ShapeDtypeStruct((count, KVW), BF),
+            jax.ShapeDtypeStruct((count + EXTRA, KVW), BF),
             jax.ShapeDtypeStruct((count, PADDED), F32),
-            jax.ShapeDtypeStruct((1, PADDED), F32),
+            jax.ShapeDtypeStruct((count, PADDED), BF),
         ),
-        in_specs=[VMEM] * (6 + len(shares)) + [ANY],
+        in_specs=[VMEM] * (7 + len(shares)) + [ANY],
         out_specs=[VMEM] * 3,
         scratch_shapes=[pltpu.VMEM((shards, QKV_BLOCKS * rows, LANES), BF), pltpu.SemaphoreType.DMA],
         compiler_params=BIG,
+        cost_estimate=cost(6),
         name="qkv_backward",
-    )(dq, cos, sin, x, gain, dm, *shares, weights)
-
-
-def both_t(own, other, at, width):
-    parts = [ref[:, at : at + width].astype(F32).T.astype(BF) for ref in (own, other)]
-    return jnp.concatenate(parts, 1)
+    )(dq, cos, sin, x, gain, dm, *shares, dgf, weights)
 
 
 def own_rows(turned, core, rows):
     split = turned.reshape(-1, 2, rows, turned.shape[-1])
-    return jnp.where(core == 0, split[:, 0], split[:, 1]).reshape(-1, turned.shape[-1])
-
-
-def both(own, other, at, width):
-    where = pl.ds(pl.multiple_of(at, LANES), width)
-    return jnp.concatenate([own[:, where], other[:, where]], 0)
+    first, second = split[:, 0].reshape(-1, turned.shape[-1]), split[:, 1].reshape(-1, turned.shape[-1])
+    return jnp.where(core == 0, first, second), jnp.where(core == 0, second, first)
+
+
+def turn_kernel(place, acts_ref, own_ref, send_ref):
+    turn_acts(place[0], acts_ref, own_ref, send_ref)
+
+
+def turn(place, acts):
+    shape = jax.ShapeDtypeStruct((ACTS // 2, acts.shape[0]), BF)
+    return pl.pallas_call(
+        turn_kernel,
+        out_shape=(shape, shape),
+        in_specs=[SMEM, VMEM],
+        out_specs=[VMEM] * 2,
+        compiler_params=BIG,
+        cost_estimate=cost(4),
+        name="turn",
+    )(place, acts)
 
 
 def write_split(out, keep_ref, send_ref, at, rows, half):
@@ -865,105 +1018,248 @@
         send_ref[:, place, :] = jnp.where(half == 0, block[1], block[0])
 
 
-def grad_ffn_kernel(place, own, other, back, back_other, keep_a, send_a, keep_u, send_u, keep_o, send_o, nft, opt, hdt):
-    step = pl.program_id(0)
-    core, half, section = place[0], place[1], place[2]
-    chips = keep_a.shape[0]
+def grad_ffn_kernel(place, own_hbm, other_hbm, back_hbm, back_other_hbm, *refs):
+    outs, (left, back, *held, sems, out_sems) = refs[:8], refs[8:]
+    keep_a, send_a, keep_u, send_u = held[:2], held[2:4], held[4:6], held[6:8]
+    half, section = place[1], place[2]
+    count = back.shape[0] // 2
+    chips = keep_a[0].shape[0]
     rows, ff_rows = PADDED // (2 * chips), FF // (2 * chips)
     steps = FF // CHUNK
-
-    @pl.when(step == 0)
-    def _():
-        nft[...] = own_rows(both_t(own, other, FF + PADDED, PADDED), core, rows)
-
-    @pl.when(step == steps)
-    def _():
-        hdt[...] = own_rows(both_t(own, other, 0, FF), core, ff_rows)
-
-    @pl.when(step == 3 * steps)
-    def _():
-        opt[...] = own_rows(both_t(own, other, FF, PADDED), core, rows)
-
-    def write_a(out, height, to):
-        for i in range(out.shape[1] // LANES):
-            to[:, i * height : (i + 1) * height, :] = out[:, i * LANES : (i + 1) * LANES].reshape(chips, height, LANES)
-
-    @pl.when(step < steps)
-    def _():
-        out = dot(nft[...], both(back, back_other, step * CHUNK, CHUNK)).astype(BF)
-        pl.when(section == 1)(lambda: write_a(out, rows, keep_a))
-        pl.when(section == 0)(lambda: write_a(out, rows, send_a))
-
-    @pl.when((step >= steps) & (step < 2 * steps))
-    def _():
-        width = PADDED // steps
-        out = dot(hdt[...], both(back, back_other, 2 * FF + PADDED + (step - steps) * width, width)).astype(BF)
-        pl.when(section == 0)(lambda: write_a(out, ff_rows, keep_a))
-        pl.when(section == 1)(lambda: write_a(out, ff_rows, send_a))
-
-    @pl.when((step >= 2 * steps) & (step < 3 * steps))
-    def _():
-        out = dot(nft[...], both(back, back_other, FF + (step - 2 * steps) * CHUNK, CHUNK)).astype(BF)
-        write_split(out, keep_u, send_u, 0, rows, half)
-
-    @pl.when(step == 3 * steps)
-    def _():
-        out = dot(opt[...], both(back, back_other, 2 * FF, PADDED)).astype(BF)
-        write_split(out, keep_o, send_o, 0, rows, half)
+    hd, op, nf = (0, FF // 2), (FF // 2, PADDED // 2), ((FF + PADDED) // 2, PADDED // 2)
+    loads = []
+
+    def load(at, width, height, first):
+        group = []
+        for side, (turned, wide) in enumerate(((own_hbm, back_hbm), (other_hbm, back_other_hbm))):
+            place_l = (pl.ds(height[0], height[1]), pl.ds(side * count, count))
+            place_b = (pl.ds(side * count, count), pl.ds(at, width))
+            if first:
+                group.append(pltpu.make_async_copy(turned.at[place_l[0], :], left.at[place_l], sems.at[4 * len(loads) + 2 * side]))
+            group.append(pltpu.make_async_copy(wide.at[:, place_b[1]], back.at[place_b], sems.at[4 * len(loads) + 2 * side + 1]))
+        loads.append(group)
+        for copy in group:
+            copy.start()
+
+    load(0, FF, nf, True)
+    load(2 * FF + PADDED, PADDED, hd, True)
+    load(FF, FF, nf, False)
+    load(2 * FF, PADDED, op, True)
+
+    def ready(i):
+        for copy in loads[i]:
+            copy.wait()
+
+    def product(which, at, width):
+        return dot(left[which[0] : which[0] + which[1], :], back[:, at : at + width]).astype(BF)
+
+    def as_blocks(out, height):
+        width = out.shape[1] // LANES
+        return [out[:, i * LANES : (i + 1) * LANES].reshape(chips, height, LANES) for i in range(width)]
+
+    sent = []
+
+    def finish(*which):
+        for i in which:
+            sent.append(pltpu.make_async_copy(held[i], outs[i], out_sems.at[i]))
+            sent[-1].start()
+
+    ready(0)
+    ready(1)
+    block = CHUNK // LANES * rows
+    narrow_width = PADDED // steps
+    for j in range(steps):
+        gate = jnp.concatenate(as_blocks(product(nf, j * CHUNK, CHUNK), rows), 1)
+        down = jnp.concatenate(as_blocks(product(hd, 2 * FF + PADDED + j * narrow_width, narrow_width), ff_rows), 1)
+        at = slice(j % 2 * block, (j % 2 + 1) * block)
+        keep_a[j // 2][:, at, :] = jnp.where(section == 0, down, gate)
+        send_a[j // 2][:, at, :] = jnp.where(section == 0, gate, down)
+        if j % 2:
+            finish(j // 2, 2 + j // 2)
+    ready(2)
+    for j in range(steps):
+        h = j // (steps - 1)
+        write_split(product(nf, FF + j * CHUNK, CHUNK), keep_u[h], send_u[h], (j - h * (steps - 1)) * block, rows, half)
+        if j == steps - 2:
+            finish(4, 6)
+    ready(3)
+    write_split(product(op, 2 * FF, PADDED), keep_u[1], send_u[1], block, rows, half)
+    finish(5, 7)
+    for copy in sent:
+        copy.wait()
 
 
 def grad_ffn(place, own, other, back, back_other, shards):
-    count = own.shape[0]
+    count = own.shape[1]
     chips = shards // 2
-    rows, ff_rows = PADDED // shards, FF // shards
+    rows = PADDED // shards
     steps = FF // CHUNK
     block = CHUNK // LANES * rows
-    whole = lambda shape: pl.BlockSpec(shape, lambda j, place: (0,) * len(shape))
-    early = lambda j: jnp.clip(j, 0, steps - 1)
-    late = lambda j: jnp.clip(j - steps, 0, steps - 1)
-    last = lambda j: jnp.clip(j - 2 * steps, 0, steps - 1)
-    a_spec = lambda when: pl.BlockSpec((chips, block, LANES), lambda j, place: (0, jnp.where(place[2] == when, late(j), early(j)), 0))
-    u_spec = pl.BlockSpec((chips // 2, block, LANES), lambda j, place: (0, last(j), 0))
-    wide = lambda first, height: jax.ShapeDtypeStruct((first, height, LANES), BF)
+    shapes = [(chips, 2 * block, LANES)] * 4
+    shapes += [(chips // 2, height, LANES) for height in ((steps - 1) * block, block + OUT_BLOCKS * rows) * 2]
     return pl.pallas_call(
         grad_ffn_kernel,
-        grid_spec=pltpu.PrefetchScalarGridSpec(
-            num_scalar_prefetch=1,
-            grid=(3 * steps + 1,),
-            in_specs=[whole((count, ACTS))] * 2 + [whole((count, BACK))] * 2,
-            out_specs=[a_spec(0), a_spec(1), u_spec, u_spec] + [whole((chips // 2, OUT_BLOCKS * rows, LANES))] * 2,
-            scratch_shapes=[
-                pltpu.VMEM((PADDED // 2, 2 * count), BF),
-                pltpu.VMEM((PADDED // 2, 2 * count), BF),
-                pltpu.VMEM((FF // 2, 2 * count), BF),
-            ],
-        ),
-        out_shape=[wide(chips, steps * block)] * 2 + [wide(chips // 2, steps * block)] * 2 + [wide(chips // 2, OUT_BLOCKS * rows)] * 2,
+        out_shape=[jax.ShapeDtypeStruct(shape, BF) for shape in shapes],
+        in_specs=[SMEM] + [ANY] * 4,
+        out_specs=[ANY] * 8,
+        scratch_shapes=[pltpu.VMEM((ACTS // 2, 2 * count), BF), pltpu.VMEM((2 * count, BACK), BF)]
+        + [pltpu.VMEM(shape, BF) for shape in shapes]
+        + [pltpu.SemaphoreType.DMA((16,)), pltpu.SemaphoreType.DMA((8,))],
         compiler_params=BIG,
+        cost_estimate=cost(11),
         name="grad_ffn",
     )(place, own, other, back, back_other)
 
 
-def grad_attn_kernel(place, own, other, grad, grad_other, keep, send):
+def grad_attn_kernel(place, own, other, *refs):
+    grads, keep, send = refs[:-2], refs[-2], refs[-1]
     core, half = place[0], place[1]
-    blocks = grad.shape[1] // LANES
-    rows = keep.shape[1] // blocks
-    turned = own_rows(both_t(own, other, FF + 2 * PADDED, PADDED), core, rows)
-    out = dot(turned, jnp.concatenate([grad[...], grad_other[...]], 0)).astype(BF)
-    write_split(out, keep, send, 0, rows, half)
-
-
-def grad_attn(place, own, other, grad, grad_other, shards):
-    rows = PADDED // shards
-    shape = jax.ShapeDtypeStruct((shards // 4, grad.shape[1] // LANES * rows, LANES), BF)
+    count = own.shape[1]
+    rows = PADDED // 16
+    na = slice((FF + 2 * PADDED) // 2, ACTS // 2)
+    at = 0
+    for grad, grad_other in zip(grads[::2], grads[1::2]):
+        if len(grad_other.shape) == 3:
+            right = jnp.concatenate([grad_other[0], grad_other[1, :, : PADDED - KVW]], 1)
+        else:
+            right = grad_other[:count, :]
+        out = (dot(own[na, :], grad[:count, :]) + dot(other[na, :], right)).astype(BF)
+        write_split(out, keep, send, at, rows, half)
+        at += grad.shape[1] // LANES * rows
+        if grad.shape[0] > count:
+            gains = gain_columns(grad[count:, :], grad_other[count:, :])
+            write_split(own_rows(gains, core, rows)[0], keep, send, at, rows, half)
+            at += rows
+
+
+def grad_attn(place, own, other, *grads):
+    rows = PADDED // 16
+    blocks = sum(grad.shape[1] // LANES + (grad.shape[0] > own.shape[1]) for grad in grads[::2])
+    shape = jax.ShapeDtypeStruct((4, blocks * rows, LANES), BF)
     return pl.pallas_call(
         grad_attn_kernel,
         out_shape=(shape, shape),
-        in_specs=[SMEM] + [VMEM] * 4,
+        in_specs=[SMEM] + [VMEM] * (2 + len(grads)),
         out_specs=[VMEM] * 2,
         compiler_params=BIG,
+        cost_estimate=cost(4),
         name="grad_attn",
-    )(place, own, other, grad, grad_other)
+    )(place, own, other, *grads)
+
+
+def narrow(values, spread):
+    if values.dtype == BF:
+        return dot_nt(values, spread)
+    total, left = None, values
+    for _ in range(3):
+        part = left.astype(BF)
+        left = left - part.astype(F32)
+        out = dot_nt(part, spread)
+        total = out if total is None else total + out
+    return total
+
+
+def narrow_t(values, spread):
+    if values.dtype == BF:
+        return dot_nt(spread, values)
+    total, left = None, values
+    for _ in range(3):
+        part = left.astype(BF)
+        left = left - part.astype(F32)
+        out = dot_nt(spread, part)
+        total = out if total is None else total + out
+    return total
+
+
+def sum_block(ref, other, j, height):
+    at = slice(j * height, (j + 1) * height)
+    out = ref[at, :].astype(F32)
+    return out if other is None else out + other[at, :].astype(F32)
+
+
+def sum_matrix(ref, other, first, count, height):
+    return jnp.concatenate([sum_block(ref, other, first + j, height) for j in range(count)], 1)
+
+
+def unpack_up_kernel(place, *refs):
+    parts, (e_ref, up_ref, o_ref) = refs[:-3], refs[-3:]
+    size, rows = up_ref.shape[0], parts[0].shape[0] // (FF_BLOCKS - CHUNK // LANES)
+    cut = FF_BLOCKS - CHUNK // LANES
+    for layer in range(2):
+
+        @pl.when(place[2] == layer)
+        def _():
+            u, got_u, v, got_v = parts[4 * layer : 4 * layer + 4]
+            for j in range(FF_BLOCKS):
+                block = sum_block(u, got_u, j, rows) if j < cut else sum_block(v, got_v, j - cut, rows)
+                up_ref[:, 0, j * LANES : (j + 1) * LANES] = block[:size]
+            o_ref[:, 0, :] = narrow(sum_matrix(v, got_v, FF_BLOCKS - cut, OUT_BLOCKS, rows), e_ref[...])[:size]
+
+
+def unpack_down_kernel(place, *refs):
+    parts, (e_ref, gate_ref, down_ref) = refs[:-3], refs[-3:]
+    size, ff_rows = gate_ref.shape[0], down_ref.shape[0]
+    rows = parts[0].shape[0] // FF_BLOCKS
+    for layer in range(2):
+
+        @pl.when(place[2] == layer)
+        def _():
+            a, got_a = parts[2 * layer : 2 * layer + 2]
+            down, gate = (a, got_a) if layer == 0 else (got_a, a)
+            for j in range(FF_BLOCKS):
+                gate_ref[:, 0, j * LANES : (j + 1) * LANES] = sum_block(gate, None, j, rows)[:size]
+            down_ref[...] = narrow(sum_matrix(down, None, 0, OUT_BLOCKS, ff_rows), e_ref[...])
+
+
+def unpack_qkv_kernel(place, *refs):
+    parts, (q_ref, k_ref, v_ref, gain_ref) = refs[:-4], refs[-4:]
+    size = q_ref.shape[0]
+    kv_blocks = KVW // LANES
+    rows = parts[0].shape[0] // (OUT_BLOCKS + kv_blocks + 1)
+    for layer in range(2):
+
+        @pl.when(place[2] == layer)
+        def _():
+            s, got = parts[2 * layer : 2 * layer + 2]
+            q_ref[:, 0, :] = sum_matrix(s, got, 0, OUT_BLOCKS, rows)[:size, :D]
+            both = sum_matrix(s, got, OUT_BLOCKS, kv_blocks, rows)
+            k_ref[:, 0, :] = both[:size, : KV * HD]
+            v_ref[:, 0, :] = both[:size, KV * HD :]
+            gain_ref[...] = sum_block(s, got, OUT_BLOCKS + kv_blocks, rows).T
+
+
+def unpack(kernel, name, place, parts, shapes):
+    return pl.pallas_call(
+        kernel,
+        out_shape=[jax.ShapeDtypeStruct(shape, F32) for shape in shapes],
+        in_specs=[SMEM] + [VMEM] * len(parts),
+        out_specs=[VMEM] * len(shapes),
+        compiler_params=BIG,
+        cost_estimate=cost(4),
+        name=name,
+    )(place, *parts)
+
+
+def join_kernel(place, own0, own1, got, e_ref, out_ref):
+    section = place[2]
+    for layer, own in enumerate((own0, own1)):
+
+        @pl.when(section == layer)
+        def _():
+            out_ref[layer] = narrow_t(own[...], e_ref[...]).astype(out_ref.dtype)
+            out_ref[1 - layer] = narrow_t(got[...], e_ref[...]).astype(out_ref.dtype)
+
+
+def join(place, own0, own1, got, spread, dtype):
+    return pl.pallas_call(
+        join_kernel,
+        out_shape=jax.ShapeDtypeStruct((2, D, own0.shape[0]), dtype),
+        in_specs=[SMEM] + [VMEM] * 4,
+        out_specs=VMEM,
+        compiler_params=BIG,
+        cost_estimate=cost(4),
+        name="join",
+    )(place, own0, own1, got, spread).transpose(0, 2, 1)
 
 
 def spread_matrix(shards):
@@ -994,19 +1290,22 @@
     return lax.psum_scatter(parts, "z", scatter_dimension=0, tiled=False)
 
 
+def scatter_z_small(parts, *before_last):
+    count, me = lax.axis_size("z"), lax.axis_index("z")
+    while parts.shape[0] > 1:
+        step = parts.shape[0] // 2
+        split = parts.reshape((2, step) + parts.shape[1:])
+        bit = lax.rem(lax.div(me, step), 2)
+        keep = lax.dynamic_index_in_dim(split, bit, 0, False)
+        send = lax.dynamic_index_in_dim(split, 1 - bit, 0, False)
+        if step == 1 and before_last:
+            send = after(send, *before_last)
+        parts = plus(keep, lax.ppermute(send, "z", [(i, i ^ step) for i in range(count)]))
+    return parts[0]
+
+
 def to_owner(part, layer):
     return lax.ppermute(part, "section", [(1 - layer, layer)])
-
-
-def total_over(values):
-    count = lax.axis_size("z")
-    for axis in ("core", "dp"):
-        values = values + swap(values, axis)
-    step = 1
-    while step < count:
-        values = values + lax.ppermute(values, "z", [(i, i ^ step) for i in range(count)])
-        step *= 2
-    return values + swap(values, "section")
 
 
 def per_device_blocks(tokens, cotangent, positions, attn_gain, w_query, w_key, w_value, w_out, ffn_gain, w_gate, w_up, w_down):
@@ -1035,138 +1334,152 @@
     qkv = jnp.concatenate([w_key[0], w_value[0], w_query[0], gains, jnp.zeros((size, HD - 2), BF)], -1)
     narrow = jnp.concatenate([qkv, widen(w_out[0]), w_gate[0], w_up[0]], -1)
     shard = jnp.concatenate([to_blocks(padded(narrow)), to_blocks(widen(w_down[0]))], 0)
-    got = swap(shard, "section")
-    shard0 = jnp.where(section == 0, shard, got)
-    shard1 = jnp.where(section == 0, got, shard)
-
-    early = lax.all_gather(jnp.concatenate([shard0, shard1[:qkv_rows]], 0), plane, axis=0)
-    late = lax.all_gather(after(shard1[qkv_rows:], early), plane, axis=0)
-    base1 = shard0.shape[0]
-
-    def gains_at(base):
+    first, rest = shard[:qkv_rows], shard[qkv_rows:]
+    got_first = swap(first, "section")
+    got_rest = swap(after(rest, got_first), "section")
+
+    def layer_shard(own, got, layer):
+        return jnp.where(section == layer, own, got)
+
+    def gathered(*pieces):
+        block = pieces[0] if len(pieces) == 1 else jnp.concatenate(pieces, 0)
+        return lax.all_gather(block, plane, axis=0)
+
+    def gains_at(whole, base):
         at = base + (QKV_BLOCKS - 1) * room
-        gain = early[:, at : at + room, HD : HD + 2].reshape(-1, 2).T.astype(F32)
+        gain = whole[:, at : at + room, HD : HD + 2].reshape(-1, 2).T.astype(F32)
         return gain[:1], gain[1:]
 
-    w0 = (early, 0, early, qkv_rows) + gains_at(0)
-    w1 = (early, base1, late, 0) + gains_at(base1)
+    early = gathered(layer_shard(first, got_first, 0))
+    middle = gathered(layer_shard(rest, got_rest, 0), after(layer_shard(first, got_first, 1), early))
+    base1 = rest.shape[0]
+    w0 = (early, 0, middle, 0) + gains_at(early, 0)
     angle_cos, angle_sin = rope_tables(mine(positions))
     cos = jnp.concatenate([angle_cos[:, 0]] * 2, -1)
     sin = jnp.concatenate([angle_sin[:, 0]] * 2, -1)
 
-    def forward(x, layer):
-        w_a, at_a, w_f, at_f, gain_a, gain_f = layer
+    def attention(x, layer, *earlier):
+        w_a, at_a, gain_a = layer[0], layer[1], layer[4]
         na, q, kv = qkv_forward(x, gain_a, cos, sin, w_a, at_a)
         kv_all = spread_kv(kv)
-        o, lse = attend(block_range, q, kv_all)
-        acts, mixed, g, u, y = ffn_forward(o, x, na, gain_f, spread, w_f, at_f)
-        return y, (x, q, kv_all, o, lse, acts, mixed, g, u)
-
-    y0, saved0 = forward(widen(mine(tokens)), w0)
-    y1, saved1 = forward(y0, w1)
-
-    def backward_ffn(dy, layer, saved):
+        o, op, lse = attend(block_range, after(q, *earlier) if earlier else q, kv_all, spread)
+        return na, op, (x, q, kv_all, o, lse)
+
+    x0 = widen(mine(tokens))
+    na0, op0, saved0 = attention(x0, w0)
+    late = gathered(after(layer_shard(rest, got_rest, 1), *saved0[2][0]))
+    w1 = (middle, base1, late, 0) + gains_at(middle, base1)
+    acts0, mixed0, gu0, y0 = ffn_forward(op0, x0, na0, w0[5], w0[2], w0[3])
+    own0, send0 = turn(place, acts0)
+    na1, op1, saved1 = attention(y0, w1, own0)
+    y1, own1, send1, back1, dm1, do1, dgf1 = ffn_both(
+        place, op1, y0, na1, w1[5], widen(mine(cotangent)), spread, w1[2], w1[3]
+    )
+
+    def backward_attn(do, saved):
+        x, q, kv_all, o, lse = saved
+        return attend_back(block_range, q, o, do, lse, cos, sin, kv_all)
+
+    def backward_qkv(dq, shares, dm, dgf, layer, saved):
         w_a, at_a, w_f, at_f, gain_a, gain_f = layer
-        x, q, kv_all, o, lse, acts, mixed, g, u = saved
-        return ffn_backward(dy, g, u, mixed, gain_f, spread, w_f, at_f)
-
-    def backward_attn(do, saved):
-        x, q, kv_all, o, lse, acts, mixed, g, u = saved
-        return attend_back(block_range, q, o, do, lse, cos, sin, kv_all)
-
-    def backward_qkv(dq, shares, dm, layer, saved):
-        w_a, at_a, w_f, at_f, gain_a, gain_f = layer
-        return qkv_backward(dq, shares, cos, sin, saved[0], gain_a, dm, w_a, at_a)
+        return qkv_backward(dq, shares, cos, sin, saved[0], gain_a, dm, dgf, w_a, at_a)
 
     def halve(total):
         split = total.reshape((2, chips // 2) + total.shape[1:])
         return lax.dynamic_index_in_dim(split, half, 0, False), lax.dynamic_index_in_dim(split, 1 - half, 0, False)
 
-    acts1, acts0 = saved1[5], saved0[5]
-    other1, other0 = swap(acts1, "core"), swap(acts0, "core")
-    back1, dm1, do1, dgf1 = backward_ffn(widen(mine(cotangent)), w1, saved1)
-    back_other1 = swap(back1, "core")
-    dq1, dkv1 = backward_attn(do1, saved1)
-    shares1 = collect_kv(dkv1)
-    dq_other1 = swap(dq1, "core")
-    keep_a1, send_a1, keep_u1, send_u1, keep_o1, send_o1 = grad_ffn(place, acts1, other1, back1, back_other1, shards)
-    keep_q1, send_q1 = grad_attn(place, acts1, other1, dq1, dq_other1, shards)
-    got_a1, got_u1 = swap(send_a1, "section"), swap(send_u1, "dp")
-    got_o1, got_q1 = swap(send_o1, "dp"), swap(send_q1, "dp")
-    dkv_low1, dx1, dga1 = backward_qkv(dq1, shares1, dm1, w1, saved1)
-    dkv_other1 = swap(dkv_low1, "core")
-    dx1_low = dx1.astype(BF)
-    back0, dm0, do0, dgf0 = backward_ffn(dx1_low, w0, saved0)
-    back_other0 = swap(back0, "core")
-    keep_k1, send_k1 = grad_attn(place, acts1, other1, dkv_low1, dkv_other1, shards)
-    got_k1 = swap(send_k1, "dp")
-    do0 = after(do0, got_a1, got_u1, got_o1, got_q1)
-    keep_a1, send_a1 = halve(plus(keep_a1, got_a1))
-    got_a1 = swap(send_a1, "dp")
-    part_u1 = scatter_z(plus(keep_u1, got_u1))
-    dq0, dkv0 = backward_attn(do0, saved0)
-    shares0 = collect_kv(dkv0)
-    dq_other0 = swap(dq0, "core")
-    keep_a0, send_a0, keep_u0, send_u0, keep_o0, send_o0 = grad_ffn(place, acts0, other0, back0, back_other0, shards)
-    keep_q0, send_q0 = grad_attn(place, acts0, other0, dq0, dq_other0, shards)
-    got_a0, got_u0 = swap(send_a0, "section"), swap(send_u0, "dp")
-    got_o0, got_q0 = swap(send_o0, "dp"), swap(send_q0, "dp")
-    part_a1 = scatter_z(plus(keep_a1, got_a1))
-    oqk = lambda keeps, gots: jnp.concatenate([plus(keep, got) for keep, got in zip(keeps, gots)], 1)
-    part_s1 = scatter_z(oqk((keep_o1, keep_q1, keep_k1), (got_o1, got_q1, got_k1)))
-    dkv_low0, dx0, dga0 = backward_qkv(dq0, shares0, dm0, w0, saved0)
-    dkv_other0 = swap(dkv_low0, "core")
-    keep_k0, send_k0 = grad_attn(place, acts0, other0, dkv_low0, dkv_other0, shards)
+    def scatter(*pieces):
+        total = scatter_z(jnp.concatenate(pieces, 1) if len(pieces) > 1 else pieces[0])
+        cuts, at = [], 0
+        for piece in pieces:
+            cuts.append(total[at : at + piece.shape[1]])
+            at += piece.shape[1]
+        return cuts
+
+    def cross(keep, got):
+        keep, send = halve(plus(keep, got))
+        return keep, swap(send, "dp")
+
+    def swap_all(sends, axis):
+        return [swap(send, axis) for send in sends]
+
+    def all_after(values, *earlier):
+        return [after(value, *earlier) for value in values]
+
+    other0, other1 = swap(send0, "core"), swap(send1, "core")
+
+    def swap_all(sends, axis):
+        return [swap(send, axis) for send in sends]
+
+    def query_grads(own, got):
+        return own, got[-2:]
+
+    grads1 = grad_ffn(place, own1, other1, back1, swap(back1, "core"), shards)
+    keep_a1, send_a1, keep_u1, send_u1 = grads1[:2], grads1[2:4], grads1[4:6], grads1[6:8]
+    got_a1, got_u1 = swap_all(send_a1, "section"), swap_all(send_u1, "dp")
+    got_y = swap(jnp.where(section == 0, y1, y0), "section")
+    dq1, dkv1, away1 = backward_attn(after(do1, send_u1[0], got_y), saved1)
+    dkv1, away1 = after(dkv1, got_a1[0], got_u1[0]), after(away1, got_a1[0], got_u1[0])
+    got1 = swap(away1, "core")
+    shares1 = collect_kv(dkv1, got1)
+    dq1 = after(dq1, got_a1[1], got_u1[1])
+    keep_a1, keep_u1 = all_after(keep_a1, shares1[-1]), all_after(keep_u1, shares1[-1])
+    sum_u1 = scatter(*map(plus, keep_u1, got_u1))
+
+    (keep_b1, got_b1), (keep_c1, got_c1) = map(cross, keep_a1, got_a1)
+    dkv_low1, dx1_low, back0, dm0, do0, dgf0 = both_back(
+        dq1, shares1, cos, sin, y0, w1[4], dm1, dgf1, w1[0], w1[1], mixed0, w0[5], gu0, spread, w0[2], w0[3]
+    )
+    back0 = after(back0, got_b1, got_c1)
+    keep_s1, send_s1 = grad_attn(place, own1, other1, *query_grads(dq1, got1), dkv_low1, swap(dkv_low1, "core"))
+    grads0 = grad_ffn(place, own0, other0, after(back0, send_s1), swap(back0, "core"), shards)
+    keep_a0, send_a0, keep_u0, send_u0 = grads0[:2], grads0[2:4], grads0[4:6], grads0[6:8]
+    got_a0 = swap_all(send_a0, "section")
+    got_u0 = [swap(send_u0[0], "dp"), swap(jnp.concatenate([send_u0[1], send_s1], 1), "dp")]
+    away_u1 = to_owner(jnp.concatenate(sum_u1, 0), 1)
+    dq0, dkv0, away0 = backward_attn(after(do0, send_u0[0], away_u1), saved0)
+    away0 = after(away0, got_a0[0], got_u0[0])
+    sum_a1 = scatter(plus(keep_b1, got_b1), plus(keep_c1, got_c1))
+    (sum_v0,) = scatter(plus(after(keep_u0[0], dkv0), got_u0[0]))
+    got0 = swap(away0, "core")
+    shares0 = collect_kv(dkv0, got0, [(got_a0[1], got_u0[1]), tuple(sum_a1)])
+    keep_q0, send_q0 = grad_attn(place, own0, other0, *query_grads(dq0, got0))
+    keep_b0, got_b0 = cross(after(keep_a0[0], dkv0), got_a0[0])
+    kept = after(jnp.concatenate([keep_u0[1], keep_s1], 1), shares0[-1], sum_v0)
+    late0 = plus(kept, got_u0[1])
+    away_a1 = to_owner(jnp.concatenate(sum_a1, 0), 1)
+    dq0 = after(dq0, send_q0, late0, away_a1, got_b0)
+    dkv_low0, dx0, dx0_low = backward_qkv(dq0, shares0, dm0, dgf0, w0, saved0)
+    got_q0 = swap(after(send_q0, shares0[-1]), "dp")
+    keep_c0, got_c0 = cross(after(keep_a0[1], shares0[-1]), got_a0[1])
+    (sum_w0,) = scatter(late0)
+    keep_k0, send_k0 = grad_attn(place, own0, other0, after(dkv_low0, got_c0), swap(dkv_low0, "core"))
+    last0 = [plus(after(keep, sum_w0), got) for keep, got in ((keep_b0, got_b0), (keep_c0, got_c0))]
+    sum_a0 = jnp.concatenate(scatter(*last0), 0)
     got_k0 = swap(send_k0, "dp")
-    keep_a0, send_a0 = halve(plus(keep_a0, got_a0))
-    got_a0 = swap(send_a0, "dp")
-    part_u0 = scatter_z(plus(keep_u0, got_u0))
-    part_a0 = scatter_z(plus(keep_a0, got_a0))
-    part_s0 = scatter_z(oqk((keep_o0, keep_q0, keep_k0), (got_o0, got_q0, got_k0)))
-
-    def whole(part_u, part_s, part_a, layer):
-        u = part_u.astype(F32) + to_owner(part_u, layer).astype(F32)
-        s = part_s.astype(F32) + to_owner(part_s, layer).astype(F32)
-        away = to_owner(part_a, layer)
-        down, gate = (part_a, away) if layer == 0 else (away, part_a)
-        return u, s, gate.astype(F32), down.astype(F32)
-
-    sums = zip(whole(part_u0, part_s0, part_a0, 0), whole(part_u1, part_s1, part_a1, 1))
-    up, small, gate, down = (jnp.where(section == 0, own0, own1) for own0, own1 in sums)
-
-    def narrow_low(array_in):
-        return project_t(array_in, spread).astype(BF)
-
-    def narrow_wide(array_in):
-        return array_in.reshape(array_in.shape[0], shards, room)[:, :, :size].reshape(array_in.shape[0], D)
-
-    def pair(own, got):
-        return jnp.where(section == 0, jnp.stack([own, got]), jnp.stack([got, own]))
-
-    got = swap(narrow_low(jnp.where(section == 0, y1, y0)), "section")
-    section_out = pair(narrow_low(jnp.where(section == 0, y0, y1)), got)
-    got = swap(narrow_low(jnp.where(section == 0, dx1_low, dx0.astype(BF))), "section").astype(F32)
-    input_grad = pair(narrow_wide(jnp.where(section == 0, dx0, dx1_low.astype(F32))), got)
-    up = from_blocks(up, room)[:size]
-    gate = from_blocks(gate, room)[:size]
-    small = from_blocks(small, room)[:size]
-    down = narrow_wide(from_blocks(down, ff_rows))
-    kd = KV * HD
-    gain_grads = total_over(jnp.concatenate([dga0, dgf0, dga1, dgf1], 0)).reshape(2, 2, PADDED)
-    gain = lax.dynamic_slice_in_dim(mine(gain_grads), lax.axis_index(plane) * room, room, 1)[:, :size]
-    outs = (
-        section_out,
-        input_grad,
-        gain[0],
-        small[:, PADDED : PADDED + D],
-        small[:, 2 * PADDED : 2 * PADDED + kd],
-        small[:, 2 * PADDED + kd :],
-        narrow_wide(small[:, :PADDED]),
-        gain[1],
-        gate,
-        up,
-        down,
-    )
+    keep_q0, keep_k0 = after(keep_q0, *last0), after(keep_k0, *last0)
+    pieces = [plus(keep_q0, got_q0), plus(keep_k0, got_k0)]
+
+    cut = send_u0[1].shape[1]
+    sum_s1, sum_w0 = sum_w0[cut:], sum_w0[:cut]
+    away_s1 = to_owner(sum_s1, 1)
+    wide = lambda width: (size, 1, width)
+    parts = [part for own in (sum_v0, sum_w0) for part in (own, to_owner(own, 0))]
+    cut_u = sum_u1[0].shape[0]
+    parts += [sum_u1[0], away_u1[:cut_u], sum_u1[1], away_u1[cut_u:]]
+    g_up, g_o = unpack(unpack_up_kernel, "unpack_up", place, parts + [spread], (wide(FF), wide(D)))
+    sum_s0 = scatter_z_small(jnp.concatenate(pieces, 1), g_up)
+    parts = [sum_s0, to_owner(sum_s0, 0), sum_s1, away_s1]
+    shapes = (wide(D), wide(KV * HD), wide(KV * HD), (LANES, room))
+    g_q, g_k, g_v, gains = unpack(unpack_qkv_kernel, "unpack_qkv", place, parts, shapes)
+    parts = [after(sum_a0, g_up, g_q), to_owner(sum_a0, 0), jnp.concatenate(sum_a1, 0), away_a1]
+    g_gate, g_down = unpack(unpack_down_kernel, "unpack_down", place, parts + [spread], (wide(FF), (ff_rows, D)))
+    section_out = join(place, y0, y1, got_y, spread, BF)
+    got = swap(jnp.where(section == 0, dx1_low, dx0_low), "section")
+    input_grad = join(place, dx0, dx1_low, got, spread, F32)
+    flat = lambda part: part.transpose(1, 0, 2)[0]
+    g_q, g_k, g_v, g_o, g_gate, g_up = map(flat, (g_q, g_k, g_v, g_o, g_gate, g_up))
+    outs = (section_out, input_grad, gains[0, :size], g_q, g_k, g_v, g_o, gains[1, :size], g_gate, g_up, g_down)
     return tuple(part[None] for part in outs)
 
 

time: 831 us -> 744 us (0.90)
  waiting for transfers between devices: 459 us -> 396 us
    ppermute x30 -> x28, waiting for transfers between devices: 159 us -> 113 us  [swap(): return lax.ppermute(block, axis, [(0, 1), (1, 0)])]
    ppermute x2, waiting for transfers between devices: 0.01 us -> 26.4 us  [scatter_z_small(): lax.ppermute(send, 'z', [(i, i ^ step) for i in range(count)])]
    all_gather x2 -> x3, waiting for transfers between devices: 127 us -> 101 us  [gathered(): return lax.all_gather(block, plane, axis=0)]
    ppermute x12, waiting for transfers between devices: 160 us -> 147 us  [move_z(): return lax.ppermute(block, 'z', route)]
    slice x8 -> x15, local copies, waits for them, and re-layouts: 3 us -> 13.8 us  [the longest x4 4.82 us: scatter(): cuts.append(total[at:at + piece.shape[1]])]
    pallas_call x2, Pallas kernels: 12.8 us -> 21.6 us  [attend(): pl.pallas_call(functools.partial(attend_kernel, zs), out_shape=(jax.Shape...]
    pallas_call x4 -> x3, Pallas kernels: 18.4 us -> 12.1 us  [grad_attn(): pl.pallas_call(grad_attn_kernel, out_shape=(shape, shape), in_specs=[SMEM...]
    ppermute x30 -> x28, starting transfers between devices: 29 us -> 24.5 us  [swap(): return lax.ppermute(block, axis, [(0, 1), (1, 0)])]
  transfers between devices with their start and end apart: 58 -> 57, of which waited for: 26 -> 36; matrix products, arithmetic and copies ran while one was open for 8% -> 7% of each run, Pallas kernels for 17% -> 20%
where the time goes in v2:
time: 744 us; the launch traced here: 734 us
  waiting for transfers between devices  396 us (53%)
  Pallas kernels  171 us (23%)
  starting transfers between devices  76.6 us (10%)
  other arithmetic  38 us (5%)
  local copies, waits for them, and re-layouts  28.4 us (4%)
  between operations  15.8 us (2%)
  matrix products  8.51 us (1%)
    ppermute x12, waiting for transfers between devices, move_z(): return lax.ppermute(block, 'z', route)  147 us
    ppermute x28, waiting for transfers between devices, swap(): return lax.ppermute(block, axis, [(0, 1), (1, 0)])  113 us
    all_gather x3, waiting for transfers between devices, gathered(): return lax.all_gather(block, plane, axis=0)  101 us
    ppermute x12, starting transfers between devices, move_z(): return lax.ppermute(block, 'z', route)  34 us
    ppermute x2, waiting for transfers between devices, scatter_z_small(): lax.ppermute(send, 'z', [(i, i ^ step) for i in range(count)])  26.4 us
    ppermute x28, starting transfers between devices, swap(): return lax.ppermute(block, axis, [(0, 1), (1, 0)])  24.5 us
    pallas_call x2, Pallas kernels, grad_ffn(): pl.pallas_call(grad_ffn_kernel, out_shape=[jax.ShapeDtypeStruct(shape, BF...  22.2 us
    pallas_call x2, Pallas kernels, attend(): pl.pallas_call(functools.partial(attend_kernel, zs), out_shape=(jax.Shape...  21.6 us
  transfers between devices with their start and end apart: 57, of which 36 were waited for; matrix products, arithmetic and copies ran while one was open for 7% of the time, Pallas kernels for 20%

profile of v2, /device:TPU:0, one launch (start us, length us, event | category | flops | bytes accessed | tf_op | source)
XLA Modules:
  0.0 734.1 jit_solution(829171537159163104)
XLA Ops:
  24.3 24.0 %collective-permute-done.5 = bf16[4352,128]{1,0:T(8,128)(2,1)S(1)} collective-permute-done((bf16[4352,128]{1,0:T(8,128)(2,1)S(1)}, bf16[4352,128]{1,0:T(8,128)(2,1)S(1)}, u32[]{:S(2)}, u32[]{:S(2)}) %collective-permute-start.5) | collective-permute-done | bytes 1114144 | tf_op jit(solution)/shard_map/ppermute | solution.py:153
  49.5 19.1 %all-gather.7.cloned.1.call-done = bf16[13312,128]{1,0:T(8,128)(2,1)} async-done(((bf16[832,128]{1,0:T(8,128)(2,1)}), bf16[13312,128]{1,0:T(8,128)(2,1)}) %all-gather.7.cloned.1.call-update) | async-done | bytes 3407888 | tf_op jit(solution)/shard_map/all_gather | solution.py:1346
  90.2 10.8 %collective-permute-done.1.refs_1_ = bf16[256,640]{1,0:T(8,128)(2,1)S(1)} collective-permute-done((bf16[256,640]{1,0:T(8,128)(2,1)}, bf16[256,640]{1,0:T(8,128)(2,1)S(1)}, u32[]{:S(2)}, u32[]{:S(2)}) %collective-permute-start.1) | collective-permute-done | bytes 327712 | tf_op jit(solution)/shard_map/ppermute | solution.py:159
  101.0 14.0 %collective-permute-done.2.refs_2_ = bf16[256,640]{1,0:T(8,128)(2,1)S(1)} collective-permute-done((bf16[256,640]{1,0:T(8,128)(2,1)}, bf16[256,640]{1,0:T(8,128)(2,1)S(1)}, u32[]{:S(2)}, u32[]{:S(2)}) %collective-permute-start.2) | collective-permute-done | bytes 327712 | tf_op jit(solution)/shard_map/ppermute | solution.py:159
  115.1 13.8 %collective-permute-done.3.refs_3_ = bf16[256,640]{1,0:T(8,128)(2,1)S(1)} collective-permute-done((bf16[256,640]{1,0:T(8,128)(2,1)}, bf16[256,640]{1,0:T(8,128)(2,1)S(1)}, u32[]{:S(2)}, u32[]{:S(2)}) %collective-permute-start.3) | collective-permute-done | bytes 327712 | tf_op jit(solution)/shard_map/ppermute | solution.py:159
  140.1 56.7 %all-gather.9.cloned.1.call-done = bf16[82944,128]{1,0:T(8,128)(2,1)} async-done(((bf16[5184,128]{1,0:T(8,128)(2,1)}), bf16[82944,128]{1,0:T(8,128)(2,1)}) %all-gather.9.cloned.1.call-update) | async-done | bytes 21233680 | tf_op jit(solution)/shard_map/all_gather | solution.py:1346
  198.8 11.2 %ffn_forward.1 = (bf16[256,5632]{1,0:T(8,128)(2,1)}, f32[256,1024]{1,0:T(8,128)}, bf16[2,256,2560]{2,1,0:T(8,128)(2,1)}, bf16[256,1024]{1,0:T(8,128)(2,1)}) custom-call(bf16[256,1024]{1,0:T(8,128)(2,1)} %get-tuple-element.114.op_ref, bf16[256,1024]{1,0:T(8,128)(2,1)} %convolution_convert_fusion.1.x_ref, bf16[256,1024]{1,0:T(8,128)(2,1)} %get-tuple-element.115.na_ref, ...), custom_call_target="tpu_custom_call" | custom-call | flops 10350000128 | bytes 33210000 | tf_op jit(solution)/shard_map/ffn_forward/pallas_call | solution.py:746
  216.0 10.8 %collective-permute-start.6 = (bf16[256,640]{1,0:T(8,128)(2,1)}, bf16[256,640]{1,0:T(8,128)(2,1)S(1)}, u32[]{:S(2)}, u32[]{:S(2)}) collective-permute-start(bf16[256,640]{1,0:T(8,128)(2,1)} %get-tuple-element.123.refs_0_), channel_id=1, source_target_pairs={{0,2},{2,4},{4,6},{1,3},{3,5},{5,7},{8,10},{10,12},{12,14},{9,11},... | collective-permute-start | bytes 983048 | tf_op jit(solution)/shard_map/ppermute | solution.py:159
  233.6 8.6 %collective-permute-done.6.refs_1_ = bf16[256,640]{1,0:T(8,128)(2,1)S(1)} collective-permute-done((bf16[256,640]{1,0:T(8,128)(2,1)}, bf16[256,640]{1,0:T(8,128)(2,1)S(1)}, u32[]{:S(2)}, u32[]{:S(2)}) %collective-permute-start.6) | collective-permute-done | bytes 327712 | tf_op jit(solution)/shard_map/ppermute | solution.py:159
  242.2 14.0 %collective-permute-done.7.refs_2_ = bf16[256,640]{1,0:T(8,128)(2,1)S(1)} collective-permute-done((bf16[256,640]{1,0:T(8,128)(2,1)}, bf16[256,640]{1,0:T(8,128)(2,1)S(1)}, u32[]{:S(2)}, u32[]{:S(2)}) %collective-permute-start.7) | collective-permute-done | bytes 327712 | tf_op jit(solution)/shard_map/ppermute | solution.py:159
  256.2 13.6 %collective-permute-done.8.refs_3_ = bf16[256,640]{1,0:T(8,128)(2,1)S(1)} collective-permute-done((bf16[256,640]{1,0:T(8,128)(2,1)}, bf16[256,640]{1,0:T(8,128)(2,1)S(1)}, u32[]{:S(2)}, u32[]{:S(2)}) %collective-permute-start.8) | collective-permute-done | bytes 327712 | tf_op jit(solution)/shard_map/ppermute | solution.py:159
  279.3 15.1 %attend.3 = (bf16[256,960]{1,0:T(8,128)(2,1)}, bf16[256,1024]{1,0:T(8,128)(2,1)}, f32[5,768]{1,0:T(8,128)}) custom-call(s32[2]{0:T(128)} %pad_add_fusion.1.rng, bf16[256,960]{1,0:T(8,128)(2,1)} %get-tuple-element.122.q_ref, bf16[256,640]{1,0:T(8,128)(2,1)} %get-tuple-element.123.refs_0_, bf16[256,640]{1,0:T(8,128)(2,1)} %copy-done.40, ...), custom_call_target="tpu_custom_call" | custom-call | flops 27599998976 | bytes 88560000 | tf_op jit(solution)/shard_map/attend/pallas_call | solution.py:462
  294.4 25.3 %all-gather.11.cloned.1.call-done = bf16[69632,128]{1,0:T(8,128)(2,1)} async-done(((bf16[4352,128]{1,0:T(8,128)(2,1)}), bf16[69632,128]{1,0:T(8,128)(2,1)}) %all-gather.11.cloned.1.call-update) | async-done | bytes 17825808 | tf_op jit(solution)/shard_map/all_gather | solution.py:1346
  319.7 18.9 %ffn_both.1 = (bf16[256,1024]{1,0:T(8,128)(2,1)}, bf16[2816,256]{1,0:T(8,128)(2,1)}, bf16[2816,256]{1,0:T(8,128)(2,1)}, bf16[256,7168]{1,0:T(8,128)(2,1)}, f32[2...) custom-call(s32[3]{0:T(128)} %pad_add_fusion.place, bf16[256,1024]{1,0:T(8,128)(2,1)} %get-tuple-element.124.op_ref, ...), custom_call_target="tpu_custom_call" | custom-call | flops 23000000512 | bytes 73800000 | tf_op jit(solution)/shard_map/ffn_both/pallas_call | solution.py:841
  349.7 11.1 %grad_ffn.2 = (bf16[8,640,128]{2,1,0:T(8,128)(2,1)}, bf16[8,640,128]{2,1,0:T(8,128)(2,1)}, bf16[8,640,128]{2,1,0:T(8,128)(2,1)}, bf16[8,640,128]{2,1,0:T(8,128)(...) custom-call(s32[3]{0:T(128)} %pad_add_fusion.place, ...), custom_call_target="tpu_custom_call" | custom-call | flops 12650000384 | bytes 40590000 | tf_op jit(solution)/shard_map/grad_ffn/pallas_call | solution.py:1100
  364.9 8.5 %attend_back.2 = (bf16[256,1024]{1,0:T(8,128)(2,1)}, bf16[4,256,640]{2,1,0:T(8,128)(2,1)}, bf16[6,256,640]{2,1,0:T(8,128)(2,1)}) custom-call(s32[2]{0:T(128)} %pad_add_fusion.1.rng, bf16[256,960]{1,0:T(8,128)(2,1)} %get-tuple-element.122.q_ref, bf16[256,960]{1,0:T(8,128)(2,1)} %get-tuple-element.129.o_ref, bf16[256,960]{1,0:T(8,128)(2,1)} %get-tuple-element.135.do_ref, ...), custom_call_target="tpu_custom_call" | custom-call | flops 27599998976 | bytes 88560000 | tf_op jit(solution)/shard_map/attend_back/pallas_call | solution.py:575
  373.4 11.5 %collective-permute-done.16 = bf16[4,960,128]{2,1,0:T(8,128)(2,1)S(1)} collective-permute-done((bf16[4,960,128]{2,1,0:T(8,128)(2,1)}, bf16[4,960,128]{2,1,0:T(8,128)(2,1)S(1)}, u32[]{:S(2)}, u32[]{:S(2)}) %collective-permute-start.16) | collective-permute-done | bytes 983072 | tf_op jit(solution)/shard_map/ppermute | solution.py:153
  384.9 9.3 %collective-permute-done.15 = bf16[8,640,128]{2,1,0:T(8,128)(2,1)S(1)} collective-permute-done((bf16[8,640,128]{2,1,0:T(8,128)(2,1)}, bf16[8,640,128]{2,1,0:T(8,128)(2,1)S(1)}, u32[]{:S(2)}, u32[]{:S(2)}) %collective-permute-start.15) | collective-permute-done | bytes 1310752 | tf_op jit(solution)/shard_map/ppermute | solution.py:153
  404.0 15.6 %collective-permute-done.18 = bf16[256,640]{1,0:T(8,128)(2,1)S(1)} collective-permute-done((bf16[256,640]{1,0:T(8,128)(2,1)S(1)}, bf16[256,640]{1,0:T(8,128)(2,1)S(1)}, u32[]{:S(2)}, u32[]{:S(2)}) %collective-permute-start.18) | collective-permute-done | bytes 327712 | tf_op jit(solution)/shard_map/ppermute | solution.py:159
  421.6 11.9 %collective-permute-done.19 = bf16[256,640]{1,0:T(8,128)(2,1)S(1)} collective-permute-done((bf16[256,640]{1,0:T(8,128)(2,1)S(1)}, bf16[256,640]{1,0:T(8,128)(2,1)S(1)}, u32[]{:S(2)}, u32[]{:S(2)}) %collective-permute-start.19) | collective-permute-done | bytes 327712 | tf_op jit(solution)/shard_map/ppermute | solution.py:159
  453.1 21.2 %both_back.1 = (bf16[272,640]{1,0:T(8,128)(2,1)}, bf16[256,1024]{1,0:T(8,128)(2,1)}, bf16[256,7168]{1,0:T(8,128)(2,1)}, f32[256,1024]{1,0:T(8,128)}, bf16[256,960]{1,0:T(8,128)(2,1)}, /*index=5*/f32[1,1024]{1,0:T(1,128)}) custom-call(bf16[256,1024]{1,0:T(8,128)(2,1)} %get-tuple-element.140.dq_ref.refs_0_, f32[256,128]{1,0:T(8,128)} %get-tuple-element.243.cos_ref, ...), custom_call_target="tpu_custom_call" | custom-call | flops 20700000256 | bytes 66420000 | tf_op jit(solution)/shard_map/both_back/pallas_call | solution.py:897
  499.7 11.1 %grad_ffn.3 = (bf16[8,640,128]{2,1,0:T(8,128)(2,1)}, bf16[8,640,128]{2,1,0:T(8,128)(2,1)}, bf16[8,640,128]{2,1,0:T(8,128)(2,1)}, bf16[8,640,128]{2,1,0:T(8,128)(...) custom-call(s32[3]{0:T(128)} %pad_add_fusion.place, ...), custom_call_target="tpu_custom_call" | custom-call | flops 12650000384 | bytes 40590000 | tf_op jit(solution)/shard_map/grad_ffn/pallas_call | solution.py:1100
  513.2 8.9 %attend_back.3 = (bf16[256,1024]{1,0:T(8,128)(2,1)}, bf16[4,256,640]{2,1,0:T(8,128)(2,1)}, bf16[6,256,640]{2,1,0:T(8,128)(2,1)}) custom-call(s32[2]{0:T(128)} %pad_add_fusion.1.rng, bf16[256,960]{1,0:T(8,128)(2,1)} %get-tuple-element.112.q_ref, bf16[256,960]{1,0:T(8,128)(2,1)} %get-tuple-element.128.o_ref, bf16[256,960]{1,0:T(8,128)(2,1)} %get-tuple-element.166.do_ref, ...), custom_call_target="tpu_custom_call" | custom-call | flops 27599998976 | bytes 88560000 | tf_op jit(solution)/shard_map/attend_back/pallas_call | solution.py:575
  522.1 12.2 %collective-permute-done.28 = bf16[4,960,128]{2,1,0:T(8,128)(2,1)S(1)} collective-permute-done((bf16[4,960,128]{2,1,0:T(8,128)(2,1)}, bf16[4,960,128]{2,1,0:T(8,128)(2,1)S(1)}, u32[]{:S(2)}, u32[]{:S(2)}) %collective-permute-start.28) | collective-permute-done | bytes 983072 | tf_op jit(solution)/shard_map/ppermute | solution.py:153
  534.3 8.8 %collective-permute-done.27 = bf16[8,640,128]{2,1,0:T(8,128)(2,1)S(1)} collective-permute-done((bf16[8,640,128]{2,1,0:T(8,128)(2,1)}, bf16[8,640,128]{2,1,0:T(8,128)(2,1)S(1)}, u32[]{:S(2)}, u32[]{:S(2)}) %collective-permute-start.27) | collective-permute-done | bytes 1310752 | tf_op jit(solution)/shard_map/ppermute | solution.py:153
  551.6 21.0 %collective-permute-done.30 = bf16[256,640]{1,0:T(8,128)(2,1)} collective-permute-done((bf16[256,640]{1,0:T(8,128)(2,1)}, bf16[256,640]{1,0:T(8,128)(2,1)}, u32[]{:S(2)}, u32[]{:S(2)}) %collective-permute-start.30) | collective-permute-done | bytes 327712 | tf_op jit(solution)/shard_map/ppermute | solution.py:159
  575.0 9.3 %collective-permute-done.31 = bf16[256,640]{1,0:T(8,128)(2,1)S(1)} collective-permute-done((bf16[256,640]{1,0:T(8,128)(2,1)S(1)}, bf16[256,640]{1,0:T(8,128)(2,1)S(1)}, u32[]{:S(2)}, u32[]{:S(2)}) %collective-permute-start.31) | collective-permute-done | bytes 327712 | tf_op jit(solution)/shard_map/ppermute | solution.py:159
  587.2 10.5 %collective-permute-done.34.refs_1_ = bf16[256,640]{1,0:T(8,128)(2,1)S(1)} collective-permute-done((bf16[256,640]{1,0:T(8,128)(2,1)}, bf16[256,640]{1,0:T(8,128)(2,1)S(1)}, u32[]{:S(2)}, u32[]{:S(2)}) %collective-permute-start.34) | collective-permute-done | bytes 327712 | tf_op jit(solution)/shard_map/ppermute | solution.py:159
  615.8 7.8 %collective-permute-done.36 = bf16[4,640,128]{2,1,0:T(8,128)(2,1)S(1)} collective-permute-done((bf16[4,640,128]{2,1,0:T(8,128)(2,1)S(1)}, bf16[4,640,128]{2,1,0:T(8,128)(2,1)S(1)}, u32[]{:S(2)}, u32[]{:S(2)}) %collective-permute-start.36) | collective-permute-done | bytes 655392 | tf_op jit(solution)/shard_map/ppermute | solution.py:153
  650.6 9.5 %collective-permute-done.41 = bf16[4,384,128]{2,1,0:T(8,128)(2,1)S(1)} collective-permute-done((bf16[4,384,128]{2,1,0:T(8,128)(2,1)}, bf16[4,384,128]{2,1,0:T(8,128)(2,1)S(1)}, u32[]{:S(2)}, u32[]{:S(2)}) %collective-permute-start.41) | collective-permute-done | bytes 393248 | tf_op jit(solution)/shard_map/ppermute | solution.py:153
  675.1 22.5 %collective-permute-done.42 = bf16[2,896,128]{2,1,0:T(8,128)(2,1)S(1)} collective-permute-done((bf16[2,896,128]{2,1,0:T(8,128)(2,1)S(1)}, bf16[2,896,128]{2,1,0:T(8,128)(2,1)S(1)}, u32[]{:S(2)}, u32[]{:S(2)}) %collective-permute-start.42) | collective-permute-done | bytes 458784 | tf_op jit(solution)/shard_map/ppermute | solution.py:1303
  709.0 6.7 collective-permute-done.46.refs_1_
  (329 shorter events, 244.7 us)
Async XLA Ops:
  7.2 61.4 %all-gather.7.cloned.1.call-start = ((), (), s32[]{:S(2)}) async-start(), calls=%async_computation.10 | async-start | bytes 3620864 | tf_op jit(solution)/shard_map/all_gather | solution.py:1346
  20.4 176.4 %all-gather.9.cloned.1.call-start = ((), (), s32[]{:S(2)}) async-start(), calls=%async_computation.11 | async-start | bytes 22560768 | tf_op jit(solution)/shard_map/all_gather | solution.py:1346
  22.5 25.8 %collective-permute-start.5 = (bf16[4352,128]{1,0:T(8,128)(2,1)S(1)}, bf16[4352,128]{1,0:T(8,128)(2,1)S(1)}, u32[]{:S(2)}, u32[]{:S(2)}) collective-permute-start(bf16[4352,128]{1,0:T(8,128)(2,1)S(1)} %pad_maximum_fusion.8), channel_id=1, source_target_pairs={{0,16},{16,0},{1,17},{17,1},{2,18},{18,2},{3,19},{19,3},{4,20},{20... | collective-permute-start | bytes 3342344 | tf_op jit(solution)/shard_map/ppermute | solution.py:153
  69.7 250.0 %all-gather.11.cloned.1.call-start = ((), (), s32[]{:S(2)}) async-start(), calls=%async_computation.12 | async-start | bytes 18939904 | tf_op jit(solution)/shard_map/all_gather | solution.py:1346
  85.6 29.4 %collective-permute-start.2 = (bf16[256,640]{1,0:T(8,128)(2,1)}, bf16[256,640]{1,0:T(8,128)(2,1)S(1)}, u32[]{:S(2)}, u32[]{:S(2)}) collective-permute-start(bf16[256,640]{1,0:T(8,128)(2,1)} %get-tuple-element.113.refs_0_), channel_id=1, source_target_pairs={{0,4},{2,6},{1,5},{3,7},{8,12},{10,14},{9,13},{11,15},{16,20},{18,... | collective-permute-start | bytes 983048 | tf_op jit(solution)/shard_map/ppermute | solution.py:159
  88.9 40.0 %collective-permute-start.3 = (bf16[256,640]{1,0:T(8,128)(2,1)}, bf16[256,640]{1,0:T(8,128)(2,1)S(1)}, u32[]{:S(2)}, u32[]{:S(2)}) collective-permute-start(bf16[256,640]{1,0:T(8,128)(2,1)} %get-tuple-element.113.refs_0_), channel_id=1, source_target_pairs={{0,6},{1,7},{8,14},{9,15},{16,22},{17,23},{24,30},{25,31}} | collective-permute-start | bytes 983048 | tf_op jit(solution)/shard_map/ppermute | solution.py:159
  128.9 365.1 %reduce-scatter.6.cloned.1.call-start = ((), (), s32[]{:S(2)}) async-start(), calls=%async_computation.5 | async-start | bytes 2293760 | tf_op jit(solution)/shard_map/reduce_scatter | solution.py:1290
  216.0 26.2 %collective-permute-start.6 = (bf16[256,640]{1,0:T(8,128)(2,1)}, bf16[256,640]{1,0:T(8,128)(2,1)S(1)}, u32[]{:S(2)}, u32[]{:S(2)}) collective-permute-start(bf16[256,640]{1,0:T(8,128)(2,1)} %get-tuple-element.123.refs_0_), channel_id=1, source_target_pairs={{0,2},{2,4},{4,6},{1,3},{3,5},{5,7},{8,10},{10,12},{12,14},{9,11},... | collective-permute-start | bytes 983048 | tf_op jit(solution)/shard_map/ppermute | solution.py:159
  226.8 29.4 %collective-permute-start.7 = (bf16[256,640]{1,0:T(8,128)(2,1)}, bf16[256,640]{1,0:T(8,128)(2,1)S(1)}, u32[]{:S(2)}, u32[]{:S(2)}) collective-permute-start(bf16[256,640]{1,0:T(8,128)(2,1)} %get-tuple-element.123.refs_0_), channel_id=1, source_target_pairs={{0,4},{2,6},{1,5},{3,7},{8,12},{10,14},{9,13},{11,15},{16,20},{18,... | collective-permute-start | bytes 983048 | tf_op jit(solution)/shard_map/ppermute | solution.py:159
  232.2 37.6 %collective-permute-start.8 = (bf16[256,640]{1,0:T(8,128)(2,1)}, bf16[256,640]{1,0:T(8,128)(2,1)S(1)}, u32[]{:S(2)}, u32[]{:S(2)}) collective-permute-start(bf16[256,640]{1,0:T(8,128)(2,1)} %get-tuple-element.123.refs_0_), channel_id=1, source_target_pairs={{0,6},{1,7},{8,14},{9,15},{16,22},{17,23},{24,30},{25,31}} | collective-permute-start | bytes 983048 | tf_op jit(solution)/shard_map/ppermute | solution.py:159
  340.3 22.3 %collective-permute-start.10 = (bf16[256,1024]{1,0:T(8,128)(2,1)S(1)}, bf16[256,1024]{1,0:T(8,128)(2,1)S(1)}, u32[]{:S(2)}, u32[]{:S(2)}) collective-permute-start(bf16[256,1024]{1,0:T(8,128)(2,1)S(1)} %broadcast_select_fusion.3), channel_id=1, source_target_pairs={{0,16},{16,0},{1,17},{17,1},{2,18},{18,2},{3,19},{19,3},{4,20},{20... | collective-permute-start | bytes 1572872 | tf_op jit(solution)/shard_map/ppermute | solution.py:153
  360.8 24.1 %collective-permute-start.16 = (bf16[4,960,128]{2,1,0:T(8,128)(2,1)}, bf16[4,960,128]{2,1,0:T(8,128)(2,1)S(1)}, u32[]{:S(2)}, u32[]{:S(2)}) collective-permute-start(bf16[4,960,128]{2,1,0:T(8,128)(2,1)} %get-tuple-element.134), channel_id=1, source_target_pairs={{0,8},{8,0},{1,9},{9,1},{2,10},{10,2},{3,11},{11,3},{4,12},{12,4},... | collective-permute-start | bytes 2949128 | tf_op jit(solution)/shard_map/ppermute | solution.py:153
  363.4 30.7 %collective-permute-start.15 = (bf16[8,640,128]{2,1,0:T(8,128)(2,1)}, bf16[8,640,128]{2,1,0:T(8,128)(2,1)S(1)}, u32[]{:S(2)}, u32[]{:S(2)}) collective-permute-start(bf16[8,640,128]{2,1,0:T(8,128)(2,1)} %get-tuple-element.143), channel_id=1, source_target_pairs={{0,16},{16,0},{1,17},{17,1},{2,18},{18,2},{3,19},{19,3},{4,20},{20... | collective-permute-start | bytes 3932168 | tf_op jit(solution)/shard_map/ppermute | solution.py:153
  402.4 39.3 %collective-permute-start.13 = (bf16[8,640,128]{2,1,0:T(8,128)(2,1)}, bf16[8,640,128]{2,1,0:T(8,128)(2,1)S(1)}, u32[]{:S(2)}, u32[]{:S(2)}) collective-permute-start(bf16[8,640,128]{2,1,0:T(8,128)(2,1)} %get-tuple-element.138), channel_id=1, source_target_pairs={{0,16},{16,0},{1,17},{17,1},{2,18},{18,2},{3,19},{19,3},{4,20},{20... | collective-permute-start | bytes 3932168 | tf_op jit(solution)/shard_map/ppermute | solution.py:153
  447.9 26.5 %collective-permute-start.22 = (bf16[4,640,128]{2,1,0:T(8,128)(2,1)}, bf16[4,640,128]{2,1,0:T(8,128)(2,1)}, u32[]{:S(2)}, u32[]{:S(2)}) collective-permute-start(bf16[4,640,128]{2,1,0:T(8,128)(2,1)} %dynamic-slice_bitcast_fusion.5), channel_id=1, source_target_pairs={{0,8},{8,0},{1,9},{9,1},{2,10},{10,2},{3,11},{11,3},{4,12},{12,4},... | collective-permute-start | bytes 1966088 | tf_op jit(solution)/shard_map/ppermute | solution.py:153
  449.5 27.5 %collective-permute-start.23 = (bf16[4,640,128]{2,1,0:T(8,128)(2,1)}, bf16[4,640,128]{2,1,0:T(8,128)(2,1)}, u32[]{:S(2)}, u32[]{:S(2)}) collective-permute-start(bf16[4,640,128]{2,1,0:T(8,128)(2,1)} %dynamic-slice_bitcast_fusion.4), channel_id=1, source_target_pairs={{0,8},{8,0},{1,9},{9,1},{2,10},{10,2},{3,11},{11,3},{4,12},{12,4},... | collective-permute-start | bytes 1966088 | tf_op jit(solution)/shard_map/ppermute | solution.py:153
  453.1 96.7 %reduce-scatter.8.cloned.1.call-start = ((), (), s32[]{:S(2)}) async-start(), calls=%async_computation.6 | async-start | bytes 1638400 | tf_op jit(solution)/shard_map/reduce_scatter | solution.py:1290
  477.0 22.6 %collective-permute-start.25 = (bf16[256,7168]{1,0:T(8,128)(2,1)}, bf16[256,7168]{1,0:T(8,128)(2,1)}, u32[]{:S(2)}, u32[]{:S(2)}) collective-permute-start(bf16[256,7168]{1,0:T(8,128)(2,1)} %get-tuple-element.160.back_hbm), channel_id=1, source_target_pairs={{0,1},{1,0},{2,3},{3,2},{4,5},{5,4},{6,7},{7,6},{8,9},{9,8},{10,11... | collective-permute-start | bytes 11010056 | tf_op jit(solution)/shard_map/ppermute | solution.py:153
  477.5 22.1 %collective-permute-start.21 = (bf16[2816,256]{1,0:T(8,128)(2,1)}, bf16[2816,256]{1,0:T(8,128)(2,1)}, u32[]{:S(2)}, u32[]{:S(2)}) collective-permute-start(bf16[2816,256]{1,0:T(8,128)(2,1)} %get-tuple-element.151), channel_id=1, source_target_pairs={{0,1},{1,0},{2,3},{3,2},{4,5},{5,4},{6,7},{7,6},{8,9},{9,8},{10,11... | collective-permute-start | bytes 4325384 | tf_op jit(solution)/shard_map/ppermute | solution.py:153
  493.4 93.8 %reduce-scatter.10.cloned.1.call-start = ((), (), s32[]{:S(2)}) async-start(), calls=%async_computation.7 | async-start | bytes 1228800 | tf_op jit(solution)/shard_map/reduce_scatter | solution.py:1290
  510.8 23.5 %collective-permute-start.28 = (bf16[4,960,128]{2,1,0:T(8,128)(2,1)}, bf16[4,960,128]{2,1,0:T(8,128)(2,1)S(1)}, u32[]{:S(2)}, u32[]{:S(2)}) collective-permute-start(bf16[4,960,128]{2,1,0:T(8,128)(2,1)} %get-tuple-element.161), channel_id=1, source_target_pairs={{0,8},{8,0},{1,9},{9,1},{2,10},{10,2},{3,11},{11,3},{4,12},{12,4},... | collective-permute-start | bytes 2949128 | tf_op jit(solution)/shard_map/ppermute | solution.py:153
  513.1 30.0 %collective-permute-start.27 = (bf16[8,640,128]{2,1,0:T(8,128)(2,1)}, bf16[8,640,128]{2,1,0:T(8,128)(2,1)S(1)}, u32[]{:S(2)}, u32[]{:S(2)}) collective-permute-start(bf16[8,640,128]{2,1,0:T(8,128)(2,1)} %get-tuple-element.170), channel_id=1, source_target_pairs={{0,16},{16,0},{1,17},{17,1},{2,18},{18,2},{3,19},{19,3},{4,20},{20... | collective-permute-start | bytes 3932168 | tf_op jit(solution)/shard_map/ppermute | solution.py:153
  544.6 41.2 %collective-permute-start.33 = (bf16[4,1728,128]{2,1,0:T(8,128)(2,1)}, bf16[4,1728,128]{2,1,0:T(8,128)(2,1)}, u32[]{:S(2)}, u32[]{:S(2)}) collective-permute-start(bf16[4,1728,128]{2,1,0:T(8,128)(2,1)} %pad_maximum_fusion.2), channel_id=1, source_target_pairs={{0,8},{8,0},{1,9},{9,1},{2,10},{10,2},{3,11},{11,3},{4,12},{12,4},... | collective-permute-start | bytes 5308424 | tf_op jit(solution)/shard_map/ppermute | solution.py:153
  546.6 100.9 %reduce-scatter.12.cloned.1.call-start = ((), (), s32[]{:S(2)}) async-start(), calls=%async_computation.8 | async-start | bytes 2211840 | tf_op jit(solution)/shard_map/reduce_scatter | solution.py:1290
  546.6 38.6 %collective-permute-start.32 = (bf16[8,640,128]{2,1,0:T(8,128)(2,1)}, bf16[8,640,128]{2,1,0:T(8,128)(2,1)}, u32[]{:S(2)}, u32[]{:S(2)}) collective-permute-start(bf16[8,640,128]{2,1,0:T(8,128)(2,1)} %get-tuple-element.177), channel_id=1, source_target_pairs={{0,16},{16,0},{1,17},{17,1},{2,18},{18,2},{3,19},{19,3},{4,20},{20... | collective-permute-start | bytes 3932168 | tf_op jit(solution)/shard_map/ppermute | solution.py:153
  548.5 24.2 %collective-permute-start.30 = (bf16[256,640]{1,0:T(8,128)(2,1)}, bf16[256,640]{1,0:T(8,128)(2,1)}, u32[]{:S(2)}, u32[]{:S(2)}) collective-permute-start(bf16[256,640]{1,0:T(8,128)(2,1)} %get-tuple-element.214), channel_id=1, source_target_pairs={{2,0},{4,2},{6,4},{3,1},{5,3},{7,5},{10,8},{12,10},{14,12},{11,9},... | collective-permute-start | bytes 983048 | tf_op jit(solution)/shard_map/ppermute | solution.py:159
  601.8 104.9 %reduce-scatter.14.cloned.1.call-start = ((), (), s32[]{:S(2)}) async-start(), calls=%async_computation.9 | async-start | bytes 1638400 | tf_op jit(solution)/shard_map/reduce_scatter | solution.py:1290
  614.6 27.7 %collective-permute-start.38 = (bf16[4,640,128]{2,1,0:T(8,128)(2,1)S(1)}, bf16[4,640,128]{2,1,0:T(8,128)(2,1)S(1)}, u32[]{:S(2)}, u32[]{:S(2)}) collective-permute-start(bf16[4,640,128]{2,1,0:T(8,128)(2,1)S(1)} %get-tuple-element.220), channel_id=1, source_target_pairs={{0,8},{8,0},{1,9},{9,1},{2,10},{10,2},{3,11},{11,3},{4,12},{12,4},... | collective-permute-start | bytes 1966088 | tf_op jit(solution)/shard_map/ppermute | solution.py:153
  635.8 33.4 %collective-permute-start.43 = (bf16[960,128]{1,0:T(8,128)(2,1)}, bf16[960,128]{1,0:T(8,128)(2,1)}, u32[]{:S(2)}, u32[]{:S(2)}) collective-permute-start(bf16[960,128]{1,0:T(8,128)(2,1)} %bitcast.57.refs_0_), channel_id=1, source_target_pairs={{16,0},{17,1},{18,2},{19,3},{20,4},{21,5},{22,6},{23,7},{24,8},{25... | collective-permute-start | bytes 737288 | tf_op jit(solution)/shard_map/ppermute | solution.py:1308
  637.1 23.1 %collective-permute-start.39 = (bf16[4,512,128]{2,1,0:T(8,128)(2,1)}, bf16[4,512,128]{2,1,0:T(8,128)(2,1)S(1)}, u32[]{:S(2)}, u32[]{:S(2)}) collective-permute-start(bf16[4,512,128]{2,1,0:T(8,128)(2,1)} %get-tuple-element.197), channel_id=1, source_target_pairs={{0,8},{8,0},{1,9},{9,1},{2,10},{10,2},{3,11},{11,3},{4,12},{12,4},... | collective-permute-start | bytes 1572872 | tf_op jit(solution)/shard_map/ppermute | solution.py:153
  639.0 24.3 %collective-permute-start.37 = (bf16[256,1024]{1,0:T(8,128)(2,1)}, bf16[256,1024]{1,0:T(8,128)(2,1)}, u32[]{:S(2)}, u32[]{:S(2)}) collective-permute-start(bf16[256,1024]{1,0:T(8,128)(2,1)} %broadcast_select_fusion.2), channel_id=1, source_target_pairs={{0,16},{16,0},{1,17},{17,1},{2,18},{18,2},{3,19},{19,3},{4,20},{20... | collective-permute-start | bytes 1572872 | tf_op jit(solution)/shard_map/ppermute | solution.py:153
  660.5 37.1 %collective-permute-start.42 = (bf16[2,896,128]{2,1,0:T(8,128)(2,1)S(1)}, bf16[2,896,128]{2,1,0:T(8,128)(2,1)S(1)}, u32[]{:S(2)}, u32[]{:S(2)}) collective-permute-start(bf16[2,896,128]{2,1,0:T(8,128)(2,1)S(1)} %dynamic-slice_bitcast_fusion.6), channel_id=1, source_target_pairs={{0,4},{2,6},{4,0},{6,2},{1,5},{3,7},{5,1},{7,3},{8,12},{10,14},{12... | collective-permute-start | bytes 1376264 | tf_op jit(solution)/shard_map/ppermute | solution.py:1303
  (89 other events, 1106.5 us)
Sparse Core Ops, SparseCore 0:
  20.5 48.0 all-gather.6
  70.7 126.0 all-gather.8
  198.4 121.2 all-gather.10
  453.2 40.7 reduce-scatter.5
  496.2 30.3 reduce-scatter.7
  546.7 35.2 reduce-scatter.9
  601.9 37.6 reduce-scatter.11
  649.2 42.6 reduce-scatter.13

commit v3 on v2

--- a/solution.py
+++ b/solution.py
@@ -609,10 +609,11 @@
     count = lax.axis_size("z")
     moving = plus(grads[count - 1], got[count - 1])
     for d in range(count - 2, -1, -1):
-        moved = move_z(after(moving, *before[d]) if d < len(before) else moving, -1)
+        moving = after(moving, *before[d]) if d < len(before) else moving
+        moved = move_z(moving, -1)
         own = plus(grads[d], got[d])
         if d == 0:
-            return [own, moved]
+            return [own, moved], moving
         moving = plus(own, moved)
 
 
@@ -1388,8 +1389,10 @@
         split = total.reshape((2, chips // 2) + total.shape[1:])
         return lax.dynamic_index_in_dim(split, half, 0, False), lax.dynamic_index_in_dim(split, 1 - half, 0, False)
 
-    def scatter(*pieces):
-        total = scatter_z(jnp.concatenate(pieces, 1) if len(pieces) > 1 else pieces[0])
+    def scatter(*pieces, joined=None):
+        if joined is None:
+            joined = jnp.concatenate(pieces, 1) if len(pieces) > 1 else pieces[0]
+        total = scatter_z(joined)
         cuts, at = [], 0
         for piece in pieces:
             cuts.append(total[at : at + piece.shape[1]])
@@ -1414,50 +1417,55 @@
     def query_grads(own, got):
         return own, got[-2:]
 
-    grads1 = grad_ffn(place, own1, other1, back1, swap(back1, "core"), shards)
+    got_y = swap(jnp.where(section == 0, y1, y0), "section")
+    back_other1 = swap(back1, "core")
+    dq1, dkv1, away1 = backward_attn(do1, saved1)
+    got1 = swap(away1, "core")
+    grads1 = grad_ffn(place, own1, other1, after(back1, dkv1), back_other1, shards)
     keep_a1, send_a1, keep_u1, send_u1 = grads1[:2], grads1[2:4], grads1[4:6], grads1[6:8]
     got_a1, got_u1 = swap_all(send_a1, "section"), swap_all(send_u1, "dp")
-    got_y = swap(jnp.where(section == 0, y1, y0), "section")
-    dq1, dkv1, away1 = backward_attn(after(do1, send_u1[0], got_y), saved1)
-    dkv1, away1 = after(dkv1, got_a1[0], got_u1[0]), after(away1, got_a1[0], got_u1[0])
-    got1 = swap(away1, "core")
-    shares1 = collect_kv(dkv1, got1)
-    dq1 = after(dq1, got_a1[1], got_u1[1])
-    keep_a1, keep_u1 = all_after(keep_a1, shares1[-1]), all_after(keep_u1, shares1[-1])
-    sum_u1 = scatter(*map(plus, keep_u1, got_u1))
-
-    (keep_b1, got_b1), (keep_c1, got_c1) = map(cross, keep_a1, got_a1)
+    shares1, _ = collect_kv(dkv1, got1, [(got_a1[0], got_u1[0]), (), (send_u1[0],)])
+    dq1 = after(dq1, got_y)
     dkv_low1, dx1_low, back0, dm0, do0, dgf0 = both_back(
         dq1, shares1, cos, sin, y0, w1[4], dm1, dgf1, w1[0], w1[1], mixed0, w0[5], gu0, spread, w0[2], w0[3]
     )
-    back0 = after(back0, got_b1, got_c1)
+
+    back0 = after(back0, got_a1[1], got_u1[1])
+    keep_a1, keep_u1 = all_after(keep_a1, dkv_low1), all_after(keep_u1, dkv_low1)
+    in_u1 = list(map(plus, keep_u1, got_u1))
+    joined_u1 = jnp.concatenate(in_u1, 1)
+    sum_u1 = scatter(*in_u1, joined=joined_u1)
+    back_other0 = swap(back0, "core")
+    grads0 = grad_ffn(place, own0, other0, after(back0, joined_u1), back_other0, shards)
+    keep_a0, send_a0, keep_u0, send_u0 = grads0[:2], grads0[2:4], grads0[4:6], grads0[6:8]
+    (keep_b1, got_b1), (keep_c1, got_c1) = map(cross, keep_a1, got_a1)
+    got1 = after(got1, send_u0[0])
     keep_s1, send_s1 = grad_attn(place, own1, other1, *query_grads(dq1, got1), dkv_low1, swap(dkv_low1, "core"))
-    grads0 = grad_ffn(place, own0, other0, after(back0, send_s1), swap(back0, "core"), shards)
-    keep_a0, send_a0, keep_u0, send_u0 = grads0[:2], grads0[2:4], grads0[4:6], grads0[6:8]
     got_a0 = swap_all(send_a0, "section")
     got_u0 = [swap(send_u0[0], "dp"), swap(jnp.concatenate([send_u0[1], send_s1], 1), "dp")]
     away_u1 = to_owner(jnp.concatenate(sum_u1, 0), 1)
-    dq0, dkv0, away0 = backward_attn(after(do0, send_u0[0], away_u1), saved0)
-    away0 = after(away0, got_a0[0], got_u0[0])
+    dq0, dkv0, away0 = backward_attn(after(do0, send_s1), saved0)
+    away0 = after(away0, got_a0[0], got_u0[0], got_b1, got_c1, *sum_u1)
+    keep_b1, keep_c1 = after(keep_b1, away0), after(keep_c1, away0)
     sum_a1 = scatter(plus(keep_b1, got_b1), plus(keep_c1, got_c1))
-    (sum_v0,) = scatter(plus(after(keep_u0[0], dkv0), got_u0[0]))
     got0 = swap(away0, "core")
-    shares0 = collect_kv(dkv0, got0, [(got_a0[1], got_u0[1]), tuple(sum_a1)])
+    shares0, last = collect_kv(dkv0, got0, [(got_a0[1], got_u0[1])])
     keep_q0, send_q0 = grad_attn(place, own0, other0, *query_grads(dq0, got0))
-    keep_b0, got_b0 = cross(after(keep_a0[0], dkv0), got_a0[0])
-    kept = after(jnp.concatenate([keep_u0[1], keep_s1], 1), shares0[-1], sum_v0)
-    late0 = plus(kept, got_u0[1])
+    keep_b0, got_b0 = cross(after(keep_a0[0], away0), got_a0[0])
+    kept = after(jnp.concatenate([keep_u0[1], keep_s1], 1), last)
+    late0 = [plus(after(keep_u0[0], last), got_u0[0]), plus(kept, got_u0[1])]
+    joined0 = jnp.concatenate(late0, 1)
     away_a1 = to_owner(jnp.concatenate(sum_a1, 0), 1)
-    dq0 = after(dq0, send_q0, late0, away_a1, got_b0)
+    dq0 = after(dq0, send_q0, joined0, away_u1, got_b0)
     dkv_low0, dx0, dx0_low = backward_qkv(dq0, shares0, dm0, dgf0, w0, saved0)
     got_q0 = swap(after(send_q0, shares0[-1]), "dp")
     keep_c0, got_c0 = cross(after(keep_a0[1], shares0[-1]), got_a0[1])
-    (sum_w0,) = scatter(late0)
+    sum_v0, sum_w0 = scatter(*late0, joined=joined0)
     keep_k0, send_k0 = grad_attn(place, own0, other0, after(dkv_low0, got_c0), swap(dkv_low0, "core"))
     last0 = [plus(after(keep, sum_w0), got) for keep, got in ((keep_b0, got_b0), (keep_c0, got_c0))]
     sum_a0 = jnp.concatenate(scatter(*last0), 0)
     got_k0 = swap(send_k0, "dp")
-    keep_q0, keep_k0 = after(keep_q0, *last0), after(keep_k0, *last0)
+    keep_q0, keep_k0 = after(keep_q0, away_a1, *last0), after(keep_k0, *last0)
     pieces = [plus(keep_q0, got_q0), plus(keep_k0, got_k0)]
 
     cut = send_u0[1].shape[1]
@@ -1468,12 +1476,13 @@
     cut_u = sum_u1[0].shape[0]
     parts += [sum_u1[0], away_u1[:cut_u], sum_u1[1], away_u1[cut_u:]]
     g_up, g_o = unpack(unpack_up_kernel, "unpack_up", place, parts + [spread], (wide(FF), wide(D)))
-    sum_s0 = scatter_z_small(jnp.concatenate(pieces, 1), g_up)
-    parts = [sum_s0, to_owner(sum_s0, 0), sum_s1, away_s1]
+    away_a0 = to_owner(sum_a0, 0)
+    sum_s0 = scatter_z_small(jnp.concatenate(pieces, 1), g_up, away_a0)
+    parts = [sum_a0, away_a0, jnp.concatenate(sum_a1, 0), away_a1]
+    g_gate, g_down = unpack(unpack_down_kernel, "unpack_down", place, parts + [spread], (wide(FF), (ff_rows, D)))
+    parts = [after(sum_s0, g_gate), to_owner(sum_s0, 0), sum_s1, away_s1]
     shapes = (wide(D), wide(KV * HD), wide(KV * HD), (LANES, room))
     g_q, g_k, g_v, gains = unpack(unpack_qkv_kernel, "unpack_qkv", place, parts, shapes)
-    parts = [after(sum_a0, g_up, g_q), to_owner(sum_a0, 0), jnp.concatenate(sum_a1, 0), away_a1]
-    g_gate, g_down = unpack(unpack_down_kernel, "unpack_down", place, parts + [spread], (wide(FF), (ff_rows, D)))
     section_out = join(place, y0, y1, got_y, spread, BF)
     got = swap(jnp.where(section == 0, dx1_low, dx0_low), "section")
     input_grad = join(place, dx0, dx1_low, got, spread, F32)

time: 744 us -> 723 us (0.972)
  waiting for transfers between devices: 396 us -> 374 us
    ppermute x28, waiting for transfers between devices: 113 us -> 38.2 us  [swap(): return lax.ppermute(block, axis, [(0, 1), (1, 0)])]
    ppermute x12, waiting for transfers between devices: 147 us -> 187 us  [move_z(): return lax.ppermute(block, 'z', route)]
    reduce_scatter x5 -> x4, waiting for transfers between devices: 0.64 us -> 26.6 us  [scatter_z(): return lax.psum_scatter(parts, 'z', scatter_dimension=0, tiled=False)]
    ppermute x2, waiting for transfers between devices: 26.4 us -> 17.6 us  [scatter_z_small(): lax.ppermute(send, 'z', [(i, i ^ step) for i in range(count)])]
  transfers between devices with their start and end apart: 57 -> 56, of which waited for: 36 -> 25; matrix products, arithmetic and copies ran while one was open for 7% -> 8% of each run, Pallas kernels for 20% -> 21%
where the time goes in v3:
time: 723 us; the launch traced here: 713 us
  waiting for transfers between devices  374 us (52%)
  Pallas kernels  171 us (24%)
  starting transfers between devices  76.9 us (11%)
  other arithmetic  41.1 us (6%)
  local copies, waits for them, and re-layouts  26 us (4%)
  between operations  16 us (2%)
  matrix products  8.59 us (1%)
    ppermute x12, waiting for transfers between devices, move_z(): return lax.ppermute(block, 'z', route)  187 us
    all_gather x3, waiting for transfers between devices, gathered(): return lax.all_gather(block, plane, axis=0)  101 us
    ppermute x28, waiting for transfers between devices, swap(): return lax.ppermute(block, axis, [(0, 1), (1, 0)])  38.2 us
    ppermute x12, starting transfers between devices, move_z(): return lax.ppermute(block, 'z', route)  34.2 us
    ppermute x28, starting transfers between devices, swap(): return lax.ppermute(block, axis, [(0, 1), (1, 0)])  28.1 us
    reduce_scatter x4, waiting for transfers between devices, scatter_z(): return lax.psum_scatter(parts, 'z', scatter_dimension=0, tiled=False)  26.6 us
    pallas_call x2, Pallas kernels, grad_ffn(): pl.pallas_call(grad_ffn_kernel, out_shape=[jax.ShapeDtypeStruct(shape, BF...  21.9 us
    pallas_call x2, Pallas kernels, attend(): pl.pallas_call(functools.partial(attend_kernel, zs), out_shape=(jax.Shape...  21.6 us
  transfers between devices with their start and end apart: 56, of which 25 were waited for; matrix products, arithmetic and copies ran while one was open for 8% of the time, Pallas kernels for 21%

profile of v3, /device:TPU:0, one launch (start us, length us, event | category | flops | bytes accessed | tf_op | source)
XLA Modules:
  0.0 712.9 jit_solution(8076756285358235402)
XLA Ops:
  24.3 24.0 %collective-permute-done.5 = bf16[4352,128]{1,0:T(8,128)(2,1)S(1)} collective-permute-done((bf16[4352,128]{1,0:T(8,128)(2,1)S(1)}, bf16[4352,128]{1,0:T(8,128)(2,1)S(1)}, u32[]{:S(2)}, u32[]{:S(2)}) %collective-permute-start.5) | collective-permute-done | bytes 1114144 | tf_op jit(solution)/shard_map/ppermute | solution.py:153
  49.5 19.1 %all-gather.7.cloned.1.call-done = bf16[13312,128]{1,0:T(8,128)(2,1)} async-done(((bf16[832,128]{1,0:T(8,128)(2,1)}), bf16[13312,128]{1,0:T(8,128)(2,1)}) %all-gather.7.cloned.1.call-update) | async-done | bytes 3407888 | tf_op jit(solution)/shard_map/all_gather | solution.py:1347
  75.4 6.4 qkv_forward.2
  90.1 10.9 %collective-permute-done.1.refs_1_ = bf16[256,640]{1,0:T(8,128)(2,1)S(1)} collective-permute-done((bf16[256,640]{1,0:T(8,128)(2,1)}, bf16[256,640]{1,0:T(8,128)(2,1)S(1)}, u32[]{:S(2)}, u32[]{:S(2)}) %collective-permute-start.1) | collective-permute-done | bytes 327712 | tf_op jit(solution)/shard_map/ppermute | solution.py:159
  101.0 14.0 %collective-permute-done.2.refs_2_ = bf16[256,640]{1,0:T(8,128)(2,1)S(1)} collective-permute-done((bf16[256,640]{1,0:T(8,128)(2,1)}, bf16[256,640]{1,0:T(8,128)(2,1)S(1)}, u32[]{:S(2)}, u32[]{:S(2)}) %collective-permute-start.2) | collective-permute-done | bytes 327712 | tf_op jit(solution)/shard_map/ppermute | solution.py:159
  115.1 13.8 %collective-permute-done.3.refs_3_ = bf16[256,640]{1,0:T(8,128)(2,1)S(1)} collective-permute-done((bf16[256,640]{1,0:T(8,128)(2,1)}, bf16[256,640]{1,0:T(8,128)(2,1)S(1)}, u32[]{:S(2)}, u32[]{:S(2)}) %collective-permute-start.3) | collective-permute-done | bytes 327712 | tf_op jit(solution)/shard_map/ppermute | solution.py:159
  133.5 6.6 attend.2
  140.1 56.7 %all-gather.9.cloned.1.call-done = bf16[82944,128]{1,0:T(8,128)(2,1)} async-done(((bf16[5184,128]{1,0:T(8,128)(2,1)}), bf16[82944,128]{1,0:T(8,128)(2,1)}) %all-gather.9.cloned.1.call-update) | async-done | bytes 21233680 | tf_op jit(solution)/shard_map/all_gather | solution.py:1347
  198.8 11.3 %ffn_forward.1 = (bf16[256,5632]{1,0:T(8,128)(2,1)}, f32[256,1024]{1,0:T(8,128)}, bf16[2,256,2560]{2,1,0:T(8,128)(2,1)}, bf16[256,1024]{1,0:T(8,128)(2,1)}) custom-call(bf16[256,1024]{1,0:T(8,128)(2,1)} %get-tuple-element.116.op_ref, bf16[256,1024]{1,0:T(8,128)(2,1)} %convolution_convert_fusion.1.x_ref, bf16[256,1024]{1,0:T(8,128)(2,1)} %get-tuple-element.117.na_ref, ...), custom_call_target="tpu_custom_call" | custom-call | flops 10350000128 | bytes 33210000 | tf_op jit(solution)/shard_map/ffn_forward/pallas_call | solution.py:747
  216.1 10.8 %collective-permute-start.6 = (bf16[256,640]{1,0:T(8,128)(2,1)}, bf16[256,640]{1,0:T(8,128)(2,1)S(1)}, u32[]{:S(2)}, u32[]{:S(2)}) collective-permute-start(bf16[256,640]{1,0:T(8,128)(2,1)} %get-tuple-element.125.refs_0_), channel_id=1, source_target_pairs={{0,2},{2,4},{4,6},{1,3},{3,5},{5,7},{8,10},{10,12},{12,14},{9,11},... | collective-permute-start | bytes 983048 | tf_op jit(solution)/shard_map/ppermute | solution.py:159
  233.6 8.6 %collective-permute-done.6.refs_1_ = bf16[256,640]{1,0:T(8,128)(2,1)S(1)} collective-permute-done((bf16[256,640]{1,0:T(8,128)(2,1)}, bf16[256,640]{1,0:T(8,128)(2,1)S(1)}, u32[]{:S(2)}, u32[]{:S(2)}) %collective-permute-start.6) | collective-permute-done | bytes 327712 | tf_op jit(solution)/shard_map/ppermute | solution.py:159
  242.2 14.0 %collective-permute-done.7.refs_2_ = bf16[256,640]{1,0:T(8,128)(2,1)S(1)} collective-permute-done((bf16[256,640]{1,0:T(8,128)(2,1)}, bf16[256,640]{1,0:T(8,128)(2,1)S(1)}, u32[]{:S(2)}, u32[]{:S(2)}) %collective-permute-start.7) | collective-permute-done | bytes 327712 | tf_op jit(solution)/shard_map/ppermute | solution.py:159
  256.3 13.6 %collective-permute-done.8.refs_3_ = bf16[256,640]{1,0:T(8,128)(2,1)S(1)} collective-permute-done((bf16[256,640]{1,0:T(8,128)(2,1)}, bf16[256,640]{1,0:T(8,128)(2,1)S(1)}, u32[]{:S(2)}, u32[]{:S(2)}) %collective-permute-start.8) | collective-permute-done | bytes 327712 | tf_op jit(solution)/shard_map/ppermute | solution.py:159
  279.5 15.1 %attend.3 = (bf16[256,960]{1,0:T(8,128)(2,1)}, bf16[256,1024]{1,0:T(8,128)(2,1)}, f32[5,768]{1,0:T(8,128)}) custom-call(s32[2]{0:T(128)} %pad_add_fusion.1.rng, bf16[256,960]{1,0:T(8,128)(2,1)} %get-tuple-element.124.q_ref, bf16[256,640]{1,0:T(8,128)(2,1)} %get-tuple-element.125.refs_0_, bf16[256,640]{1,0:T(8,128)(2,1)} %copy-done.29, ...), custom_call_target="tpu_custom_call" | custom-call | flops 27599998976 | bytes 88560000 | tf_op jit(solution)/shard_map/attend/pallas_call | solution.py:462
  294.6 25.1 %all-gather.11.cloned.1.call-done = bf16[69632,128]{1,0:T(8,128)(2,1)} async-done(((bf16[4352,128]{1,0:T(8,128)(2,1)}), bf16[69632,128]{1,0:T(8,128)(2,1)}) %all-gather.11.cloned.1.call-update) | async-done | bytes 17825808 | tf_op jit(solution)/shard_map/all_gather | solution.py:1347
  319.7 18.8 %ffn_both.1 = (bf16[256,1024]{1,0:T(8,128)(2,1)}, bf16[2816,256]{1,0:T(8,128)(2,1)}, bf16[2816,256]{1,0:T(8,128)(2,1)}, bf16[256,7168]{1,0:T(8,128)(2,1)}, f32[2...) custom-call(s32[3]{0:T(128)} %pad_add_fusion.place, bf16[256,1024]{1,0:T(8,128)(2,1)} %get-tuple-element.126.op_ref, ...), custom_call_target="tpu_custom_call" | custom-call | flops 23000000512 | bytes 73800000 | tf_op jit(solution)/shard_map/ffn_both/pallas_call | solution.py:842
  339.1 8.5 %attend_back.2 = (bf16[256,1024]{1,0:T(8,128)(2,1)}, bf16[4,256,640]{2,1,0:T(8,128)(2,1)}, bf16[6,256,640]{2,1,0:T(8,128)(2,1)}) custom-call(s32[2]{0:T(128)} %pad_add_fusion.1.rng, bf16[256,960]{1,0:T(8,128)(2,1)} %get-tuple-element.124.q_ref, bf16[256,960]{1,0:T(8,128)(2,1)} %get-tuple-element.131.o_ref, bf16[256,960]{1,0:T(8,128)(2,1)} %get-tuple-element.132.do_ref, ...), custom_call_target="tpu_custom_call" | custom-call | flops 27599998976 | bytes 88560000 | tf_op jit(solution)/shard_map/attend_back/pallas_call | solution.py:575
  352.0 11.0 %grad_ffn.2 = (bf16[8,640,128]{2,1,0:T(8,128)(2,1)}, bf16[8,640,128]{2,1,0:T(8,128)(2,1)}, bf16[8,640,128]{2,1,0:T(8,128)(2,1)}, bf16[8,640,128]{2,1,0:T(8,128)(...) custom-call(s32[3]{0:T(128)} %pad_add_fusion.place, ...), custom_call_target="tpu_custom_call" | custom-call | flops 12650000384 | bytes 40590000 | tf_op jit(solution)/shard_map/grad_ffn/pallas_call | solution.py:1101
  369.0 19.5 %collective-permute-done.14 = bf16[256,640]{1,0:T(8,128)(2,1)S(1)} collective-permute-done((bf16[256,640]{1,0:T(8,128)(2,1)S(1)}, bf16[256,640]{1,0:T(8,128)(2,1)S(1)}, u32[]{:S(2)}, u32[]{:S(2)}) %collective-permute-start.14) | collective-permute-done | bytes 327712 | tf_op jit(solution)/shard_map/ppermute | solution.py:159
  390.6 16.0 %collective-permute-done.15 = bf16[256,640]{1,0:T(8,128)(2,1)S(1)} collective-permute-done((bf16[256,640]{1,0:T(8,128)(2,1)S(1)}, bf16[256,640]{1,0:T(8,128)(2,1)S(1)}, u32[]{:S(2)}, u32[]{:S(2)}) %collective-permute-start.15) | collective-permute-done | bytes 327712 | tf_op jit(solution)/shard_map/ppermute | solution.py:159
  410.5 6.3 collective-permute-done.18.refs_1_
  417.5 20.9 %both_back.1 = (bf16[272,640]{1,0:T(8,128)(2,1)}, bf16[256,1024]{1,0:T(8,128)(2,1)}, bf16[256,7168]{1,0:T(8,128)(2,1)}, f32[256,1024]{1,0:T(8,128)}, bf16[256,960]{1,0:T(8,128)(2,1)}, /*index=5*/f32[1,1024]{1,0:T(1,128)}) custom-call(bf16[256,1024]{1,0:T(8,128)(2,1)} %get-tuple-element.135.dq_ref.refs_0_, f32[256,128]{1,0:T(8,128)} %get-tuple-element.251.cos_ref, ...), custom_call_target="tpu_custom_call" | custom-call | flops 20700000256 | bytes 66420000 | tf_op jit(solution)/shard_map/both_back/pallas_call | solution.py:898
  451.0 10.9 %grad_ffn.3 = (bf16[8,640,128]{2,1,0:T(8,128)(2,1)}, bf16[8,640,128]{2,1,0:T(8,128)(2,1)}, bf16[8,640,128]{2,1,0:T(8,128)(2,1)}, bf16[8,640,128]{2,1,0:T(8,128)(...) custom-call(s32[3]{0:T(128)} %pad_add_fusion.place, ...), custom_call_target="tpu_custom_call" | custom-call | flops 12650000384 | bytes 40590000 | tf_op jit(solution)/shard_map/grad_ffn/pallas_call | solution.py:1101
  469.9 8.8 %attend_back.3 = (bf16[256,1024]{1,0:T(8,128)(2,1)}, bf16[4,256,640]{2,1,0:T(8,128)(2,1)}, bf16[6,256,640]{2,1,0:T(8,128)(2,1)}) custom-call(s32[2]{0:T(128)} %pad_add_fusion.1.rng, bf16[256,960]{1,0:T(8,128)(2,1)} %get-tuple-element.114.q_ref, bf16[256,960]{1,0:T(8,128)(2,1)} %get-tuple-element.130.o_ref, bf16[256,960]{1,0:T(8,128)(2,1)} %get-tuple-element.165.do_ref, ...), custom_call_target="tpu_custom_call" | custom-call | flops 27599998976 | bytes 88560000 | tf_op jit(solution)/shard_map/attend_back/pallas_call | solution.py:575
  478.7 19.8 %reduce-scatter.5.cloned.1.call-done = bf16[1,1792,128]{2,1,0:T(8,128)(2,1)} async-done(((bf16[4,1792,128]{2,1,0:T(8,128)(2,1)}), bf16[1,1792,128]{2,1,0:T(8,128)(2,1)}) %reduce-scatter.5.cloned.1.call-update) | async-done | bytes 458768 | tf_op jit(solution)/shard_map/reduce_scatter | solution.py:1291
  513.4 16.3 %collective-permute-done.29 = bf16[256,640]{1,0:T(8,128)(2,1)S(1)} collective-permute-done((bf16[256,640]{1,0:T(8,128)(2,1)S(1)}, bf16[256,640]{1,0:T(8,128)(2,1)S(1)}, u32[]{:S(2)}, u32[]{:S(2)}) %collective-permute-start.29) | collective-permute-done | bytes 327712 | tf_op jit(solution)/shard_map/ppermute | solution.py:159
  531.2 31.7 %collective-permute-done.30 = bf16[256,640]{1,0:T(8,128)(2,1)S(1)} collective-permute-done((bf16[256,640]{1,0:T(8,128)(2,1)S(1)}, bf16[256,640]{1,0:T(8,128)(2,1)S(1)}, u32[]{:S(2)}, u32[]{:S(2)}) %collective-permute-start.30) | collective-permute-done | bytes 327712 | tf_op jit(solution)/shard_map/ppermute | solution.py:159
  589.8 22.1 %collective-permute-done.35.refs_1_ = bf16[256,640]{1,0:T(8,128)(2,1)S(1)} collective-permute-done((bf16[256,640]{1,0:T(8,128)(2,1)}, bf16[256,640]{1,0:T(8,128)(2,1)S(1)}, u32[]{:S(2)}, u32[]{:S(2)}) %collective-permute-start.35) | collective-permute-done | bytes 327712 | tf_op jit(solution)/shard_map/ppermute | solution.py:159
  613.9 6.5 qkv_backward.1
  624.3 6.8 reduce-scatter.9.cloned.1.call-done
  652.9 8.3 %collective-permute-done.41 = bf16[4,384,128]{2,1,0:T(8,128)(2,1)S(1)} collective-permute-done((bf16[4,384,128]{2,1,0:T(8,128)(2,1)}, bf16[4,384,128]{2,1,0:T(8,128)(2,1)S(1)}, u32[]{:S(2)}, u32[]{:S(2)}) %collective-permute-start.41) | collective-permute-done | bytes 393248 | tf_op jit(solution)/shard_map/ppermute | solution.py:153
  673.8 11.9 %collective-permute-done.42 = bf16[2,896,128]{2,1,0:T(8,128)(2,1)S(1)} collective-permute-done((bf16[2,896,128]{2,1,0:T(8,128)(2,1)S(1)}, bf16[2,896,128]{2,1,0:T(8,128)(2,1)S(1)}, u32[]{:S(2)}, u32[]{:S(2)}) %collective-permute-start.42) | collective-permute-done | bytes 458784 | tf_op jit(solution)/shard_map/ppermute | solution.py:1304
  (316 shorter events, 203.0 us)
Async XLA Ops:
  7.2 61.4 %all-gather.7.cloned.1.call-start = ((), (), s32[]{:S(2)}) async-start(), calls=%async_computation.8 | async-start | bytes 3620864 | tf_op jit(solution)/shard_map/all_gather | solution.py:1347
  20.4 176.4 %all-gather.9.cloned.1.call-start = ((), (), s32[]{:S(2)}) async-start(), calls=%async_computation.9 | async-start | bytes 22560768 | tf_op jit(solution)/shard_map/all_gather | solution.py:1347
  22.5 25.8 %collective-permute-start.5 = (bf16[4352,128]{1,0:T(8,128)(2,1)S(1)}, bf16[4352,128]{1,0:T(8,128)(2,1)S(1)}, u32[]{:S(2)}, u32[]{:S(2)}) collective-permute-start(bf16[4352,128]{1,0:T(8,128)(2,1)S(1)} %pad_maximum_fusion.9), channel_id=1, source_target_pairs={{0,16},{16,0},{1,17},{17,1},{2,18},{18,2},{3,19},{19,3},{4,20},{20... | collective-permute-start | bytes 3342344 | tf_op jit(solution)/shard_map/ppermute | solution.py:153
  69.7 250.0 %all-gather.11.cloned.1.call-start = ((), (), s32[]{:S(2)}) async-start(), calls=%async_computation.10 | async-start | bytes 18939904 | tf_op jit(solution)/shard_map/all_gather | solution.py:1347
  81.8 19.3 %collective-permute-start.1 = (bf16[256,640]{1,0:T(8,128)(2,1)}, bf16[256,640]{1,0:T(8,128)(2,1)S(1)}, u32[]{:S(2)}, u32[]{:S(2)}) collective-permute-start(bf16[256,640]{1,0:T(8,128)(2,1)} %get-tuple-element.115.refs_0_), channel_id=1, source_target_pairs={{0,2},{2,4},{4,6},{1,3},{3,5},{5,7},{8,10},{10,12},{12,14},{9,11},... | collective-permute-start | bytes 983048 | tf_op jit(solution)/shard_map/ppermute | solution.py:159
  85.7 29.4 %collective-permute-start.2 = (bf16[256,640]{1,0:T(8,128)(2,1)}, bf16[256,640]{1,0:T(8,128)(2,1)S(1)}, u32[]{:S(2)}, u32[]{:S(2)}) collective-permute-start(bf16[256,640]{1,0:T(8,128)(2,1)} %get-tuple-element.115.refs_0_), channel_id=1, source_target_pairs={{0,4},{2,6},{1,5},{3,7},{8,12},{10,14},{9,13},{11,15},{16,20},{18,... | collective-permute-start | bytes 983048 | tf_op jit(solution)/shard_map/ppermute | solution.py:159
  88.8 40.1 %collective-permute-start.3 = (bf16[256,640]{1,0:T(8,128)(2,1)}, bf16[256,640]{1,0:T(8,128)(2,1)S(1)}, u32[]{:S(2)}, u32[]{:S(2)}) collective-permute-start(bf16[256,640]{1,0:T(8,128)(2,1)} %get-tuple-element.115.refs_0_), channel_id=1, source_target_pairs={{0,6},{1,7},{8,14},{9,15},{16,22},{17,23},{24,30},{25,31}} | collective-permute-start | bytes 983048 | tf_op jit(solution)/shard_map/ppermute | solution.py:159
  128.9 369.6 %reduce-scatter.5.cloned.1.call-start = ((), (), s32[]{:S(2)}) async-start(), calls=%async_computation.4 | async-start | bytes 2293760 | tf_op jit(solution)/shard_map/reduce_scatter | solution.py:1291
  216.1 26.1 %collective-permute-start.6 = (bf16[256,640]{1,0:T(8,128)(2,1)}, bf16[256,640]{1,0:T(8,128)(2,1)S(1)}, u32[]{:S(2)}, u32[]{:S(2)}) collective-permute-start(bf16[256,640]{1,0:T(8,128)(2,1)} %get-tuple-element.125.refs_0_), channel_id=1, source_target_pairs={{0,2},{2,4},{4,6},{1,3},{3,5},{5,7},{8,10},{10,12},{12,14},{9,11},... | collective-permute-start | bytes 983048 | tf_op jit(solution)/shard_map/ppermute | solution.py:159
  226.8 29.4 %collective-permute-start.7 = (bf16[256,640]{1,0:T(8,128)(2,1)}, bf16[256,640]{1,0:T(8,128)(2,1)S(1)}, u32[]{:S(2)}, u32[]{:S(2)}) collective-permute-start(bf16[256,640]{1,0:T(8,128)(2,1)} %get-tuple-element.125.refs_0_), channel_id=1, source_target_pairs={{0,4},{2,6},{1,5},{3,7},{8,12},{10,14},{9,13},{11,15},{16,20},{18,... | collective-permute-start | bytes 983048 | tf_op jit(solution)/shard_map/ppermute | solution.py:159
  232.3 37.6 %collective-permute-start.8 = (bf16[256,640]{1,0:T(8,128)(2,1)}, bf16[256,640]{1,0:T(8,128)(2,1)S(1)}, u32[]{:S(2)}, u32[]{:S(2)}) collective-permute-start(bf16[256,640]{1,0:T(8,128)(2,1)} %get-tuple-element.125.refs_0_), channel_id=1, source_target_pairs={{0,6},{1,7},{8,14},{9,15},{16,22},{17,23},{24,30},{25,31}} | collective-permute-start | bytes 983048 | tf_op jit(solution)/shard_map/ppermute | solution.py:159
  363.0 43.7 %collective-permute-start.16 = (bf16[8,640,128]{2,1,0:T(8,128)(2,1)}, bf16[8,640,128]{2,1,0:T(8,128)(2,1)S(1)}, u32[]{:S(2)}, u32[]{:S(2)}) collective-permute-start(bf16[8,640,128]{2,1,0:T(8,128)(2,1)} %get-tuple-element.145), channel_id=1, source_target_pairs={{0,16},{16,0},{1,17},{17,1},{2,18},{18,2},{3,19},{19,3},{4,20},{20... | collective-permute-start | bytes 3932168 | tf_op jit(solution)/shard_map/ppermute | solution.py:153
  365.7 22.8 %collective-permute-start.14 = (bf16[256,640]{1,0:T(8,128)(2,1)S(1)}, bf16[256,640]{1,0:T(8,128)(2,1)S(1)}, u32[]{:S(2)}, u32[]{:S(2)}) collective-permute-start(bf16[256,640]{1,0:T(8,128)(2,1)S(1)} %get-tuple-element.144), channel_id=1, source_target_pairs={{2,0},{4,2},{6,4},{3,1},{5,3},{7,5},{10,8},{12,10},{14,12},{11,9},... | collective-permute-start | bytes 983048 | tf_op jit(solution)/shard_map/ppermute | solution.py:159
  367.4 39.3 %collective-permute-start.17 = (bf16[4,960,128]{2,1,0:T(8,128)(2,1)}, bf16[4,960,128]{2,1,0:T(8,128)(2,1)S(1)}, u32[]{:S(2)}, u32[]{:S(2)}) collective-permute-start(bf16[4,960,128]{2,1,0:T(8,128)(2,1)} %get-tuple-element.143), channel_id=1, source_target_pairs={{0,8},{8,0},{1,9},{9,1},{2,10},{10,2},{3,11},{11,3},{4,12},{12,4},... | collective-permute-start | bytes 2949128 | tf_op jit(solution)/shard_map/ppermute | solution.py:153
  408.1 31.4 %collective-permute-start.20 = (bf16[8,640,128]{2,1,0:T(8,128)(2,1)}, bf16[8,640,128]{2,1,0:T(8,128)(2,1)}, u32[]{:S(2)}, u32[]{:S(2)}) collective-permute-start(bf16[8,640,128]{2,1,0:T(8,128)(2,1)} %get-tuple-element.153), channel_id=1, source_target_pairs={{0,16},{16,0},{1,17},{17,1},{2,18},{18,2},{3,19},{19,3},{4,20},{20... | collective-permute-start | bytes 3932168 | tf_op jit(solution)/shard_map/ppermute | solution.py:153
  408.9 29.7 %collective-permute-start.21 = (bf16[4,832,128]{2,1,0:T(8,128)(2,1)}, bf16[4,832,128]{2,1,0:T(8,128)(2,1)S(1)}, u32[]{:S(2)}, u32[]{:S(2)}) collective-permute-start(bf16[4,832,128]{2,1,0:T(8,128)(2,1)} %get-tuple-element.154), channel_id=1, source_target_pairs={{0,8},{8,0},{1,9},{9,1},{2,10},{10,2},{3,11},{11,3},{4,12},{12,4},... | collective-permute-start | bytes 2555912 | tf_op jit(solution)/shard_map/ppermute | solution.py:153
  439.9 23.9 %collective-permute-start.23 = (bf16[272,640]{1,0:T(8,128)(2,1)}, bf16[272,640]{1,0:T(8,128)(2,1)}, u32[]{:S(2)}, u32[]{:S(2)}) collective-permute-start(bf16[272,640]{1,0:T(8,128)(2,1)} %get-tuple-element.157.refs_2_), channel_id=1, source_target_pairs={{0,1},{1,0},{2,3},{3,2},{4,5},{5,4},{6,7},{7,6},{8,9},{9,8},{10,11... | collective-permute-start | bytes 1044488 | tf_op jit(solution)/shard_map/ppermute | solution.py:153
  443.1 145.7 %reduce-scatter.7.cloned.1.call-start = ((), (), s32[]{:S(2)}) async-start(), calls=%async_computation.5 | async-start | bytes 1638400 | tf_op jit(solution)/shard_map/reduce_scatter | solution.py:1291
  447.0 54.1 %collective-permute-start.27 = (bf16[4,640,128]{2,1,0:T(8,128)(2,1)}, bf16[4,640,128]{2,1,0:T(8,128)(2,1)}, u32[]{:S(2)}, u32[]{:S(2)}) collective-permute-start(bf16[4,640,128]{2,1,0:T(8,128)(2,1)} %get-tuple-element.226), channel_id=1, source_target_pairs={{0,8},{8,0},{1,9},{9,1},{2,10},{10,2},{3,11},{11,3},{4,12},{12,4},... | collective-permute-start | bytes 1966088 | tf_op jit(solution)/shard_map/ppermute | solution.py:153
  450.0 51.1 %collective-permute-start.26 = (bf16[4,640,128]{2,1,0:T(8,128)(2,1)}, bf16[4,640,128]{2,1,0:T(8,128)(2,1)}, u32[]{:S(2)}, u32[]{:S(2)}) collective-permute-start(bf16[4,640,128]{2,1,0:T(8,128)(2,1)} %get-tuple-element.224), channel_id=1, source_target_pairs={{0,8},{8,0},{1,9},{9,1},{2,10},{10,2},{3,11},{11,3},{4,12},{12,4},... | collective-permute-start | bytes 1966088 | tf_op jit(solution)/shard_map/ppermute | solution.py:153
  461.9 39.3 %collective-permute-start.25 = (bf16[4,960,128]{2,1,0:T(8,128)(2,1)}, bf16[4,960,128]{2,1,0:T(8,128)(2,1)}, u32[]{:S(2)}, u32[]{:S(2)}) collective-permute-start(bf16[4,960,128]{2,1,0:T(8,128)(2,1)} %get-tuple-element.162), channel_id=1, source_target_pairs={{0,8},{8,0},{1,9},{9,1},{2,10},{10,2},{3,11},{11,3},{4,12},{12,4},... | collective-permute-start | bytes 2949128 | tf_op jit(solution)/shard_map/ppermute | solution.py:153
  469.0 32.2 %collective-permute-start.24 = (bf16[8,640,128]{2,1,0:T(8,128)(2,1)S(1)}, bf16[8,640,128]{2,1,0:T(8,128)(2,1)}, u32[]{:S(2)}, u32[]{:S(2)}) collective-permute-start(bf16[8,640,128]{2,1,0:T(8,128)(2,1)S(1)} %copy-done.43), channel_id=1, source_target_pairs={{0,16},{16,0},{1,17},{17,1},{2,18},{18,2},{3,19},{19,3},{4,20},{20... | collective-permute-start | bytes 3932168 | tf_op jit(solution)/shard_map/ppermute | solution.py:153
  504.0 59.9 %collective-permute-start.32 = (bf16[4,1728,128]{2,1,0:T(8,128)(2,1)}, bf16[4,1728,128]{2,1,0:T(8,128)(2,1)}, u32[]{:S(2)}, u32[]{:S(2)}) collective-permute-start(bf16[4,1728,128]{2,1,0:T(8,128)(2,1)} %pad_maximum_fusion.2), channel_id=1, source_target_pairs={{0,8},{8,0},{1,9},{9,1},{2,10},{10,2},{3,11},{11,3},{4,12},{12,4},... | collective-permute-start | bytes 5308424 | tf_op jit(solution)/shard_map/ppermute | solution.py:153
  505.4 58.4 %collective-permute-start.31 = (bf16[8,640,128]{2,1,0:T(8,128)(2,1)}, bf16[8,640,128]{2,1,0:T(8,128)(2,1)}, u32[]{:S(2)}, u32[]{:S(2)}) collective-permute-start(bf16[8,640,128]{2,1,0:T(8,128)(2,1)} %get-tuple-element.178), channel_id=1, source_target_pairs={{0,16},{16,0},{1,17},{17,1},{2,18},{18,2},{3,19},{19,3},{4,20},{20... | collective-permute-start | bytes 3932168 | tf_op jit(solution)/shard_map/ppermute | solution.py:153
  510.6 120.5 %reduce-scatter.9.cloned.1.call-start = ((), (), s32[]{:S(2)}) async-start(), calls=%async_computation.6 | async-start | bytes 3440640 | tf_op jit(solution)/shard_map/reduce_scatter | solution.py:1291
  529.8 33.2 %collective-permute-start.30 = (bf16[256,640]{1,0:T(8,128)(2,1)S(1)}, bf16[256,640]{1,0:T(8,128)(2,1)S(1)}, u32[]{:S(2)}, u32[]{:S(2)}) collective-permute-start(bf16[256,640]{1,0:T(8,128)(2,1)S(1)} %fusion.3), channel_id=1, source_target_pairs={{2,0},{4,2},{6,4},{3,1},{5,3},{7,5},{10,8},{12,10},{14,12},{11,9},... | collective-permute-start | bytes 983048 | tf_op jit(solution)/shard_map/ppermute | solution.py:159
  569.0 102.4 %reduce-scatter.11.cloned.1.call-start = ((), (), s32[]{:S(2)}) async-start(), calls=%async_computation.7 | async-start | bytes 1638400 | tf_op jit(solution)/shard_map/reduce_scatter | solution.py:1291
  582.7 29.2 %collective-permute-start.35 = (bf16[256,640]{1,0:T(8,128)(2,1)}, bf16[256,640]{1,0:T(8,128)(2,1)S(1)}, u32[]{:S(2)}, u32[]{:S(2)}) collective-permute-start(bf16[256,640]{1,0:T(8,128)(2,1)} %fusion.4), channel_id=1, source_target_pairs={{2,0},{4,2},{6,4},{3,1},{5,3},{7,5},{10,8},{12,10},{14,12},{11,9},... | collective-permute-start | bytes 983048 | tf_op jit(solution)/shard_map/ppermute | solution.py:159
  613.8 18.6 %collective-permute-start.38 = (bf16[4,640,128]{2,1,0:T(8,128)(2,1)S(1)}, bf16[4,640,128]{2,1,0:T(8,128)(2,1)S(1)}, u32[]{:S(2)}, u32[]{:S(2)}) collective-permute-start(bf16[4,640,128]{2,1,0:T(8,128)(2,1)S(1)} %get-tuple-element.228), channel_id=1, source_target_pairs={{0,8},{8,0},{1,9},{9,1},{2,10},{10,2},{3,11},{11,3},{4,12},{12,4},... | collective-permute-start | bytes 1966088 | tf_op jit(solution)/shard_map/ppermute | solution.py:153
  633.8 19.1 %collective-permute-start.37 = (bf16[1280,128]{1,0:T(8,128)(2,1)S(1)}, bf16[1280,128]{1,0:T(8,128)(2,1)S(1)}, u32[]{:S(2)}, u32[]{:S(2)}) collective-permute-start(bf16[1280,128]{1,0:T(8,128)(2,1)S(1)} %pad_maximum_fusion.12.refs_2_), channel_id=1, source_target_pairs={{0,16},{1,17},{2,18},{3,19},{4,20},{5,21},{6,22},{7,23},{8,24},{9,... | collective-permute-start | bytes 983048 | tf_op jit(solution)/shard_map/ppermute | solution.py:1309
  637.2 25.1 %collective-permute-start.39 = (bf16[4,512,128]{2,1,0:T(8,128)(2,1)S(1)}, bf16[4,512,128]{2,1,0:T(8,128)(2,1)S(1)}, u32[]{:S(2)}, u32[]{:S(2)}) collective-permute-start(bf16[4,512,128]{2,1,0:T(8,128)(2,1)S(1)} %copy-done.45), channel_id=1, source_target_pairs={{0,8},{8,0},{1,9},{9,1},{2,10},{10,2},{3,11},{11,3},{4,12},{12,4},... | collective-permute-start | bytes 1572872 | tf_op jit(solution)/shard_map/ppermute | solution.py:153
  662.6 23.0 %collective-permute-start.42 = (bf16[2,896,128]{2,1,0:T(8,128)(2,1)S(1)}, bf16[2,896,128]{2,1,0:T(8,128)(2,1)S(1)}, u32[]{:S(2)}, u32[]{:S(2)}) collective-permute-start(bf16[2,896,128]{2,1,0:T(8,128)(2,1)S(1)} %dynamic-slice_bitcast_fusion.8), channel_id=1, source_target_pairs={{0,4},{2,6},{4,0},{6,2},{1,5},{3,7},{5,1},{7,3},{8,12},{10,14},{12... | collective-permute-start | bytes 1376264 | tf_op jit(solution)/shard_map/ppermute | solution.py:1304
  (82 other events, 964.7 us)
Sparse Core Ops, SparseCore 0:
  20.5 48.0 all-gather.6
  70.7 126.0 all-gather.8
  198.4 121.2 all-gather.10
  443.2 55.2 reduce-scatter.4
  510.7 56.4 reduce-scatter.6
  569.4 61.6 reduce-scatter.8
  633.9 30.9 reduce-scatter.10

commit v4 on v3

--- a/solution.py
+++ b/solution.py
@@ -1417,7 +1417,6 @@
     def query_grads(own, got):
         return own, got[-2:]
 
-    got_y = swap(jnp.where(section == 0, y1, y0), "section")
     back_other1 = swap(back1, "core")
     dq1, dkv1, away1 = backward_attn(do1, saved1)
     got1 = swap(away1, "core")
@@ -1425,12 +1424,12 @@
     keep_a1, send_a1, keep_u1, send_u1 = grads1[:2], grads1[2:4], grads1[4:6], grads1[6:8]
     got_a1, got_u1 = swap_all(send_a1, "section"), swap_all(send_u1, "dp")
     shares1, _ = collect_kv(dkv1, got1, [(got_a1[0], got_u1[0]), (), (send_u1[0],)])
-    dq1 = after(dq1, got_y)
     dkv_low1, dx1_low, back0, dm0, do0, dgf0 = both_back(
         dq1, shares1, cos, sin, y0, w1[4], dm1, dgf1, w1[0], w1[1], mixed0, w0[5], gu0, spread, w0[2], w0[3]
     )
 
     back0 = after(back0, got_a1[1], got_u1[1])
+    got_y = swap(after(jnp.where(section == 0, y1, y0), back0), "section")
     keep_a1, keep_u1 = all_after(keep_a1, dkv_low1), all_after(keep_u1, dkv_low1)
     in_u1 = list(map(plus, keep_u1, got_u1))
     joined_u1 = jnp.concatenate(in_u1, 1)
@@ -1444,7 +1443,7 @@
     got_a0 = swap_all(send_a0, "section")
     got_u0 = [swap(send_u0[0], "dp"), swap(jnp.concatenate([send_u0[1], send_s1], 1), "dp")]
     away_u1 = to_owner(jnp.concatenate(sum_u1, 0), 1)
-    dq0, dkv0, away0 = backward_attn(after(do0, send_s1), saved0)
+    dq0, dkv0, away0 = backward_attn(after(do0, send_s1, got_y), saved0)
     away0 = after(away0, got_a0[0], got_u0[0], got_b1, got_c1, *sum_u1)
     keep_b1, keep_c1 = after(keep_b1, away0), after(keep_c1, away0)
     sum_a1 = scatter(plus(keep_b1, got_b1), plus(keep_c1, got_c1))

time: 723 us -> 716 us (level)
  waiting for transfers between devices: 374 us -> 363 us
    reduce_scatter x4, waiting for transfers between devices: 26.6 us -> 16.2 us  [scatter_z(): return lax.psum_scatter(parts, 'z', scatter_dimension=0, tiled=False)]
  transfers between devices with their start and end apart: 56 -> 56, of which waited for: 25 -> 27; matrix products, arithmetic and copies ran while one was open for 8% -> 9% of each run, Pallas kernels for 21% -> 21%
where the time goes in v4:
time: 716 us; the launch traced here: 706 us
  waiting for transfers between devices  363 us (51%)
  Pallas kernels  170 us (24%)
  starting transfers between devices  78.8 us (11%)
  other arithmetic  43.3 us (6%)
  local copies, waits for them, and re-layouts  26 us (4%)
  between operations  16 us (2%)
  matrix products  8.59 us (1%)
    ppermute x12, waiting for transfers between devices, move_z(): return lax.ppermute(block, 'z', route)  180 us
    all_gather x3, waiting for transfers between devices, gathered(): return lax.all_gather(block, plane, axis=0)  101 us
    ppermute x28, waiting for transfers between devices, swap(): return lax.ppermute(block, axis, [(0, 1), (1, 0)])  44.9 us
    ppermute x12, starting transfers between devices, move_z(): return lax.ppermute(block, 'z', route)  34.2 us
    ppermute x28, starting transfers between devices, swap(): return lax.ppermute(block, axis, [(0, 1), (1, 0)])  29.2 us
    pallas_call x2, Pallas kernels, grad_ffn(): pl.pallas_call(grad_ffn_kernel, out_shape=[jax.ShapeDtypeStruct(shape, BF...  21.9 us
    pallas_call x2, Pallas kernels, attend(): pl.pallas_call(functools.partial(attend_kernel, zs), out_shape=(jax.Shape...  21.6 us
    pallas_call x1, Pallas kernels, both_back(): pl.pallas_call(functools.partial(both_back_kernel, base, first, len(share...  20.9 us
  transfers between devices with their start and end apart: 56, of which 27 were waited for; matrix products, arithmetic and copies ran while one was open for 9% of the time, Pallas kernels for 21%

profile of v4, /device:TPU:0, one launch (start us, length us, event | category | flops | bytes accessed | tf_op | source)
XLA Modules:
  0.0 705.6 jit_solution(10296746703456001355)
XLA Ops:
  24.3 24.0 %collective-permute-done.5 = bf16[4352,128]{1,0:T(8,128)(2,1)S(1)} collective-permute-done((bf16[4352,128]{1,0:T(8,128)(2,1)S(1)}, bf16[4352,128]{1,0:T(8,128)(2,1)S(1)}, u32[]{:S(2)}, u32[]{:S(2)}) %collective-permute-start.5) | collective-permute-done | bytes 1114144 | tf_op jit(solution)/shard_map/ppermute | solution.py:153
  49.5 19.1 %all-gather.7.cloned.1.call-done = bf16[13312,128]{1,0:T(8,128)(2,1)} async-done(((bf16[832,128]{1,0:T(8,128)(2,1)}), bf16[13312,128]{1,0:T(8,128)(2,1)}) %all-gather.7.cloned.1.call-update) | async-done | bytes 3407888 | tf_op jit(solution)/shard_map/all_gather | solution.py:1347
  75.4 6.4 qkv_forward.2
  90.1 10.9 %collective-permute-done.1.refs_1_ = bf16[256,640]{1,0:T(8,128)(2,1)S(1)} collective-permute-done((bf16[256,640]{1,0:T(8,128)(2,1)}, bf16[256,640]{1,0:T(8,128)(2,1)S(1)}, u32[]{:S(2)}, u32[]{:S(2)}) %collective-permute-start.1) | collective-permute-done | bytes 327712 | tf_op jit(solution)/shard_map/ppermute | solution.py:159
  101.0 14.0 %collective-permute-done.2.refs_2_ = bf16[256,640]{1,0:T(8,128)(2,1)S(1)} collective-permute-done((bf16[256,640]{1,0:T(8,128)(2,1)}, bf16[256,640]{1,0:T(8,128)(2,1)S(1)}, u32[]{:S(2)}, u32[]{:S(2)}) %collective-permute-start.2) | collective-permute-done | bytes 327712 | tf_op jit(solution)/shard_map/ppermute | solution.py:159
  115.1 13.8 %collective-permute-done.3.refs_3_ = bf16[256,640]{1,0:T(8,128)(2,1)S(1)} collective-permute-done((bf16[256,640]{1,0:T(8,128)(2,1)}, bf16[256,640]{1,0:T(8,128)(2,1)S(1)}, u32[]{:S(2)}, u32[]{:S(2)}) %collective-permute-start.3) | collective-permute-done | bytes 327712 | tf_op jit(solution)/shard_map/ppermute | solution.py:159
  133.5 6.6 attend.2
  140.1 56.7 %all-gather.9.cloned.1.call-done = bf16[82944,128]{1,0:T(8,128)(2,1)} async-done(((bf16[5184,128]{1,0:T(8,128)(2,1)}), bf16[82944,128]{1,0:T(8,128)(2,1)}) %all-gather.9.cloned.1.call-update) | async-done | bytes 21233680 | tf_op jit(solution)/shard_map/all_gather | solution.py:1347
  198.8 11.3 %ffn_forward.1 = (bf16[256,5632]{1,0:T(8,128)(2,1)}, f32[256,1024]{1,0:T(8,128)}, bf16[2,256,2560]{2,1,0:T(8,128)(2,1)}, bf16[256,1024]{1,0:T(8,128)(2,1)}) custom-call(bf16[256,1024]{1,0:T(8,128)(2,1)} %get-tuple-element.116.op_ref, bf16[256,1024]{1,0:T(8,128)(2,1)} %convolution_convert_fusion.1.x_ref, bf16[256,1024]{1,0:T(8,128)(2,1)} %get-tuple-element.117.na_ref, ...), custom_call_target="tpu_custom_call" | custom-call | flops 10350000128 | bytes 33210000 | tf_op jit(solution)/shard_map/ffn_forward/pallas_call | solution.py:747
  216.1 10.8 %collective-permute-start.6 = (bf16[256,640]{1,0:T(8,128)(2,1)}, bf16[256,640]{1,0:T(8,128)(2,1)S(1)}, u32[]{:S(2)}, u32[]{:S(2)}) collective-permute-start(bf16[256,640]{1,0:T(8,128)(2,1)} %get-tuple-element.125.refs_0_), channel_id=1, source_target_pairs={{0,2},{2,4},{4,6},{1,3},{3,5},{5,7},{8,10},{10,12},{12,14},{9,11},... | collective-permute-start | bytes 983048 | tf_op jit(solution)/shard_map/ppermute | solution.py:159
  233.6 8.6 %collective-permute-done.6.refs_1_ = bf16[256,640]{1,0:T(8,128)(2,1)S(1)} collective-permute-done((bf16[256,640]{1,0:T(8,128)(2,1)}, bf16[256,640]{1,0:T(8,128)(2,1)S(1)}, u32[]{:S(2)}, u32[]{:S(2)}) %collective-permute-start.6) | collective-permute-done | bytes 327712 | tf_op jit(solution)/shard_map/ppermute | solution.py:159
  242.2 14.0 %collective-permute-done.7.refs_2_ = bf16[256,640]{1,0:T(8,128)(2,1)S(1)} collective-permute-done((bf16[256,640]{1,0:T(8,128)(2,1)}, bf16[256,640]{1,0:T(8,128)(2,1)S(1)}, u32[]{:S(2)}, u32[]{:S(2)}) %collective-permute-start.7) | collective-permute-done | bytes 327712 | tf_op jit(solution)/shard_map/ppermute | solution.py:159
  256.3 13.6 %collective-permute-done.8.refs_3_ = bf16[256,640]{1,0:T(8,128)(2,1)S(1)} collective-permute-done((bf16[256,640]{1,0:T(8,128)(2,1)}, bf16[256,640]{1,0:T(8,128)(2,1)S(1)}, u32[]{:S(2)}, u32[]{:S(2)}) %collective-permute-start.8) | collective-permute-done | bytes 327712 | tf_op jit(solution)/shard_map/ppermute | solution.py:159
  279.5 15.1 %attend.3 = (bf16[256,960]{1,0:T(8,128)(2,1)}, bf16[256,1024]{1,0:T(8,128)(2,1)}, f32[5,768]{1,0:T(8,128)}) custom-call(s32[2]{0:T(128)} %pad_add_fusion.1.rng, bf16[256,960]{1,0:T(8,128)(2,1)} %get-tuple-element.124.q_ref, bf16[256,640]{1,0:T(8,128)(2,1)} %get-tuple-element.125.refs_0_, bf16[256,640]{1,0:T(8,128)(2,1)} %copy-done.28, ...), custom_call_target="tpu_custom_call" | custom-call | flops 27599998976 | bytes 88560000 | tf_op jit(solution)/shard_map/attend/pallas_call | solution.py:462
  294.6 25.1 %all-gather.11.cloned.1.call-done = bf16[69632,128]{1,0:T(8,128)(2,1)} async-done(((bf16[4352,128]{1,0:T(8,128)(2,1)}), bf16[69632,128]{1,0:T(8,128)(2,1)}) %all-gather.11.cloned.1.call-update) | async-done | bytes 17825808 | tf_op jit(solution)/shard_map/all_gather | solution.py:1347
  319.7 18.8 %ffn_both.1 = (bf16[256,1024]{1,0:T(8,128)(2,1)}, bf16[2816,256]{1,0:T(8,128)(2,1)}, bf16[2816,256]{1,0:T(8,128)(2,1)}, bf16[256,7168]{1,0:T(8,128)(2,1)}, f32[2...) custom-call(s32[3]{0:T(128)} %pad_add_fusion.place, bf16[256,1024]{1,0:T(8,128)(2,1)} %get-tuple-element.126.op_ref, ...), custom_call_target="tpu_custom_call" | custom-call | flops 23000000512 | bytes 73800000 | tf_op jit(solution)/shard_map/ffn_both/pallas_call | solution.py:842
  339.1 8.5 %attend_back.2 = (bf16[256,1024]{1,0:T(8,128)(2,1)}, bf16[4,256,640]{2,1,0:T(8,128)(2,1)}, bf16[6,256,640]{2,1,0:T(8,128)(2,1)}) custom-call(s32[2]{0:T(128)} %pad_add_fusion.1.rng, bf16[256,960]{1,0:T(8,128)(2,1)} %get-tuple-element.124.q_ref, bf16[256,960]{1,0:T(8,128)(2,1)} %get-tuple-element.130.o_ref, bf16[256,960]{1,0:T(8,128)(2,1)} %get-tuple-element.131.do_ref, ...), custom_call_target="tpu_custom_call" | custom-call | flops 27599998976 | bytes 88560000 | tf_op jit(solution)/shard_map/attend_back/pallas_call | solution.py:575
  352.0 11.0 %grad_ffn.2 = (bf16[8,640,128]{2,1,0:T(8,128)(2,1)}, bf16[8,640,128]{2,1,0:T(8,128)(2,1)}, bf16[8,640,128]{2,1,0:T(8,128)(2,1)}, bf16[8,640,128]{2,1,0:T(8,128)(...) custom-call(s32[3]{0:T(128)} %pad_add_fusion.place, ...), custom_call_target="tpu_custom_call" | custom-call | flops 12650000384 | bytes 40590000 | tf_op jit(solution)/shard_map/grad_ffn/pallas_call | solution.py:1101
  369.0 19.5 %collective-permute-done.13 = bf16[256,640]{1,0:T(8,128)(2,1)S(1)} collective-permute-done((bf16[256,640]{1,0:T(8,128)(2,1)S(1)}, bf16[256,640]{1,0:T(8,128)(2,1)S(1)}, u32[]{:S(2)}, u32[]{:S(2)}) %collective-permute-start.13) | collective-permute-done | bytes 327712 | tf_op jit(solution)/shard_map/ppermute | solution.py:159
  389.9 16.7 %collective-permute-done.14 = bf16[256,640]{1,0:T(8,128)(2,1)S(1)} collective-permute-done((bf16[256,640]{1,0:T(8,128)(2,1)S(1)}, bf16[256,640]{1,0:T(8,128)(2,1)S(1)}, u32[]{:S(2)}, u32[]{:S(2)}) %collective-permute-start.14) | collective-permute-done | bytes 327712 | tf_op jit(solution)/shard_map/ppermute | solution.py:159
  410.3 6.5 collective-permute-done.17.refs_1_
  417.5 20.9 %both_back.1 = (bf16[272,640]{1,0:T(8,128)(2,1)}, bf16[256,1024]{1,0:T(8,128)(2,1)}, bf16[256,7168]{1,0:T(8,128)(2,1)}, f32[256,1024]{1,0:T(8,128)}, bf16[256,960]{1,0:T(8,128)(2,1)}, /*index=5*/f32[1,1024]{1,0:T(1,128)}) custom-call(bf16[256,1024]{1,0:T(8,128)(2,1)} %get-tuple-element.133.dq_ref.refs_0_, f32[256,128]{1,0:T(8,128)} %get-tuple-element.251.cos_ref, ...), custom_call_target="tpu_custom_call" | custom-call | flops 20700000256 | bytes 66420000 | tf_op jit(solution)/shard_map/both_back/pallas_call | solution.py:898
  454.0 10.8 %grad_ffn.3 = (bf16[8,640,128]{2,1,0:T(8,128)(2,1)}, bf16[8,640,128]{2,1,0:T(8,128)(2,1)}, bf16[8,640,128]{2,1,0:T(8,128)(2,1)}, bf16[8,640,128]{2,1,0:T(8,128)(...) custom-call(s32[3]{0:T(128)} %pad_add_fusion.place, ...), custom_call_target="tpu_custom_call" | custom-call | flops 12650000384 | bytes 40590000 | tf_op jit(solution)/shard_map/grad_ffn/pallas_call | solution.py:1101
  472.7 8.8 %attend_back.3 = (bf16[256,1024]{1,0:T(8,128)(2,1)}, bf16[4,256,640]{2,1,0:T(8,128)(2,1)}, bf16[6,256,640]{2,1,0:T(8,128)(2,1)}) custom-call(s32[2]{0:T(128)} %pad_add_fusion.1.rng, bf16[256,960]{1,0:T(8,128)(2,1)} %get-tuple-element.114.q_ref, bf16[256,960]{1,0:T(8,128)(2,1)} %get-tuple-element.153.o_ref, bf16[256,960]{1,0:T(8,128)(2,1)} %get-tuple-element.165.do_ref, ...), custom_call_target="tpu_custom_call" | custom-call | flops 27599998976 | bytes 88560000 | tf_op jit(solution)/shard_map/attend_back/pallas_call | solution.py:575
  481.5 10.9 %reduce-scatter.5.cloned.1.call-done = bf16[1,1792,128]{2,1,0:T(8,128)(2,1)} async-done(((bf16[4,1792,128]{2,1,0:T(8,128)(2,1)}), bf16[1,1792,128]{2,1,0:T(8,128)(2,1)}) %reduce-scatter.5.cloned.1.call-update) | async-done | bytes 458768 | tf_op jit(solution)/shard_map/reduce_scatter | solution.py:1291
  495.0 6.3 collective-permute-done.25
  513.2 28.1 %collective-permute-done.29 = bf16[256,640]{1,0:T(8,128)(2,1)S(1)} collective-permute-done((bf16[256,640]{1,0:T(8,128)(2,1)S(1)}, bf16[256,640]{1,0:T(8,128)(2,1)S(1)}, u32[]{:S(2)}, u32[]{:S(2)}) %collective-permute-start.29) | collective-permute-done | bytes 327712 | tf_op jit(solution)/shard_map/ppermute | solution.py:159
  542.9 15.1 %collective-permute-done.30 = bf16[256,640]{1,0:T(8,128)(2,1)S(1)} collective-permute-done((bf16[256,640]{1,0:T(8,128)(2,1)S(1)}, bf16[256,640]{1,0:T(8,128)(2,1)S(1)}, u32[]{:S(2)}, u32[]{:S(2)}) %collective-permute-start.30) | collective-permute-done | bytes 327712 | tf_op jit(solution)/shard_map/ppermute | solution.py:159
  585.4 19.3 %collective-permute-done.35.refs_1_ = bf16[256,640]{1,0:T(8,128)(2,1)S(1)} collective-permute-done((bf16[256,640]{1,0:T(8,128)(2,1)}, bf16[256,640]{1,0:T(8,128)(2,1)S(1)}, u32[]{:S(2)}, u32[]{:S(2)}) %collective-permute-start.35) | collective-permute-done | bytes 327712 | tf_op jit(solution)/shard_map/ppermute | solution.py:159
  608.0 6.5 qkv_backward.1
  645.7 8.3 %collective-permute-done.41 = bf16[4,384,128]{2,1,0:T(8,128)(2,1)S(1)} collective-permute-done((bf16[4,384,128]{2,1,0:T(8,128)(2,1)}, bf16[4,384,128]{2,1,0:T(8,128)(2,1)S(1)}, u32[]{:S(2)}, u32[]{:S(2)}) %collective-permute-start.41) | collective-permute-done | bytes 393248 | tf_op jit(solution)/shard_map/ppermute | solution.py:153
  666.6 11.9 %collective-permute-done.42 = bf16[2,896,128]{2,1,0:T(8,128)(2,1)S(1)} collective-permute-done((bf16[2,896,128]{2,1,0:T(8,128)(2,1)S(1)}, bf16[2,896,128]{2,1,0:T(8,128)(2,1)S(1)}, u32[]{:S(2)}, u32[]{:S(2)}) %collective-permute-start.42) | collective-permute-done | bytes 458784 | tf_op jit(solution)/shard_map/ppermute | solution.py:1304
  (316 shorter events, 212.0 us)
Async XLA Ops:
  7.2 61.4 %all-gather.7.cloned.1.call-start = ((), (), s32[]{:S(2)}) async-start(), calls=%async_computation.8 | async-start | bytes 3620864 | tf_op jit(solution)/shard_map/all_gather | solution.py:1347
  20.4 176.4 %all-gather.9.cloned.1.call-start = ((), (), s32[]{:S(2)}) async-start(), calls=%async_computation.9 | async-start | bytes 22560768 | tf_op jit(solution)/shard_map/all_gather | solution.py:1347
  22.5 25.8 %collective-permute-start.5 = (bf16[4352,128]{1,0:T(8,128)(2,1)S(1)}, bf16[4352,128]{1,0:T(8,128)(2,1)S(1)}, u32[]{:S(2)}, u32[]{:S(2)}) collective-permute-start(bf16[4352,128]{1,0:T(8,128)(2,1)S(1)} %pad_maximum_fusion.9), channel_id=1, source_target_pairs={{0,16},{16,0},{1,17},{17,1},{2,18},{18,2},{3,19},{19,3},{4,20},{20... | collective-permute-start | bytes 3342344 | tf_op jit(solution)/shard_map/ppermute | solution.py:153
  69.7 250.0 %all-gather.11.cloned.1.call-start = ((), (), s32[]{:S(2)}) async-start(), calls=%async_computation.10 | async-start | bytes 18939904 | tf_op jit(solution)/shard_map/all_gather | solution.py:1347
  81.8 19.3 %collective-permute-start.1 = (bf16[256,640]{1,0:T(8,128)(2,1)}, bf16[256,640]{1,0:T(8,128)(2,1)S(1)}, u32[]{:S(2)}, u32[]{:S(2)}) collective-permute-start(bf16[256,640]{1,0:T(8,128)(2,1)} %get-tuple-element.115.refs_0_), channel_id=1, source_target_pairs={{0,2},{2,4},{4,6},{1,3},{3,5},{5,7},{8,10},{10,12},{12,14},{9,11},... | collective-permute-start | bytes 983048 | tf_op jit(solution)/shard_map/ppermute | solution.py:159
  85.7 29.4 %collective-permute-start.2 = (bf16[256,640]{1,0:T(8,128)(2,1)}, bf16[256,640]{1,0:T(8,128)(2,1)S(1)}, u32[]{:S(2)}, u32[]{:S(2)}) collective-permute-start(bf16[256,640]{1,0:T(8,128)(2,1)} %get-tuple-element.115.refs_0_), channel_id=1, source_target_pairs={{0,4},{2,6},{1,5},{3,7},{8,12},{10,14},{9,13},{11,15},{16,20},{18,... | collective-permute-start | bytes 983048 | tf_op jit(solution)/shard_map/ppermute | solution.py:159
  88.8 40.1 %collective-permute-start.3 = (bf16[256,640]{1,0:T(8,128)(2,1)}, bf16[256,640]{1,0:T(8,128)(2,1)S(1)}, u32[]{:S(2)}, u32[]{:S(2)}) collective-permute-start(bf16[256,640]{1,0:T(8,128)(2,1)} %get-tuple-element.115.refs_0_), channel_id=1, source_target_pairs={{0,6},{1,7},{8,14},{9,15},{16,22},{17,23},{24,30},{25,31}} | collective-permute-start | bytes 983048 | tf_op jit(solution)/shard_map/ppermute | solution.py:159
  128.9 363.5 %reduce-scatter.5.cloned.1.call-start = ((), (), s32[]{:S(2)}) async-start(), calls=%async_computation.4 | async-start | bytes 2293760 | tf_op jit(solution)/shard_map/reduce_scatter | solution.py:1291
  216.1 26.1 %collective-permute-start.6 = (bf16[256,640]{1,0:T(8,128)(2,1)}, bf16[256,640]{1,0:T(8,128)(2,1)S(1)}, u32[]{:S(2)}, u32[]{:S(2)}) collective-permute-start(bf16[256,640]{1,0:T(8,128)(2,1)} %get-tuple-element.125.refs_0_), channel_id=1, source_target_pairs={{0,2},{2,4},{4,6},{1,3},{3,5},{5,7},{8,10},{10,12},{12,14},{9,11},... | collective-permute-start | bytes 983048 | tf_op jit(solution)/shard_map/ppermute | solution.py:159
  226.8 29.4 %collective-permute-start.7 = (bf16[256,640]{1,0:T(8,128)(2,1)}, bf16[256,640]{1,0:T(8,128)(2,1)S(1)}, u32[]{:S(2)}, u32[]{:S(2)}) collective-permute-start(bf16[256,640]{1,0:T(8,128)(2,1)} %get-tuple-element.125.refs_0_), channel_id=1, source_target_pairs={{0,4},{2,6},{1,5},{3,7},{8,12},{10,14},{9,13},{11,15},{16,20},{18,... | collective-permute-start | bytes 983048 | tf_op jit(solution)/shard_map/ppermute | solution.py:159
  232.3 37.6 %collective-permute-start.8 = (bf16[256,640]{1,0:T(8,128)(2,1)}, bf16[256,640]{1,0:T(8,128)(2,1)S(1)}, u32[]{:S(2)}, u32[]{:S(2)}) collective-permute-start(bf16[256,640]{1,0:T(8,128)(2,1)} %get-tuple-element.125.refs_0_), channel_id=1, source_target_pairs={{0,6},{1,7},{8,14},{9,15},{16,22},{17,23},{24,30},{25,31}} | collective-permute-start | bytes 983048 | tf_op jit(solution)/shard_map/ppermute | solution.py:159
  363.0 43.7 %collective-permute-start.15 = (bf16[8,640,128]{2,1,0:T(8,128)(2,1)}, bf16[8,640,128]{2,1,0:T(8,128)(2,1)S(1)}, u32[]{:S(2)}, u32[]{:S(2)}) collective-permute-start(bf16[8,640,128]{2,1,0:T(8,128)(2,1)} %get-tuple-element.143), channel_id=1, source_target_pairs={{0,16},{16,0},{1,17},{17,1},{2,18},{18,2},{3,19},{19,3},{4,20},{20... | collective-permute-start | bytes 3932168 | tf_op jit(solution)/shard_map/ppermute | solution.py:153
  365.7 22.8 %collective-permute-start.13 = (bf16[256,640]{1,0:T(8,128)(2,1)S(1)}, bf16[256,640]{1,0:T(8,128)(2,1)S(1)}, u32[]{:S(2)}, u32[]{:S(2)}) collective-permute-start(bf16[256,640]{1,0:T(8,128)(2,1)S(1)} %get-tuple-element.142), channel_id=1, source_target_pairs={{2,0},{4,2},{6,4},{3,1},{5,3},{7,5},{10,8},{12,10},{14,12},{11,9},... | collective-permute-start | bytes 983048 | tf_op jit(solution)/shard_map/ppermute | solution.py:159
  367.4 39.3 %collective-permute-start.16 = (bf16[4,960,128]{2,1,0:T(8,128)(2,1)S(1)}, bf16[4,960,128]{2,1,0:T(8,128)(2,1)S(1)}, u32[]{:S(2)}, u32[]{:S(2)}) collective-permute-start(bf16[4,960,128]{2,1,0:T(8,128)(2,1)S(1)} %copy-done.43), channel_id=1, source_target_pairs={{0,8},{8,0},{1,9},{9,1},{2,10},{10,2},{3,11},{11,3},{4,12},{12,4},... | collective-permute-start | bytes 2949128 | tf_op jit(solution)/shard_map/ppermute | solution.py:153
  408.0 31.3 %collective-permute-start.18 = (bf16[8,640,128]{2,1,0:T(8,128)(2,1)}, bf16[8,640,128]{2,1,0:T(8,128)(2,1)}, u32[]{:S(2)}, u32[]{:S(2)}) collective-permute-start(bf16[8,640,128]{2,1,0:T(8,128)(2,1)} %get-tuple-element.149), channel_id=1, source_target_pairs={{0,16},{16,0},{1,17},{17,1},{2,18},{18,2},{3,19},{19,3},{4,20},{20... | collective-permute-start | bytes 3932168 | tf_op jit(solution)/shard_map/ppermute | solution.py:153
  408.7 29.8 %collective-permute-start.19 = (bf16[4,832,128]{2,1,0:T(8,128)(2,1)}, bf16[4,832,128]{2,1,0:T(8,128)(2,1)S(1)}, u32[]{:S(2)}, u32[]{:S(2)}) collective-permute-start(bf16[4,832,128]{2,1,0:T(8,128)(2,1)} %get-tuple-element.150), channel_id=1, source_target_pairs={{0,8},{8,0},{1,9},{9,1},{2,10},{10,2},{3,11},{11,3},{4,12},{12,4},... | collective-permute-start | bytes 2555912 | tf_op jit(solution)/shard_map/ppermute | solution.py:153
  441.8 25.0 %collective-permute-start.23 = (bf16[272,640]{1,0:T(8,128)(2,1)}, bf16[272,640]{1,0:T(8,128)(2,1)}, u32[]{:S(2)}, u32[]{:S(2)}) collective-permute-start(bf16[272,640]{1,0:T(8,128)(2,1)} %get-tuple-element.157.refs_2_), channel_id=1, source_target_pairs={{0,1},{1,0},{2,3},{3,2},{4,5},{5,4},{6,7},{7,6},{8,9},{9,8},{10,11... | collective-permute-start | bytes 1044488 | tf_op jit(solution)/shard_map/ppermute | solution.py:153
  445.0 139.3 %reduce-scatter.7.cloned.1.call-start = ((), (), s32[]{:S(2)}) async-start(), calls=%async_computation.5 | async-start | bytes 1638400 | tf_op jit(solution)/shard_map/reduce_scatter | solution.py:1291
  448.9 46.0 %collective-permute-start.27 = (bf16[4,640,128]{2,1,0:T(8,128)(2,1)}, bf16[4,640,128]{2,1,0:T(8,128)(2,1)}, u32[]{:S(2)}, u32[]{:S(2)}) collective-permute-start(bf16[4,640,128]{2,1,0:T(8,128)(2,1)} %get-tuple-element.226), channel_id=1, source_target_pairs={{0,8},{8,0},{1,9},{9,1},{2,10},{10,2},{3,11},{11,3},{4,12},{12,4},... | collective-permute-start | bytes 1966088 | tf_op jit(solution)/shard_map/ppermute | solution.py:153
  451.9 43.1 %collective-permute-start.26 = (bf16[4,640,128]{2,1,0:T(8,128)(2,1)}, bf16[4,640,128]{2,1,0:T(8,128)(2,1)}, u32[]{:S(2)}, u32[]{:S(2)}) collective-permute-start(bf16[4,640,128]{2,1,0:T(8,128)(2,1)} %get-tuple-element.224), channel_id=1, source_target_pairs={{0,8},{8,0},{1,9},{9,1},{2,10},{10,2},{3,11},{11,3},{4,12},{12,4},... | collective-permute-start | bytes 1966088 | tf_op jit(solution)/shard_map/ppermute | solution.py:153
  452.9 18.7 %collective-permute-start.20 = (bf16[256,1024]{1,0:T(8,128)(2,1)S(1)}, bf16[256,1024]{1,0:T(8,128)(2,1)S(1)}, u32[]{:S(2)}, u32[]{:S(2)}) collective-permute-start(bf16[256,1024]{1,0:T(8,128)(2,1)S(1)} %copy-done.22), channel_id=1, source_target_pairs={{0,16},{16,0},{1,17},{17,1},{2,18},{18,2},{3,19},{19,3},{4,20},{20... | collective-permute-start | bytes 1572872 | tf_op jit(solution)/shard_map/ppermute | solution.py:153
  464.8 36.5 %collective-permute-start.25 = (bf16[4,960,128]{2,1,0:T(8,128)(2,1)}, bf16[4,960,128]{2,1,0:T(8,128)(2,1)}, u32[]{:S(2)}, u32[]{:S(2)}) collective-permute-start(bf16[4,960,128]{2,1,0:T(8,128)(2,1)} %get-tuple-element.162), channel_id=1, source_target_pairs={{0,8},{8,0},{1,9},{9,1},{2,10},{10,2},{3,11},{11,3},{4,12},{12,4},... | collective-permute-start | bytes 2949128 | tf_op jit(solution)/shard_map/ppermute | solution.py:153
  471.6 30.0 %collective-permute-start.24 = (bf16[8,640,128]{2,1,0:T(8,128)(2,1)S(1)}, bf16[8,640,128]{2,1,0:T(8,128)(2,1)}, u32[]{:S(2)}, u32[]{:S(2)}) collective-permute-start(bf16[8,640,128]{2,1,0:T(8,128)(2,1)S(1)} %copy-done.42), channel_id=1, source_target_pairs={{0,16},{16,0},{1,17},{17,1},{2,18},{18,2},{3,19},{19,3},{4,20},{20... | collective-permute-start | bytes 3932168 | tf_op jit(solution)/shard_map/ppermute | solution.py:153
  504.4 54.5 %collective-permute-start.32 = (bf16[4,1728,128]{2,1,0:T(8,128)(2,1)}, bf16[4,1728,128]{2,1,0:T(8,128)(2,1)}, u32[]{:S(2)}, u32[]{:S(2)}) collective-permute-start(bf16[4,1728,128]{2,1,0:T(8,128)(2,1)} %pad_maximum_fusion.2), channel_id=1, source_target_pairs={{0,8},{8,0},{1,9},{9,1},{2,10},{10,2},{3,11},{11,3},{4,12},{12,4},... | collective-permute-start | bytes 5308424 | tf_op jit(solution)/shard_map/ppermute | solution.py:153
  505.7 53.2 %collective-permute-start.31 = (bf16[8,640,128]{2,1,0:T(8,128)(2,1)}, bf16[8,640,128]{2,1,0:T(8,128)(2,1)}, u32[]{:S(2)}, u32[]{:S(2)}) collective-permute-start(bf16[8,640,128]{2,1,0:T(8,128)(2,1)} %get-tuple-element.178), channel_id=1, source_target_pairs={{0,16},{16,0},{1,17},{17,1},{2,18},{18,2},{3,19},{19,3},{4,20},{20... | collective-permute-start | bytes 3932168 | tf_op jit(solution)/shard_map/ppermute | solution.py:153
  510.4 113.4 %reduce-scatter.9.cloned.1.call-start = ((), (), s32[]{:S(2)}) async-start(), calls=%async_computation.6 | async-start | bytes 3440640 | tf_op jit(solution)/shard_map/reduce_scatter | solution.py:1291
  511.9 29.4 %collective-permute-start.29 = (bf16[256,640]{1,0:T(8,128)(2,1)S(1)}, bf16[256,640]{1,0:T(8,128)(2,1)S(1)}, u32[]{:S(2)}, u32[]{:S(2)}) collective-permute-start(bf16[256,640]{1,0:T(8,128)(2,1)S(1)} %get-tuple-element.218), channel_id=1, source_target_pairs={{2,0},{4,2},{6,4},{3,1},{5,3},{7,5},{10,8},{12,10},{14,12},{11,9},... | collective-permute-start | bytes 983048 | tf_op jit(solution)/shard_map/ppermute | solution.py:159
  564.1 100.1 %reduce-scatter.11.cloned.1.call-start = ((), (), s32[]{:S(2)}) async-start(), calls=%async_computation.7 | async-start | bytes 1638400 | tf_op jit(solution)/shard_map/reduce_scatter | solution.py:1291
  578.3 26.4 %collective-permute-start.35 = (bf16[256,640]{1,0:T(8,128)(2,1)}, bf16[256,640]{1,0:T(8,128)(2,1)S(1)}, u32[]{:S(2)}, u32[]{:S(2)}) collective-permute-start(bf16[256,640]{1,0:T(8,128)(2,1)} %fusion.4), channel_id=1, source_target_pairs={{2,0},{4,2},{6,4},{3,1},{5,3},{7,5},{10,8},{12,10},{14,12},{11,9},... | collective-permute-start | bytes 983048 | tf_op jit(solution)/shard_map/ppermute | solution.py:159
  626.6 19.1 %collective-permute-start.37 = (bf16[1280,128]{1,0:T(8,128)(2,1)S(1)}, bf16[1280,128]{1,0:T(8,128)(2,1)S(1)}, u32[]{:S(2)}, u32[]{:S(2)}) collective-permute-start(bf16[1280,128]{1,0:T(8,128)(2,1)S(1)} %pad_maximum_fusion.12.refs_2_), channel_id=1, source_target_pairs={{0,16},{1,17},{2,18},{3,19},{4,20},{5,21},{6,22},{7,23},{8,24},{9,... | collective-permute-start | bytes 983048 | tf_op jit(solution)/shard_map/ppermute | solution.py:1309
  630.0 25.1 %collective-permute-start.39 = (bf16[4,512,128]{2,1,0:T(8,128)(2,1)S(1)}, bf16[4,512,128]{2,1,0:T(8,128)(2,1)S(1)}, u32[]{:S(2)}, u32[]{:S(2)}) collective-permute-start(bf16[4,512,128]{2,1,0:T(8,128)(2,1)S(1)} %copy-done.45), channel_id=1, source_target_pairs={{0,8},{8,0},{1,9},{9,1},{2,10},{10,2},{3,11},{11,3},{4,12},{12,4},... | collective-permute-start | bytes 1572872 | tf_op jit(solution)/shard_map/ppermute | solution.py:153
  655.4 23.0 %collective-permute-start.42 = (bf16[2,896,128]{2,1,0:T(8,128)(2,1)S(1)}, bf16[2,896,128]{2,1,0:T(8,128)(2,1)S(1)}, u32[]{:S(2)}, u32[]{:S(2)}) collective-permute-start(bf16[2,896,128]{2,1,0:T(8,128)(2,1)S(1)} %dynamic-slice_bitcast_fusion.8), channel_id=1, source_target_pairs={{0,4},{2,6},{4,0},{6,2},{1,5},{3,7},{5,1},{7,3},{8,12},{10,14},{12... | collective-permute-start | bytes 1376264 | tf_op jit(solution)/shard_map/ppermute | solution.py:1304
  (82 other events, 905.8 us)
Sparse Core Ops, SparseCore 0:
  20.5 48.0 all-gather.6
  70.7 126.0 all-gather.8
  198.4 121.2 all-gather.10
  445.2 47.1 reduce-scatter.4
  510.5 50.7 reduce-scatter.6
  564.2 59.5 reduce-scatter.8
  626.6 30.9 reduce-scatter.10

commit v5 on v4

--- a/solution.py
+++ b/solution.py
@@ -1423,7 +1423,8 @@
     grads1 = grad_ffn(place, own1, other1, after(back1, dkv1), back_other1, shards)
     keep_a1, send_a1, keep_u1, send_u1 = grads1[:2], grads1[2:4], grads1[4:6], grads1[6:8]
     got_a1, got_u1 = swap_all(send_a1, "section"), swap_all(send_u1, "dp")
-    shares1, _ = collect_kv(dkv1, got1, [(got_a1[0], got_u1[0]), (), (send_u1[0],)])
+    shares1, _ = collect_kv(dkv1, got1, [(), (), (send_u1[0],)])
+    dq1 = after(dq1, got_a1[0], got_u1[0])
     dkv_low1, dx1_low, back0, dm0, do0, dgf0 = both_back(
         dq1, shares1, cos, sin, y0, w1[4], dm1, dgf1, w1[0], w1[1], mixed0, w0[5], gu0, spread, w0[2], w0[3]
     )

time: 716 us -> 719 us (level)
  transfers between devices with their start and end apart: 56 -> 56, of which waited for: 27 -> 29; matrix products, arithmetic and copies ran while one was open for 9% -> 9% of each run, Pallas kernels for 21% -> 20%
where the time goes in v5:
time: 719 us; the launch traced here: 709 us
  waiting for transfers between devices  364 us (51%)
  Pallas kernels  170 us (24%)
  starting transfers between devices  79.3 us (11%)
  other arithmetic  44.1 us (6%)
  local copies, waits for them, and re-layouts  26.5 us (4%)
  between operations  15.9 us (2%)
  matrix products  8.59 us (1%)
    ppermute x12, waiting for transfers between devices, move_z(): return lax.ppermute(block, 'z', route)  176 us
    all_gather x3, waiting for transfers between devices, gathered(): return lax.all_gather(block, plane, axis=0)  101 us
    ppermute x28, waiting for transfers between devices, swap(): return lax.ppermute(block, axis, [(0, 1), (1, 0)])  50 us
    ppermute x12, starting transfers between devices, move_z(): return lax.ppermute(block, 'z', route)  34.3 us
    ppermute x28, starting transfers between devices, swap(): return lax.ppermute(block, axis, [(0, 1), (1, 0)])  29.6 us
    pallas_call x2, Pallas kernels, grad_ffn(): pl.pallas_call(grad_ffn_kernel, out_shape=[jax.ShapeDtypeStruct(shape, BF...  21.9 us
    pallas_call x2, Pallas kernels, attend(): pl.pallas_call(functools.partial(attend_kernel, zs), out_shape=(jax.Shape...  21.6 us
    pallas_call x1, Pallas kernels, both_back(): pl.pallas_call(functools.partial(both_back_kernel, base, first, len(share...  20.9 us
  transfers between devices with their start and end apart: 56, of which 29 were waited for; matrix products, arithmetic and copies ran while one was open for 9% of the time, Pallas kernels for 20%

profile of v5, /device:TPU:0, one launch (start us, length us, event | category | flops | bytes accessed | tf_op | source)
XLA Modules:
  0.0 708.9 jit_solution(13885284752354913390)
XLA Ops:
  24.3 24.0 %collective-permute-done.5 = bf16[4352,128]{1,0:T(8,128)(2,1)S(1)} collective-permute-done((bf16[4352,128]{1,0:T(8,128)(2,1)S(1)}, bf16[4352,128]{1,0:T(8,128)(2,1)S(1)}, u32[]{:S(2)}, u32[]{:S(2)}) %collective-permute-start.5) | collective-permute-done | bytes 1114144 | tf_op jit(solution)/shard_map/ppermute | solution.py:153
  49.5 19.1 %all-gather.7.cloned.1.call-done = bf16[13312,128]{1,0:T(8,128)(2,1)} async-done(((bf16[832,128]{1,0:T(8,128)(2,1)}), bf16[13312,128]{1,0:T(8,128)(2,1)}) %all-gather.7.cloned.1.call-update) | async-done | bytes 3407888 | tf_op jit(solution)/shard_map/all_gather | solution.py:1347
  75.4 6.4 qkv_forward.2
  90.1 10.9 %collective-permute-done.1.refs_1_ = bf16[256,640]{1,0:T(8,128)(2,1)S(1)} collective-permute-done((bf16[256,640]{1,0:T(8,128)(2,1)}, bf16[256,640]{1,0:T(8,128)(2,1)S(1)}, u32[]{:S(2)}, u32[]{:S(2)}) %collective-permute-start.1) | collective-permute-done | bytes 327712 | tf_op jit(solution)/shard_map/ppermute | solution.py:159
  101.0 14.0 %collective-permute-done.2.refs_2_ = bf16[256,640]{1,0:T(8,128)(2,1)S(1)} collective-permute-done((bf16[256,640]{1,0:T(8,128)(2,1)}, bf16[256,640]{1,0:T(8,128)(2,1)S(1)}, u32[]{:S(2)}, u32[]{:S(2)}) %collective-permute-start.2) | collective-permute-done | bytes 327712 | tf_op jit(solution)/shard_map/ppermute | solution.py:159
  115.1 13.8 %collective-permute-done.3.refs_3_ = bf16[256,640]{1,0:T(8,128)(2,1)S(1)} collective-permute-done((bf16[256,640]{1,0:T(8,128)(2,1)}, bf16[256,640]{1,0:T(8,128)(2,1)S(1)}, u32[]{:S(2)}, u32[]{:S(2)}) %collective-permute-start.3) | collective-permute-done | bytes 327712 | tf_op jit(solution)/shard_map/ppermute | solution.py:159
  133.5 6.6 attend.2
  140.1 56.7 %all-gather.9.cloned.1.call-done = bf16[82944,128]{1,0:T(8,128)(2,1)} async-done(((bf16[5184,128]{1,0:T(8,128)(2,1)}), bf16[82944,128]{1,0:T(8,128)(2,1)}) %all-gather.9.cloned.1.call-update) | async-done | bytes 21233680 | tf_op jit(solution)/shard_map/all_gather | solution.py:1347
  198.8 11.3 %ffn_forward.1 = (bf16[256,5632]{1,0:T(8,128)(2,1)}, f32[256,1024]{1,0:T(8,128)}, bf16[2,256,2560]{2,1,0:T(8,128)(2,1)}, bf16[256,1024]{1,0:T(8,128)(2,1)}) custom-call(bf16[256,1024]{1,0:T(8,128)(2,1)} %get-tuple-element.116.op_ref, bf16[256,1024]{1,0:T(8,128)(2,1)} %convolution_convert_fusion.1.x_ref, bf16[256,1024]{1,0:T(8,128)(2,1)} %get-tuple-element.117.na_ref, ...), custom_call_target="tpu_custom_call" | custom-call | flops 10350000128 | bytes 33210000 | tf_op jit(solution)/shard_map/ffn_forward/pallas_call | solution.py:747
  216.1 10.8 %collective-permute-start.6 = (bf16[256,640]{1,0:T(8,128)(2,1)}, bf16[256,640]{1,0:T(8,128)(2,1)S(1)}, u32[]{:S(2)}, u32[]{:S(2)}) collective-permute-start(bf16[256,640]{1,0:T(8,128)(2,1)} %get-tuple-element.125.refs_0_), channel_id=1, source_target_pairs={{0,2},{2,4},{4,6},{1,3},{3,5},{5,7},{8,10},{10,12},{12,14},{9,11},... | collective-permute-start | bytes 983048 | tf_op jit(solution)/shard_map/ppermute | solution.py:159
  233.6 8.6 %collective-permute-done.6.refs_1_ = bf16[256,640]{1,0:T(8,128)(2,1)S(1)} collective-permute-done((bf16[256,640]{1,0:T(8,128)(2,1)}, bf16[256,640]{1,0:T(8,128)(2,1)S(1)}, u32[]{:S(2)}, u32[]{:S(2)}) %collective-permute-start.6) | collective-permute-done | bytes 327712 | tf_op jit(solution)/shard_map/ppermute | solution.py:159
  242.2 14.0 %collective-permute-done.7.refs_2_ = bf16[256,640]{1,0:T(8,128)(2,1)S(1)} collective-permute-done((bf16[256,640]{1,0:T(8,128)(2,1)}, bf16[256,640]{1,0:T(8,128)(2,1)S(1)}, u32[]{:S(2)}, u32[]{:S(2)}) %collective-permute-start.7) | collective-permute-done | bytes 327712 | tf_op jit(solution)/shard_map/ppermute | solution.py:159
  256.3 13.6 %collective-permute-done.8.refs_3_ = bf16[256,640]{1,0:T(8,128)(2,1)S(1)} collective-permute-done((bf16[256,640]{1,0:T(8,128)(2,1)}, bf16[256,640]{1,0:T(8,128)(2,1)S(1)}, u32[]{:S(2)}, u32[]{:S(2)}) %collective-permute-start.8) | collective-permute-done | bytes 327712 | tf_op jit(solution)/shard_map/ppermute | solution.py:159
  279.5 15.1 %attend.3 = (bf16[256,960]{1,0:T(8,128)(2,1)}, bf16[256,1024]{1,0:T(8,128)(2,1)}, f32[5,768]{1,0:T(8,128)}) custom-call(s32[2]{0:T(128)} %pad_add_fusion.1.rng, bf16[256,960]{1,0:T(8,128)(2,1)} %get-tuple-element.124.q_ref, bf16[256,640]{1,0:T(8,128)(2,1)} %get-tuple-element.125.refs_0_, bf16[256,640]{1,0:T(8,128)(2,1)} %copy-done.28, ...), custom_call_target="tpu_custom_call" | custom-call | flops 27599998976 | bytes 88560000 | tf_op jit(solution)/shard_map/attend/pallas_call | solution.py:462
  294.6 25.1 %all-gather.11.cloned.1.call-done = bf16[69632,128]{1,0:T(8,128)(2,1)} async-done(((bf16[4352,128]{1,0:T(8,128)(2,1)}), bf16[69632,128]{1,0:T(8,128)(2,1)}) %all-gather.11.cloned.1.call-update) | async-done | bytes 17825808 | tf_op jit(solution)/shard_map/all_gather | solution.py:1347
  319.7 18.8 %ffn_both.1 = (bf16[256,1024]{1,0:T(8,128)(2,1)}, bf16[2816,256]{1,0:T(8,128)(2,1)}, bf16[2816,256]{1,0:T(8,128)(2,1)}, bf16[256,7168]{1,0:T(8,128)(2,1)}, f32[2...) custom-call(s32[3]{0:T(128)} %pad_add_fusion.place, bf16[256,1024]{1,0:T(8,128)(2,1)} %get-tuple-element.126.op_ref, ...), custom_call_target="tpu_custom_call" | custom-call | flops 23000000512 | bytes 73800000 | tf_op jit(solution)/shard_map/ffn_both/pallas_call | solution.py:842
  338.6 8.5 %attend_back.2 = (bf16[256,1024]{1,0:T(8,128)(2,1)}, bf16[4,256,640]{2,1,0:T(8,128)(2,1)}, bf16[6,256,640]{2,1,0:T(8,128)(2,1)}) custom-call(s32[2]{0:T(128)} %pad_add_fusion.1.rng, bf16[256,960]{1,0:T(8,128)(2,1)} %get-tuple-element.124.q_ref, bf16[256,960]{1,0:T(8,128)(2,1)} %get-tuple-element.130.o_ref, bf16[256,960]{1,0:T(8,128)(2,1)} %get-tuple-element.131.do_ref, ...), custom_call_target="tpu_custom_call" | custom-call | flops 27599998976 | bytes 88560000 | tf_op jit(solution)/shard_map/attend_back/pallas_call | solution.py:575
  358.2 11.0 %grad_ffn.2 = (bf16[8,640,128]{2,1,0:T(8,128)(2,1)}, bf16[8,640,128]{2,1,0:T(8,128)(2,1)}, bf16[8,640,128]{2,1,0:T(8,128)(2,1)}, bf16[8,640,128]{2,1,0:T(8,128)(...) custom-call(s32[3]{0:T(128)} %pad_add_fusion.place, ...), custom_call_target="tpu_custom_call" | custom-call | flops 12650000384 | bytes 40590000 | tf_op jit(solution)/shard_map/grad_ffn/pallas_call | solution.py:1101
  374.2 18.7 %collective-permute-done.15 = bf16[256,640]{1,0:T(8,128)(2,1)S(1)} collective-permute-done((bf16[256,640]{1,0:T(8,128)(2,1)S(1)}, bf16[256,640]{1,0:T(8,128)(2,1)S(1)}, u32[]{:S(2)}, u32[]{:S(2)}) %collective-permute-start.15) | collective-permute-done | bytes 327712 | tf_op jit(solution)/shard_map/ppermute | solution.py:159
  394.4 17.1 %collective-permute-done.16 = bf16[256,640]{1,0:T(8,128)(2,1)S(1)} collective-permute-done((bf16[256,640]{1,0:T(8,128)(2,1)S(1)}, bf16[256,640]{1,0:T(8,128)(2,1)S(1)}, u32[]{:S(2)}, u32[]{:S(2)}) %collective-permute-start.16) | collective-permute-done | bytes 327712 | tf_op jit(solution)/shard_map/ppermute | solution.py:159
  416.1 6.2 collective-permute-done.17.refs_1_
  423.1 20.9 %both_back.1 = (bf16[272,640]{1,0:T(8,128)(2,1)}, bf16[256,1024]{1,0:T(8,128)(2,1)}, bf16[256,7168]{1,0:T(8,128)(2,1)}, f32[256,1024]{1,0:T(8,128)}, bf16[256,960]{1,0:T(8,128)(2,1)}, /*index=5*/f32[1,1024]{1,0:T(1,128)}) custom-call(bf16[256,1024]{1,0:T(8,128)(2,1)} %get-tuple-element.141.dq_ref.refs_0_, f32[256,128]{1,0:T(8,128)} %get-tuple-element.251.cos_ref, ...), custom_call_target="tpu_custom_call" | custom-call | flops 20700000256 | bytes 66420000 | tf_op jit(solution)/shard_map/both_back/pallas_call | solution.py:898
  459.9 10.9 %grad_ffn.3 = (bf16[8,640,128]{2,1,0:T(8,128)(2,1)}, bf16[8,640,128]{2,1,0:T(8,128)(2,1)}, bf16[8,640,128]{2,1,0:T(8,128)(2,1)}, bf16[8,640,128]{2,1,0:T(8,128)(...) custom-call(s32[3]{0:T(128)} %pad_add_fusion.place, ...), custom_call_target="tpu_custom_call" | custom-call | flops 12650000384 | bytes 40590000 | tf_op jit(solution)/shard_map/grad_ffn/pallas_call | solution.py:1101
  478.4 8.8 %attend_back.3 = (bf16[256,1024]{1,0:T(8,128)(2,1)}, bf16[4,256,640]{2,1,0:T(8,128)(2,1)}, bf16[6,256,640]{2,1,0:T(8,128)(2,1)}) custom-call(s32[2]{0:T(128)} %pad_add_fusion.1.rng, bf16[256,960]{1,0:T(8,128)(2,1)} %get-tuple-element.114.q_ref, bf16[256,960]{1,0:T(8,128)(2,1)} %get-tuple-element.153.o_ref, bf16[256,960]{1,0:T(8,128)(2,1)} %get-tuple-element.165.do_ref, ...), custom_call_target="tpu_custom_call" | custom-call | flops 27599998976 | bytes 88560000 | tf_op jit(solution)/shard_map/attend_back/pallas_call | solution.py:575
  487.2 9.9 %reduce-scatter.5.cloned.1.call-done = bf16[1,1792,128]{2,1,0:T(8,128)(2,1)} async-done(((bf16[4,1792,128]{2,1,0:T(8,128)(2,1)}), bf16[1,1792,128]{2,1,0:T(8,128)(2,1)}) %reduce-scatter.5.cloned.1.call-update) | async-done | bytes 458768 | tf_op jit(solution)/shard_map/reduce_scatter | solution.py:1291
  499.7 7.1 %collective-permute-done.25 = bf16[4,960,128]{2,1,0:T(8,128)(2,1)} collective-permute-done((bf16[4,960,128]{2,1,0:T(8,128)(2,1)}, bf16[4,960,128]{2,1,0:T(8,128)(2,1)}, u32[]{:S(2)}, u32[]{:S(2)}) %collective-permute-start.25) | collective-permute-done | bytes 983072 | tf_op jit(solution)/shard_map/ppermute | solution.py:153
  519.2 10.2 %collective-permute-done.29 = bf16[256,640]{1,0:T(8,128)(2,1)S(1)} collective-permute-done((bf16[256,640]{1,0:T(8,128)(2,1)S(1)}, bf16[256,640]{1,0:T(8,128)(2,1)S(1)}, u32[]{:S(2)}, u32[]{:S(2)}) %collective-permute-start.29) | collective-permute-done | bytes 327712 | tf_op jit(solution)/shard_map/ppermute | solution.py:159
  531.0 28.4 %collective-permute-done.30 = bf16[256,640]{1,0:T(8,128)(2,1)S(1)} collective-permute-done((bf16[256,640]{1,0:T(8,128)(2,1)S(1)}, bf16[256,640]{1,0:T(8,128)(2,1)S(1)}, u32[]{:S(2)}, u32[]{:S(2)}) %collective-permute-start.30) | collective-permute-done | bytes 327712 | tf_op jit(solution)/shard_map/ppermute | solution.py:159
  587.7 20.7 %collective-permute-done.35.refs_1_ = bf16[256,640]{1,0:T(8,128)(2,1)S(1)} collective-permute-done((bf16[256,640]{1,0:T(8,128)(2,1)}, bf16[256,640]{1,0:T(8,128)(2,1)S(1)}, u32[]{:S(2)}, u32[]{:S(2)}) %collective-permute-start.35) | collective-permute-done | bytes 327712 | tf_op jit(solution)/shard_map/ppermute | solution.py:159
  610.8 6.5 qkv_backward.1
  649.0 8.2 %collective-permute-done.41 = bf16[4,384,128]{2,1,0:T(8,128)(2,1)S(1)} collective-permute-done((bf16[4,384,128]{2,1,0:T(8,128)(2,1)}, bf16[4,384,128]{2,1,0:T(8,128)(2,1)S(1)}, u32[]{:S(2)}, u32[]{:S(2)}) %collective-permute-start.41) | collective-permute-done | bytes 393248 | tf_op jit(solution)/shard_map/ppermute | solution.py:153
  669.8 11.9 %collective-permute-done.42 = bf16[2,896,128]{2,1,0:T(8,128)(2,1)S(1)} collective-permute-done((bf16[2,896,128]{2,1,0:T(8,128)(2,1)S(1)}, bf16[2,896,128]{2,1,0:T(8,128)(2,1)S(1)}, u32[]{:S(2)}, u32[]{:S(2)}) %collective-permute-start.42) | collective-permute-done | bytes 458784 | tf_op jit(solution)/shard_map/ppermute | solution.py:1304
  (316 shorter events, 219.2 us)
Async XLA Ops:
  7.2 61.4 %all-gather.7.cloned.1.call-start = ((), (), s32[]{:S(2)}) async-start(), calls=%async_computation.8 | async-start | bytes 3620864 | tf_op jit(solution)/shard_map/all_gather | solution.py:1347
  20.4 176.4 %all-gather.9.cloned.1.call-start = ((), (), s32[]{:S(2)}) async-start(), calls=%async_computation.9 | async-start | bytes 22560768 | tf_op jit(solution)/shard_map/all_gather | solution.py:1347
  22.5 25.8 %collective-permute-start.5 = (bf16[4352,128]{1,0:T(8,128)(2,1)S(1)}, bf16[4352,128]{1,0:T(8,128)(2,1)S(1)}, u32[]{:S(2)}, u32[]{:S(2)}) collective-permute-start(bf16[4352,128]{1,0:T(8,128)(2,1)S(1)} %pad_maximum_fusion.9), channel_id=1, source_target_pairs={{0,16},{16,0},{1,17},{17,1},{2,18},{18,2},{3,19},{19,3},{4,20},{20... | collective-permute-start | bytes 3342344 | tf_op jit(solution)/shard_map/ppermute | solution.py:153
  69.7 250.0 %all-gather.11.cloned.1.call-start = ((), (), s32[]{:S(2)}) async-start(), calls=%async_computation.10 | async-start | bytes 18939904 | tf_op jit(solution)/shard_map/all_gather | solution.py:1347
  81.8 19.3 %collective-permute-start.1 = (bf16[256,640]{1,0:T(8,128)(2,1)}, bf16[256,640]{1,0:T(8,128)(2,1)S(1)}, u32[]{:S(2)}, u32[]{:S(2)}) collective-permute-start(bf16[256,640]{1,0:T(8,128)(2,1)} %get-tuple-element.115.refs_0_), channel_id=1, source_target_pairs={{0,2},{2,4},{4,6},{1,3},{3,5},{5,7},{8,10},{10,12},{12,14},{9,11},... | collective-permute-start | bytes 983048 | tf_op jit(solution)/shard_map/ppermute | solution.py:159
  85.7 29.4 %collective-permute-start.2 = (bf16[256,640]{1,0:T(8,128)(2,1)}, bf16[256,640]{1,0:T(8,128)(2,1)S(1)}, u32[]{:S(2)}, u32[]{:S(2)}) collective-permute-start(bf16[256,640]{1,0:T(8,128)(2,1)} %get-tuple-element.115.refs_0_), channel_id=1, source_target_pairs={{0,4},{2,6},{1,5},{3,7},{8,12},{10,14},{9,13},{11,15},{16,20},{18,... | collective-permute-start | bytes 983048 | tf_op jit(solution)/shard_map/ppermute | solution.py:159
  88.8 40.1 %collective-permute-start.3 = (bf16[256,640]{1,0:T(8,128)(2,1)}, bf16[256,640]{1,0:T(8,128)(2,1)S(1)}, u32[]{:S(2)}, u32[]{:S(2)}) collective-permute-start(bf16[256,640]{1,0:T(8,128)(2,1)} %get-tuple-element.115.refs_0_), channel_id=1, source_target_pairs={{0,6},{1,7},{8,14},{9,15},{16,22},{17,23},{24,30},{25,31}} | collective-permute-start | bytes 983048 | tf_op jit(solution)/shard_map/ppermute | solution.py:159
  128.9 368.2 %reduce-scatter.5.cloned.1.call-start = ((), (), s32[]{:S(2)}) async-start(), calls=%async_computation.4 | async-start | bytes 2293760 | tf_op jit(solution)/shard_map/reduce_scatter | solution.py:1291
  216.1 26.1 %collective-permute-start.6 = (bf16[256,640]{1,0:T(8,128)(2,1)}, bf16[256,640]{1,0:T(8,128)(2,1)S(1)}, u32[]{:S(2)}, u32[]{:S(2)}) collective-permute-start(bf16[256,640]{1,0:T(8,128)(2,1)} %get-tuple-element.125.refs_0_), channel_id=1, source_target_pairs={{0,2},{2,4},{4,6},{1,3},{3,5},{5,7},{8,10},{10,12},{12,14},{9,11},... | collective-permute-start | bytes 983048 | tf_op jit(solution)/shard_map/ppermute | solution.py:159
  226.8 29.4 %collective-permute-start.7 = (bf16[256,640]{1,0:T(8,128)(2,1)}, bf16[256,640]{1,0:T(8,128)(2,1)S(1)}, u32[]{:S(2)}, u32[]{:S(2)}) collective-permute-start(bf16[256,640]{1,0:T(8,128)(2,1)} %get-tuple-element.125.refs_0_), channel_id=1, source_target_pairs={{0,4},{2,6},{1,5},{3,7},{8,12},{10,14},{9,13},{11,15},{16,20},{18,... | collective-permute-start | bytes 983048 | tf_op jit(solution)/shard_map/ppermute | solution.py:159
  232.3 37.6 %collective-permute-start.8 = (bf16[256,640]{1,0:T(8,128)(2,1)}, bf16[256,640]{1,0:T(8,128)(2,1)S(1)}, u32[]{:S(2)}, u32[]{:S(2)}) collective-permute-start(bf16[256,640]{1,0:T(8,128)(2,1)} %get-tuple-element.125.refs_0_), channel_id=1, source_target_pairs={{0,6},{1,7},{8,14},{9,15},{16,22},{17,23},{24,30},{25,31}} | collective-permute-start | bytes 983048 | tf_op jit(solution)/shard_map/ppermute | solution.py:159
  369.3 23.7 %collective-permute-start.15 = (bf16[256,640]{1,0:T(8,128)(2,1)S(1)}, bf16[256,640]{1,0:T(8,128)(2,1)S(1)}, u32[]{:S(2)}, u32[]{:S(2)}) collective-permute-start(bf16[256,640]{1,0:T(8,128)(2,1)S(1)} %get-tuple-element.144), channel_id=1, source_target_pairs={{2,0},{4,2},{6,4},{3,1},{5,3},{7,5},{10,8},{12,10},{14,12},{11,9},... | collective-permute-start | bytes 983048 | tf_op jit(solution)/shard_map/ppermute | solution.py:159
  371.0 45.1 %collective-permute-start.12 = (bf16[8,640,128]{2,1,0:T(8,128)(2,1)}, bf16[8,640,128]{2,1,0:T(8,128)(2,1)S(1)}, u32[]{:S(2)}, u32[]{:S(2)}) collective-permute-start(bf16[8,640,128]{2,1,0:T(8,128)(2,1)} %get-tuple-element.139), channel_id=1, source_target_pairs={{0,16},{16,0},{1,17},{17,1},{2,18},{18,2},{3,19},{19,3},{4,20},{20... | collective-permute-start | bytes 3932168 | tf_op jit(solution)/shard_map/ppermute | solution.py:153
  372.7 43.3 %collective-permute-start.13 = (bf16[4,960,128]{2,1,0:T(8,128)(2,1)}, bf16[4,960,128]{2,1,0:T(8,128)(2,1)S(1)}, u32[]{:S(2)}, u32[]{:S(2)}) collective-permute-start(bf16[4,960,128]{2,1,0:T(8,128)(2,1)} %get-tuple-element.140), channel_id=1, source_target_pairs={{0,8},{8,0},{1,9},{9,1},{2,10},{10,2},{3,11},{11,3},{4,12},{12,4},... | collective-permute-start | bytes 2949128 | tf_op jit(solution)/shard_map/ppermute | solution.py:153
  412.9 32.0 %collective-permute-start.18 = (bf16[8,640,128]{2,1,0:T(8,128)(2,1)}, bf16[8,640,128]{2,1,0:T(8,128)(2,1)}, u32[]{:S(2)}, u32[]{:S(2)}) collective-permute-start(bf16[8,640,128]{2,1,0:T(8,128)(2,1)} %get-tuple-element.149), channel_id=1, source_target_pairs={{0,16},{16,0},{1,17},{17,1},{2,18},{18,2},{3,19},{19,3},{4,20},{20... | collective-permute-start | bytes 3932168 | tf_op jit(solution)/shard_map/ppermute | solution.py:153
  414.4 29.5 %collective-permute-start.19 = (bf16[4,832,128]{2,1,0:T(8,128)(2,1)}, bf16[4,832,128]{2,1,0:T(8,128)(2,1)S(1)}, u32[]{:S(2)}, u32[]{:S(2)}) collective-permute-start(bf16[4,832,128]{2,1,0:T(8,128)(2,1)} %get-tuple-element.150), channel_id=1, source_target_pairs={{0,8},{8,0},{1,9},{9,1},{2,10},{10,2},{3,11},{11,3},{4,12},{12,4},... | collective-permute-start | bytes 2555912 | tf_op jit(solution)/shard_map/ppermute | solution.py:153
  447.3 25.6 %collective-permute-start.23 = (bf16[272,640]{1,0:T(8,128)(2,1)}, bf16[272,640]{1,0:T(8,128)(2,1)}, u32[]{:S(2)}, u32[]{:S(2)}) collective-permute-start(bf16[272,640]{1,0:T(8,128)(2,1)} %get-tuple-element.157.refs_2_), channel_id=1, source_target_pairs={{0,1},{1,0},{2,3},{3,2},{4,5},{5,4},{6,7},{7,6},{8,9},{9,8},{10,11... | collective-permute-start | bytes 1044488 | tf_op jit(solution)/shard_map/ppermute | solution.py:153
  450.6 136.1 %reduce-scatter.7.cloned.1.call-start = ((), (), s32[]{:S(2)}) async-start(), calls=%async_computation.5 | async-start | bytes 1638400 | tf_op jit(solution)/shard_map/reduce_scatter | solution.py:1291
  454.5 45.2 %collective-permute-start.27 = (bf16[4,640,128]{2,1,0:T(8,128)(2,1)}, bf16[4,640,128]{2,1,0:T(8,128)(2,1)}, u32[]{:S(2)}, u32[]{:S(2)}) collective-permute-start(bf16[4,640,128]{2,1,0:T(8,128)(2,1)} %get-tuple-element.226), channel_id=1, source_target_pairs={{0,8},{8,0},{1,9},{9,1},{2,10},{10,2},{3,11},{11,3},{4,12},{12,4},... | collective-permute-start | bytes 1966088 | tf_op jit(solution)/shard_map/ppermute | solution.py:153
  457.5 42.3 %collective-permute-start.26 = (bf16[4,640,128]{2,1,0:T(8,128)(2,1)}, bf16[4,640,128]{2,1,0:T(8,128)(2,1)}, u32[]{:S(2)}, u32[]{:S(2)}) collective-permute-start(bf16[4,640,128]{2,1,0:T(8,128)(2,1)} %get-tuple-element.224), channel_id=1, source_target_pairs={{0,8},{8,0},{1,9},{9,1},{2,10},{10,2},{3,11},{11,3},{4,12},{12,4},... | collective-permute-start | bytes 1966088 | tf_op jit(solution)/shard_map/ppermute | solution.py:153
  458.5 19.2 %collective-permute-start.20 = (bf16[256,1024]{1,0:T(8,128)(2,1)S(1)}, bf16[256,1024]{1,0:T(8,128)(2,1)S(1)}, u32[]{:S(2)}, u32[]{:S(2)}) collective-permute-start(bf16[256,1024]{1,0:T(8,128)(2,1)S(1)} %copy-done.22), channel_id=1, source_target_pairs={{0,16},{16,0},{1,17},{17,1},{2,18},{18,2},{3,19},{19,3},{4,20},{20... | collective-permute-start | bytes 1572872 | tf_op jit(solution)/shard_map/ppermute | solution.py:153
  470.9 36.0 %collective-permute-start.25 = (bf16[4,960,128]{2,1,0:T(8,128)(2,1)}, bf16[4,960,128]{2,1,0:T(8,128)(2,1)}, u32[]{:S(2)}, u32[]{:S(2)}) collective-permute-start(bf16[4,960,128]{2,1,0:T(8,128)(2,1)} %get-tuple-element.162), channel_id=1, source_target_pairs={{0,8},{8,0},{1,9},{9,1},{2,10},{10,2},{3,11},{11,3},{4,12},{12,4},... | collective-permute-start | bytes 2949128 | tf_op jit(solution)/shard_map/ppermute | solution.py:153
  477.6 30.0 %collective-permute-start.24 = (bf16[8,640,128]{2,1,0:T(8,128)(2,1)S(1)}, bf16[8,640,128]{2,1,0:T(8,128)(2,1)}, u32[]{:S(2)}, u32[]{:S(2)}) collective-permute-start(bf16[8,640,128]{2,1,0:T(8,128)(2,1)S(1)} %copy-done.43), channel_id=1, source_target_pairs={{0,16},{16,0},{1,17},{17,1},{2,18},{18,2},{3,19},{19,3},{4,20},{20... | collective-permute-start | bytes 3932168 | tf_op jit(solution)/shard_map/ppermute | solution.py:153
  510.4 49.8 %collective-permute-start.32 = (bf16[4,1728,128]{2,1,0:T(8,128)(2,1)}, bf16[4,1728,128]{2,1,0:T(8,128)(2,1)}, u32[]{:S(2)}, u32[]{:S(2)}) collective-permute-start(bf16[4,1728,128]{2,1,0:T(8,128)(2,1)} %pad_maximum_fusion.2), channel_id=1, source_target_pairs={{0,8},{8,0},{1,9},{9,1},{2,10},{10,2},{3,11},{11,3},{4,12},{12,4},... | collective-permute-start | bytes 5308424 | tf_op jit(solution)/shard_map/ppermute | solution.py:153
  511.7 48.5 %collective-permute-start.31 = (bf16[8,640,128]{2,1,0:T(8,128)(2,1)}, bf16[8,640,128]{2,1,0:T(8,128)(2,1)}, u32[]{:S(2)}, u32[]{:S(2)}) collective-permute-start(bf16[8,640,128]{2,1,0:T(8,128)(2,1)} %get-tuple-element.178), channel_id=1, source_target_pairs={{0,16},{16,0},{1,17},{17,1},{2,18},{18,2},{3,19},{19,3},{4,20},{20... | collective-permute-start | bytes 3932168 | tf_op jit(solution)/shard_map/ppermute | solution.py:153
  516.4 110.7 %reduce-scatter.9.cloned.1.call-start = ((), (), s32[]{:S(2)}) async-start(), calls=%async_computation.6 | async-start | bytes 3440640 | tf_op jit(solution)/shard_map/reduce_scatter | solution.py:1291
  529.5 29.9 %collective-permute-start.30 = (bf16[256,640]{1,0:T(8,128)(2,1)S(1)}, bf16[256,640]{1,0:T(8,128)(2,1)S(1)}, u32[]{:S(2)}, u32[]{:S(2)}) collective-permute-start(bf16[256,640]{1,0:T(8,128)(2,1)S(1)} %fusion.3), channel_id=1, source_target_pairs={{2,0},{4,2},{6,4},{3,1},{5,3},{7,5},{10,8},{12,10},{14,12},{11,9},... | collective-permute-start | bytes 983048 | tf_op jit(solution)/shard_map/ppermute | solution.py:159
  565.4 102.0 %reduce-scatter.11.cloned.1.call-start = ((), (), s32[]{:S(2)}) async-start(), calls=%async_computation.7 | async-start | bytes 1638400 | tf_op jit(solution)/shard_map/reduce_scatter | solution.py:1291
  580.6 27.8 %collective-permute-start.35 = (bf16[256,640]{1,0:T(8,128)(2,1)}, bf16[256,640]{1,0:T(8,128)(2,1)S(1)}, u32[]{:S(2)}, u32[]{:S(2)}) collective-permute-start(bf16[256,640]{1,0:T(8,128)(2,1)} %fusion.4), channel_id=1, source_target_pairs={{2,0},{4,2},{6,4},{3,1},{5,3},{7,5},{10,8},{12,10},{14,12},{11,9},... | collective-permute-start | bytes 983048 | tf_op jit(solution)/shard_map/ppermute | solution.py:159
  629.8 19.1 %collective-permute-start.37 = (bf16[1280,128]{1,0:T(8,128)(2,1)S(1)}, bf16[1280,128]{1,0:T(8,128)(2,1)S(1)}, u32[]{:S(2)}, u32[]{:S(2)}) collective-permute-start(bf16[1280,128]{1,0:T(8,128)(2,1)S(1)} %pad_maximum_fusion.12.refs_2_), channel_id=1, source_target_pairs={{0,16},{1,17},{2,18},{3,19},{4,20},{5,21},{6,22},{7,23},{8,24},{9,... | collective-permute-start | bytes 983048 | tf_op jit(solution)/shard_map/ppermute | solution.py:1309
  633.3 25.1 %collective-permute-start.39 = (bf16[4,512,128]{2,1,0:T(8,128)(2,1)S(1)}, bf16[4,512,128]{2,1,0:T(8,128)(2,1)S(1)}, u32[]{:S(2)}, u32[]{:S(2)}) collective-permute-start(bf16[4,512,128]{2,1,0:T(8,128)(2,1)S(1)} %copy-done.45), channel_id=1, source_target_pairs={{0,8},{8,0},{1,9},{9,1},{2,10},{10,2},{3,11},{11,3},{4,12},{12,4},... | collective-permute-start | bytes 1572872 | tf_op jit(solution)/shard_map/ppermute | solution.py:153
  658.6 23.0 %collective-permute-start.42 = (bf16[2,896,128]{2,1,0:T(8,128)(2,1)S(1)}, bf16[2,896,128]{2,1,0:T(8,128)(2,1)S(1)}, u32[]{:S(2)}, u32[]{:S(2)}) collective-permute-start(bf16[2,896,128]{2,1,0:T(8,128)(2,1)S(1)} %dynamic-slice_bitcast_fusion.8), channel_id=1, source_target_pairs={{0,4},{2,6},{4,0},{6,2},{1,5},{3,7},{5,1},{7,3},{8,12},{10,14},{12... | collective-permute-start | bytes 1376264 | tf_op jit(solution)/shard_map/ppermute | solution.py:1304
  (82 other events, 881.4 us)
Sparse Core Ops, SparseCore 0:
  20.5 48.0 all-gather.6
  70.7 126.0 all-gather.8
  198.4 121.2 all-gather.10
  450.7 46.3 reduce-scatter.4
  516.5 48.4 reduce-scatter.6
  567.2 59.8 reduce-scatter.8
  629.9 30.9 reduce-scatter.10
